TPU v7x, 128 devices: a whole 4x4x4 slice. The times are simulated.
128 devices in a mesh: context: 32 (over z, x, core), tensor: 4 (over y).
Axes of the slice: x: 4, y: 4, z: 4, core: 2. Of those that a mesh axis runs over, the one named last changes fastest.
Arguments:
- query_in: bfloat16 [2, 4096, 4096], P(None, 'context', 'tensor'), may hold values from -6 to 6
- key_in: bfloat16 [2, 4096, 4096], P(None, 'context', 'tensor'), may hold values from -6 to 6
- value_in: bfloat16 [2, 4096, 4096], P(None, 'context', 'tensor'), may hold values from -6 to 6
- short_filter: float32 [3, 7, 256], P(None, None, 'tensor'), may hold values from -2.4 to 2.4
- long_filter: float32 [256, 4096], P(('tensor', 'context')), may hold values from 0 to 1
- out_weight: bfloat16 [4096, 4096], P('context', 'tensor'), may hold values from -0.09375 to 0.09375
- grad_out: bfloat16 [2, 4096, 4096], P(None, 'context', 'tensor'), may hold values from -6 to 6
Outputs:
- mixed_out: bfloat16 [2, 4096, 4096], P(None, 'context', 'tensor')
- grad_query: bfloat16 [2, 4096, 4096], P(None, 'context', 'tensor')
- grad_key: bfloat16 [2, 4096, 4096], P(None, 'context', 'tensor')
- grad_value: bfloat16 [2, 4096, 4096], P(None, 'context', 'tensor')
- grad_weight: float32 [4096, 4096], P('context', 'tensor')
- grad_long: float32 [256, 4096], P(('tensor', 'context'))
All inputs are finite; a program needn't handle non-finite values.
Results may differ from a plain program's by a relative error of at most 0.015.
Values may be sent and summed in bfloat16 or wider, within the bound.
No kernel may reach another device: no remote copies, remote signals or barrier semaphores. Data moves between devices by JAX's collectives and lax.ppermute only.
A program may use at most 128 MiB of HBM per device.

v0:
```python
import math

import jax
import jax.numpy as jnp
from jax import lax
from jax.sharding import PartitionSpec as P

GROUP = 16
TAPS = 7


precise = lax.Precision.HIGH


def shifted(value, axis, steps):
    count = lax.axis_size(axis)
    first, last = (max(0, -steps), min(count, count - steps))
    return lax.ppermute(value, axis, [(source, source + steps) for source in range(first, last)])


def transform_table(points, direction):
    indices = jnp.arange(points, dtype=jnp.int32)
    phases = indices[:, None] * indices[None, :] % points
    angles = direction * 2.0 * math.pi / points * phases.astype(jnp.float32)
    return (jnp.cos(angles), jnp.sin(angles))


def twiddles(outer_len, inner_len, direction):
    row_index = jnp.arange(outer_len, dtype=jnp.int32)[:, None]
    column_index = jnp.arange(inner_len, dtype=jnp.int32)[None, :]
    phases = row_index * column_index % (outer_len * inner_len)
    angles = direction * 2.0 * math.pi / (outer_len * inner_len) * phases.astype(jnp.float32)
    return (jnp.cos(angles)[None, :, :, None], jnp.sin(angles)[None, :, :, None])


def complex_product(first_pair, second_pair):
    return (
        first_pair[0] * second_pair[0] - first_pair[1] * second_pair[1],
        first_pair[0] * second_pair[1] + first_pair[1] * second_pair[0],
    )


def conjugate(number_pair):
    return (number_pair[0], -number_pair[1])


def forward_transform(signal, outer_len, inner_len):
    batches, points, channels = signal.shape
    folded = signal.reshape(batches, outer_len, inner_len, channels)
    cos_outer, sin_outer = transform_table(outer_len, -1.0)
    partial_value = (
        jnp.einsum("kn,bnmc->bkmc", cos_outer, folded, precision=precise),
        jnp.einsum("kn,bnmc->bkmc", sin_outer, folded, precision=precise),
    )
    partial_value = complex_product(partial_value, twiddles(outer_len, inner_len, -1.0))
    cos_inner, sin_inner = transform_table(inner_len, -1.0)
    real_part = jnp.einsum(
        "bkmc,mj->bkjc", partial_value[0], cos_inner, precision=precise
    ) - jnp.einsum("bkmc,mj->bkjc", partial_value[1], sin_inner, precision=precise)
    imag_part = jnp.einsum(
        "bkmc,mj->bkjc", partial_value[0], sin_inner, precision=precise
    ) + jnp.einsum("bkmc,mj->bkjc", partial_value[1], cos_inner, precision=precise)
    return (real_part, imag_part)


def inverse_transform(spectrum, keep_rows):
    batches, outer_len, inner_len, channels = spectrum[0].shape
    cos_inner, sin_inner = transform_table(inner_len, 1.0)
    partial_value = (
        jnp.einsum("bkjc,jm->bkmc", spectrum[0], cos_inner, precision=precise)
        - jnp.einsum("bkjc,jm->bkmc", spectrum[1], sin_inner, precision=precise),
        jnp.einsum("bkjc,jm->bkmc", spectrum[0], sin_inner, precision=precise)
        + jnp.einsum("bkjc,jm->bkmc", spectrum[1], cos_inner, precision=precise),
    )
    partial_value = complex_product(partial_value, twiddles(outer_len, inner_len, 1.0))
    cos_outer, sin_outer = transform_table(outer_len, 1.0)
    real_part = jnp.einsum(
        "nk,bkmc->bnmc", cos_outer, partial_value[0], precision=precise
    ) - jnp.einsum("nk,bkmc->bnmc", sin_outer, partial_value[1], precision=precise)
    unfolded = real_part.reshape(batches, outer_len * inner_len, channels)
    return unfolded[:, :keep_rows] / float(outer_len * inner_len)


def featurize(signal, leading, tap_weights):
    local_rows = signal.shape[1]
    padded = jnp.concatenate([leading, signal], axis=1)
    summed = jnp.zeros(signal.shape, jnp.float32)
    for offset in range(TAPS):
        lead_at = TAPS - 1 - offset
        summed = summed + tap_weights[offset] * padded[:, lead_at : lead_at + local_rows].astype(
            jnp.float32
        )
    return summed


def unfeaturize(gradient, trailing, tap_weights):
    local_rows = gradient.shape[1]
    padded = jnp.concatenate([gradient, trailing], axis=1)
    summed = jnp.zeros(gradient.shape, jnp.float32)
    for offset in range(TAPS):
        summed = summed + tap_weights[offset] * padded[:, offset : offset + local_rows]
    return summed


def body(query_in, key_in, value_in, short_filter, long_filter, out_weight, grad_out):
    batches, local_rows, channels = query_in.shape
    context_size = lax.axis_size("context")
    seq_length = local_rows * context_size
    points = 2 * seq_length
    outer_len = math.gcd(points, 128)
    inner_len = points // outer_len
    grad_scale = float(batches * seq_length * GROUP) ** (-0.5)
    margin = TAPS - 1
    tap_weights = jnp.repeat(short_filter, GROUP, axis=2)
    last_rows = jnp.stack(
        [
            query_in[:, local_rows - margin :],
            key_in[:, local_rows - margin :],
            value_in[:, local_rows - margin :],
        ]
    )
    before = shifted(last_rows, "context", 1)
    query_feat = featurize(query_in, before[0], tap_weights[0])
    key_feat = featurize(key_in, before[1], tap_weights[1])
    value_feat = featurize(value_in, before[2], tap_weights[2])
    product = (key_feat * value_feat).astype(jnp.bfloat16)
    grad_full = lax.all_gather(grad_out, "tensor", axis=2, tiled=True)
    kernel = jnp.pad(long_filter, ((0, 0), (0, seq_length))).T[None]
    kernel_spec = forward_transform(kernel, outer_len, inner_len)
    kernel_spec = (
        jnp.repeat(kernel_spec[0], GROUP, axis=3),
        jnp.repeat(kernel_spec[1], GROUP, axis=3),
    )

    def padded_spectrum(blocked):
        extended = jnp.pad(blocked.astype(jnp.float32), ((0, 0), (0, seq_length), (0, 0)))
        return forward_transform(extended, outer_len, inner_len)

    product_full = lax.all_to_all(product, "context", split_axis=2, concat_axis=1, tiled=True)
    product_spec = padded_spectrum(product_full)
    conv_out = lax.all_to_all(
        inverse_transform(complex_product(product_spec, kernel_spec), seq_length).astype(
            jnp.bfloat16
        ),
        "context",
        split_axis=1,
        concat_axis=2,
        tiled=True,
    )
    gated = (query_feat * conv_out.astype(jnp.float32)).astype(jnp.bfloat16)
    weight_rows = lax.all_gather(out_weight, "context", axis=0, tiled=True)
    block_out = jnp.einsum("blc,oc->blo", gated, weight_rows, preferred_element_type=jnp.float32)
    columns = grad_full
    grad_acc = jnp.einsum("blo,oc->blc", columns, weight_rows, preferred_element_type=jnp.float32)
    grad_conv = (grad_acc * query_feat).astype(jnp.bfloat16)
    grad_conv_full = lax.all_to_all(grad_conv, "context", split_axis=2, concat_axis=1, tiled=True)
    grad_spec = padded_spectrum(grad_conv_full)
    grad_product_chan = inverse_transform(
        complex_product(grad_spec, conjugate(kernel_spec)), seq_length
    ).astype(jnp.bfloat16)
    crossed = complex_product(grad_spec, conjugate(product_spec))
    groups = crossed[0].shape[3] // GROUP
    merged = tuple(
        (
            jnp.sum(
                component.reshape(component.shape[0], outer_len, inner_len, groups, GROUP),
                axis=(0, 4),
            )[None]
            for component in crossed
        )
    )
    grad_long = inverse_transform(merged, seq_length)[0].T * grad_scale
    grad_product_chan, grad_long = (grad_product_chan, grad_long)
    grad_product = lax.all_to_all(
        grad_product_chan, "context", split_axis=1, concat_axis=2, tiled=True
    )
    mixed_out = lax.psum_scatter(
        block_out.astype(jnp.bfloat16), "tensor", scatter_dimension=2, tiled=True
    )
    columns = grad_full
    grad_weight = lax.psum_scatter(
        jnp.einsum("blo,blc->oc", columns, gated, preferred_element_type=jnp.float32).astype(
            jnp.bfloat16
        ),
        "context",
        scatter_dimension=0,
        tiled=True,
    ).astype(jnp.float32)
    product_grad = grad_product.astype(jnp.float32)
    grad_qfeat = grad_acc * conv_out.astype(jnp.float32)
    grad_kfeat = product_grad * value_feat
    grad_vfeat = product_grad * key_feat
    first_rows = jnp.stack([grad_qfeat[:, :margin], grad_kfeat[:, :margin], grad_vfeat[:, :margin]])
    following = shifted(first_rows.astype(jnp.bfloat16), "context", -1).astype(first_rows.dtype)
    grad_query = unfeaturize(grad_qfeat, following[0], tap_weights[0]).astype(jnp.bfloat16)
    grad_key = unfeaturize(grad_kfeat, following[1], tap_weights[1]).astype(jnp.bfloat16)
    grad_value = unfeaturize(grad_vfeat, following[2], tap_weights[2]).astype(jnp.bfloat16)
    return (mixed_out, grad_query, grad_key, grad_value, grad_weight, grad_long)


def solution(mesh):
    in_specs = (
        P(None, "context", "tensor"),
        P(None, "context", "tensor"),
        P(None, "context", "tensor"),
        P(None, None, "tensor"),
        P(("tensor", "context"), None),
        P("context", "tensor"),
        P(None, "context", "tensor"),
    )
    out_specs = (
        P(None, "context", "tensor"),
        P(None, "context", "tensor"),
        P(None, "context", "tensor"),
        P(None, "context", "tensor"),
        P("context", "tensor"),
        P(("tensor", "context"), None),
    )
    return jax.shard_map(body, mesh=mesh, in_specs=in_specs, out_specs=out_specs, check_vma=False)
```

profile of v0, /device:TPU:0, one launch (start us, length us, event | category | flops | bytes accessed | tf_op | source)
XLA Modules:
  0.0 448.4 jit_solution(11586722254999060880)
XLA Ops:
  15.8 27.2 %all-gather.5.cloned.1.call-done = bf16[2,128,4096]{2,1,0:T(8,128)(2,1)} async-done(((bf16[2,128,1024]{2,1,0:T(8,128)(2,1)}), bf16[2,128,4096]{2,1,0:T(8,128)(2,1)}) %all-gather.5.cloned.1.call-update) | async-done | bytes 2097168 | tf_op jit(solution)/shard_map/all_gather | solution.py:127
  43.0 55.3 %all-gather.3.cloned.1.call-done = bf16[4096,1024]{1,0:T(8,128)(2,1)} async-done(((bf16[128,1024]{1,0:T(8,128)(2,1)}), bf16[4096,1024]{1,0:T(8,128)(2,1)}) %all-gather.3.cloned.1.call-update) | async-done | bytes 8388624 | tf_op jit(solution)/shard_map/all_gather | solution.py:151
  98.4 8.4 %multiply_convert_fusion = (bf16[2,128,1024]{2,1,0:T(8,128)(2,1)S(1)}, f32[2,128,1024]{2,1,0:T(8,128)}, f32[2,128,1024]{2,1,0:T(8,128)}) fusion(bf16[2,128,1024]{2,1,0:T(8,128)(2,1)S(1)} %copy-done.13, bf16[2,6,1024]{2,1,0:T(8,128)(2,1)S(1)} %get-tuple-element.53, f32[1024]{0:T(1024)S(1)} %broadcast_in_dim.158, f32[1024]{0:T(1024)S(1)} %broadcast_in_dim.156, ...), kind=kOutput, calls=%fused_computation.200 | convolution fusion | flops 2157969408 | bytes 13684736 | tf_op jit(solution)/shard_map/blo,oc->blc/dot_general | solution.py:154
  107.8 5.5 %all-to-all-start.2 = ((bf16[2,128,1024]{1,0,2:T(2,128)(2,1)}), bf16[2,128,1024]{1,0,2:T(2,128)(2,1)S(1)}, u32[]{:S(2)}, u32[]{:S(2)}) async-start(bf16[2,128,1024]{1,0,2:T(2,128)(2,1)} %copy.124), calls=%async_computation.3 | async-start | bytes 1048576 | tf_op jit(solution)/shard_map/all_to_all | solution.py:156
  115.2 9.9 %all-to-all-done.2 = bf16[2,128,1024]{1,0,2:T(2,128)(2,1)S(1)} async-done(((bf16[2,128,1024]{1,0,2:T(2,128)(2,1)}), bf16[2,128,1024]{1,0,2:T(2,128)(2,1)S(1)}, u32[]{:S(2)}, u32[]{:S(2)}) %all-to-all-start.2) | async-done | bytes 524320 | tf_op jit(solution)/shard_map/all_to_all | solution.py:156
  153.2 3.9 copy.135
  157.0 4.8 %reshape.329 = f32[2,8192,32]{1,2,0:T(8,128)} reshape(f32[2,128,64,32]{2,1,3,0:T(8,128)} %copy.135) | data formatting | bytes 4194304 | tf_op jit(solution)/shard_map/reshape | solution.py:80
  163.9 5.3 %copy.136 = bf16[2,4096,32]{2,0,1:T(2,128)(2,1)} copy(bf16[2,4096,32]{1,2,0:T(8,128)(2,1)} %fusion.123) | data formatting | bytes 1048576 | tf_op jit(solution)/shard_map/convert_element_type | solution.py:160
  169.2 6.0 %reshape.359 = bf16[32,2,4096]{2,1,0:T(2,128)(2,1)} reshape(bf16[4096,2,32]{2,1,0:T(2,128)(2,1)} %bitcast.476) | data formatting | bytes 1048576
  175.2 4.6 %all-to-all-start.3 = ((bf16[32,2,4096]{2,1,0:T(2,128)(2,1)}), bf16[32,2,4096]{2,1,0:T(2,128)(2,1)}, u32[]{:S(2)}, u32[]{:S(2)}) async-start(bf16[32,2,4096]{2,1,0:T(2,128)(2,1)} %reshape.359), calls=%async_computation.4 | async-start | bytes 1048576 | tf_op jit(solution)/shard_map/all_to_all | solution.py:174
  182.1 9.5 %all-to-all-done.3 = bf16[32,2,4096]{2,1,0:T(2,128)(2,1)} async-done(((bf16[32,2,4096]{2,1,0:T(2,128)(2,1)}), bf16[32,2,4096]{2,1,0:T(2,128)(2,1)}, u32[]{:S(2)}, u32[]{:S(2)}) %all-to-all-start.3) | async-done | bytes 524320 | tf_op jit(solution)/shard_map/all_to_all | solution.py:174
  191.6 5.9 %reshape.360 = bf16[4096,2,32]{2,1,0:T(2,128)(2,1)} reshape(bf16[32,2,4096]{2,1,0:T(2,128)(2,1)} %all-to-all-done.3) | data formatting | bytes 1048576
  197.5 5.3 %copy.137 = bf16[2,4096,32]{1,2,0:T(8,128)(2,1)} copy(bf16[2,4096,32]{2,0,1:T(2,128)(2,1)} %bitcast.477) | data formatting | bytes 1048576 | tf_op jit(solution)/shard_map/all_to_all | solution.py:174
  208.2 5.2 %fusion.401 = (f32[2,128,1024]{2,1,0:T(8,128)}, f32[2,128,1024]{2,1,0:T(8,128)S(1)}) fusion(f32[2,128,1024]{2,1,0:T(8,128)} %copy.139, bf16[2,128,1024]{2,1,0:T(8,128)(2,1)} %param.8, bf16[2,6,1024]{2,1,0:T(8,128)(2,1)S(1)} %get-tuple-element.52, f32[1024]{0:T(1024)S(1)} %broadcast_in_dim.172, f32[1024]{0:T(1024)S(1)} %broadcast_in_dim.170, ...), kind=kLoop, calls=%fused_computation.537 | loop fusion | flops 10223616 | bytes 3723264 | tf_op jit(solution)/shard_map/mul | solution.py:192
  218.3 15.6 %all_to_all.16 = bf16[2,128,1024]{1,0,2:T(2,128)(2,1)S(1)} all-to-all(bf16[2,128,1024]{1,0,2:T(2,128)(2,1)} %copy.105), channel_id=1, replica_groups=mesh['context'=32,'tensor'=4] {'context'}, dimensions={2} | all-to-all | bytes 1048576 | tf_op jit(solution)/shard_map/all_to_all | solution.py:139
  235.2 4.3 reshape.321
  239.4 3.8 copy.108
  253.3 4.4 fusion.15
  279.5 15.2 %all_to_all.17 = bf16[32,2,4096]{2,1,0:T(2,128)(2,1)S(1)} all-to-all(bf16[32,2,4096]{2,1,0:T(2,128)(2,1)S(1)} %reshape.357), channel_id=1, replica_groups=mesh['context'=32,'tensor'=4] {'context'}, dimensions={0} | all-to-all | bytes 1048576 | tf_op jit(solution)/shard_map/all_to_all | solution.py:141
  301.6 5.7 %fusion.4 = bf16[4096,1024]{0,1:T(8,128)(2,1)} fusion(bf16[2,128,1024]{2,1,0:T(8,128)(2,1)S(1)} %get-tuple-element.47, bf16[2,128,4096]{2,1,0:T(8,128)(2,1)S(1)} %copy-done.7), kind=kOutput, calls=%fused_computation.5 | convolution fusion | flops 2151677952 | bytes 11010048 | tf_op jit(solution)/shard_map/blo,blc->oc/dot_general | solution.py:182
  307.2 11.8 %copy.163 = bf16[4096,1024]{1,0:T(8,128)(2,1)} copy(bf16[4096,1024]{0,1:T(8,128)(2,1)} %fusion.4) | data formatting | bytes 16777216
  319.1 7.1 %fusion.5 = bf16[2,128,4096]{2,1,0:T(8,128)(2,1)} fusion(bf16[2,128,1024]{2,1,0:T(8,128)(2,1)S(1)} %get-tuple-element.47, bf16[4096,1024]{1,0:T(8,128)(2,1)} %all-gather.3.cloned.1.call-done), kind=kOutput, calls=%fused_computation.6 | convolution fusion | flops 2148532224 | bytes 11010048 | tf_op jit(solution)/shard_map/blc,oc->blo/dot_general | solution.py:152
  341.9 67.8 %reduce-scatter.7.cloned.1.call-done = bf16[128,1024]{1,0:T(8,128)(2,1)} async-done(((bf16[4096,1024]{1,0:T(8,128)(2,1)}), bf16[128,1024]{1,0:T(8,128)(2,1)}) %reduce-scatter.7.cloned.1.call-update) | async-done | bytes 262160
  411.8 29.9 %reduce-scatter.5.cloned.1.call-done = bf16[2,128,1024]{2,1,0:T(8,128)(2,1)} async-done(((bf16[2,128,4096]{2,1,0:T(8,128)(2,1)}), bf16[2,128,1024]{2,1,0:T(8,128)(2,1)}) %reduce-scatter.5.cloned.1.call-update) | async-done | bytes 524304 | tf_op jit(solution)/shard_map/reduce_scatter | solution.py:177
  (175 shorter events, 111.5 us)
Async XLA Ops:
  7.2 91.2 %copy-start.13 = (bf16[2,128,1024]{2,1,0:T(8,128)(2,1)S(1)}, bf16[2,128,1024]{2,1,0:T(8,128)(2,1)}, u32[]{:S(2)}) copy-start(bf16[2,128,1024]{2,1,0:T(8,128)(2,1)} %param.7) | copy-start | bytes 1572868
  7.2 7.0 %copy-start.10 = (f32[3,7,64]{2,1,0:T(8,128)S(1)}, f32[3,7,64]{2,1,0:T(8,128)}, u32[]{:S(2)}) copy-start(f32[3,7,64]{2,1,0:T(8,128)} %param.10) | copy-start | bytes 16132
  7.2 35.9 %all-gather.5.cloned.1.call-start = ((), (), s32[]{:S(2)}) async-start(), calls=%async_computation.8 | async-start | bytes 2621440 | tf_op jit(solution)/shard_map/all_gather | solution.py:127
  7.9 90.4 %all-gather.3.cloned.1.call-start = ((), (), s32[]{:S(2)}) async-start(), calls=%async_computation.6 | async-start | bytes 8650752 | tf_op jit(solution)/shard_map/all_gather | solution.py:151
  10.3 5.5 %collective-permute-start = (bf16[3,2,6,1024]{3,2,1,0:T(8,128)(2,1)S(1)}, bf16[3,2,6,1024]{3,2,1,0:T(8,128)(2,1)S(1)}, u32[]{:S(2)}, u32[]{:S(2)}) collective-permute-start(bf16[3,2,6,1024]{3,2,1,0:T(8,128)(2,1)S(1)} %pad_maximum_fusion.6), channel_id=1, source_target_pairs={{0,4},{4,8},{8,12},{12,16},{16,20},{20,24},{24,28},{28,32},{32,36}... | collective-permute-start | bytes 221192 | tf_op jit(solution)/shard_map/ppermute | solution.py:18
  15.8 91.0 %copy-start.9 = (f32[1024]{0:T(1024)}, f32[1024]{0:T(1024)S(1)}, u32[]{:S(2)}) copy-start(f32[1024]{0:T(1024)S(1)} %broadcast_in_dim.146) | copy-start | bytes 12292
  107.8 17.2 %all-to-all-start.2 = ((bf16[2,128,1024]{1,0,2:T(2,128)(2,1)}), bf16[2,128,1024]{1,0,2:T(2,128)(2,1)S(1)}, u32[]{:S(2)}, u32[]{:S(2)}) async-start(bf16[2,128,1024]{1,0,2:T(2,128)(2,1)} %copy.124), calls=%async_computation.3 | async-start | bytes 1048576 | tf_op jit(solution)/shard_map/all_to_all | solution.py:156
  138.4 2.4 copy-start.2
  140.7 4.7 %copy-start = (f32[64,2,128,32]{2,0,3,1:T(8,128)}, f32[64,2,128,32]{2,0,3,1:T(8,128)S(1)}, u32[]{:S(2)}) copy-start(f32[64,2,128,32]{2,0,3,1:T(8,128)S(1)} %fusion.54) | copy-start | bytes 6291460
  169.2 10.7 %copy-start.12 = (f32[64]{0:T(128)S(1)}, f32[64]{0:T(128)}, u32[]{:S(2)}) copy-start(f32[64]{0:T(128)} %get-tuple-element.59) | copy-start | bytes 772
  169.2 12.1 %copy-start.11 = (f32[64]{0:T(128)S(1)}, f32[64]{0:T(128)}, u32[]{:S(2)}) copy-start(f32[64]{0:T(128)} %get-tuple-element.55) | copy-start | bytes 772
  175.2 16.4 %all-to-all-start.3 = ((bf16[32,2,4096]{2,1,0:T(2,128)(2,1)}), bf16[32,2,4096]{2,1,0:T(2,128)(2,1)}, u32[]{:S(2)}, u32[]{:S(2)}) async-start(bf16[32,2,4096]{2,1,0:T(2,128)(2,1)} %reshape.359), calls=%async_computation.4 | async-start | bytes 1048576 | tf_op jit(solution)/shard_map/all_to_all | solution.py:174
  179.9 229.8 %reduce-scatter.7.cloned.1.call-start = ((), (), s32[]{:S(2)}) async-start(), calls=%async_computation.9 | async-start | bytes 8650752
  208.2 5.2 %copy-start.4 = (f32[2,128,1024]{2,1,0:T(8,128)S(1)}, f32[2,128,1024]{2,1,0:T(8,128)}, u32[]{:S(2)}) copy-start(f32[2,128,1024]{2,1,0:T(8,128)} %copy.139) | copy-start | bytes 3145732
  208.2 5.2 %copy-start.8 = (bf16[2,128,1024]{2,1,0:T(8,128)(2,1)S(1)}, bf16[2,128,1024]{2,1,0:T(8,128)(2,1)}, u32[]{:S(2)}) copy-start(bf16[2,128,1024]{2,1,0:T(8,128)(2,1)} %param.9) | copy-start | bytes 1572868
  243.2 2.3 copy-start.3
  251.1 2.2 copy-start.1
  299.4 2.2 copy-start.7
  319.1 122.6 %reduce-scatter.5.cloned.1.call-start = ((), (), s32[]{:S(2)}) async-start(), calls=%async_computation.7 | async-start | bytes 2621440 | tf_op jit(solution)/shard_map/reduce_scatter | solution.py:177
  326.2 1.3 copy-start.5
  326.2 1.6 copy-start.6
  332.9 3.2 collective-permute-start.1
Sparse Core Ops, SparseCore 0:
  9.7 33.3 all-gather.4
  45.3 53.0 all-gather.2
  319.2 90.4 reduce-scatter.6
  412.7 28.9 reduce-scatter.4
where the time goes:
time: 457 us; the launch traced here: 448 us
  waiting for transfers between devices  202 us (44%)
  local copies, waits for them, and re-layouts  90.6 us (20%)
  matrix products  73.3 us (16%)
  blocking collectives  30.9 us (7%)
  other arithmetic  23.9 us (5%)
  between operations  14.7 us (3%)
  starting transfers between devices  13.1 us (3%)
    unnamed x5, waiting for transfers between devices  69.2 us
    all_gather x1, waiting for transfers between devices, body(): weight_rows = lax.all_gather(out_weight, 'context', axis=0, tiled=True)  55.3 us
    unnamed x37, local copies, waits for them, and re-layouts  31.3 us
    reduce_scatter x1, waiting for transfers between devices, body(): lax.psum_scatter(block_out.astype(jnp.bfloat16), 'tensor', scatter_dimens...  29.9 us
    all_gather x1, waiting for transfers between devices, body(): grad_full = lax.all_gather(grad_out, 'tensor', axis=2, tiled=True)  27.2 us
    all_to_all x1, blocking collectives, body(): lax.all_to_all(product, 'context', split_axis=2, concat_axis=1, tiled=True)  15.6 us
    all_to_all x1, blocking collectives, body(): lax.all_to_all(inverse_transform(complex_product(product_spec, kernel_spe...  15.2 us
    reshape x4, local copies, waits for them, and re-layouts, forward_transform(): folded = signal.reshape(batches, outer_len, inner_len, channels)  12.3 us
  transfers between devices with their start and end apart: 8, of which 7 were waited for; matrix products, arithmetic and copies ran while one was open for 7% of the time, Pallas kernels for 0%

commit v1 on v0

v1 whole, which is shorter than its diff:
```python
import functools

import jax
import jax.numpy as jnp
from jax import lax
from jax.experimental import pallas as pl
from jax.experimental.pallas import tpu as pltpu
from jax.sharding import PartitionSpec as P

GROUP = 16
TAPS = 7
HALO = 16
NZ, NX, NC, NY = 4, 4, 2, 4
NCTX = NZ * NX * NC
BLK = 128
CB = 256
f32 = jnp.float32
bf16 = jnp.bfloat16


def move_ctx(value, dz, dx, dc):
    pairs = []
    for z in range(NZ):
        for x in range(NX):
            for c in range(NC):
                src = (z * NX + x) * NC + c
                dst = (((z + dz) % NZ) * NX + (x + dx) % NX) * NC + (c + dc) % NC
                pairs.append((src, dst))
    return lax.ppermute(value, "context", pairs)


def move_z(value, d):
    return move_ctx(value, d, 0, 0)


def move_x(value, d):
    return move_ctx(value, 0, d, 0)


def swap_core(value):
    return move_ctx(value, 0, 0, 1)


def move_y(value, d):
    return lax.ppermute(value, "tensor", [(i, (i + d) % NY) for i in range(NY)])


def next_context(value, steps):
    first, last = (max(0, -steps), min(NCTX, NCTX - steps))
    return lax.ppermute(value, "context", [(s, s + steps) for s in range(first, last)])


def around(value, move, count=4):
    return [value] + [move(value, d) for d in range(1, count)]


def deliver(parts, move):
    return [parts[0]] + [move(part, d) for d, part in enumerate(parts) if d > 0]


def params(*sem):
    return pltpu.CompilerParams(dimension_semantics=sem, vmem_limit_bytes=48 * 1024 * 1024)


def toeplitz_kernel(filter_ref, tile_ref):
    taps = jnp.concatenate([jnp.zeros((1, BLK), f32), filter_ref[0]], axis=1)
    blocks = taps.shape[1] // BLK - 1
    tile_ref[0, 0, BLK:, :BLK] = jnp.zeros((BLK, BLK), bf16)
    for e in range(blocks):
        window = jnp.broadcast_to(taps[:, BLK * e : BLK * (e + 2)], (BLK, 2 * BLK))
        rolled = pltpu.roll(window, 0, 1, stride=1, stride_axis=0)
        piece = rolled[:, BLK:].astype(bf16)
        if e % 2 == 0:
            tile_ref[0, e // 2, :BLK, :BLK] = piece
            tile_ref[0, e // 2, BLK:, BLK:] = piece
        else:
            tile_ref[0, e // 2, :BLK, BLK:] = piece
            if e + 1 < blocks:
                tile_ref[0, e // 2 + 1, BLK:, :BLK] = piece


def toeplitz_tiles(long_filter):
    groups, length = long_filter.shape
    tiles = length // (2 * BLK)
    return pl.pallas_call(
        toeplitz_kernel,
        grid=(groups,),
        in_specs=[pl.BlockSpec((1, 1, length), lambda g: (g, 0, 0))],
        out_specs=pl.BlockSpec((1, tiles, 2 * BLK, 2 * BLK), lambda g: (g, 0, 0, 0)),
        out_shape=jax.ShapeDtypeStruct((groups, tiles, 2 * BLK, 2 * BLK), bf16),
        compiler_params=params("arbitrary"),
        cost_estimate=pl.CostEstimate(flops=8_000_000, bytes_accessed=4_300_000, transcendentals=0),
        name="toeplitz_tiles",
    )(long_filter[:, None, :])


def spread_taps(taps, block):
    rows = lax.broadcasted_iota(jnp.int32, (taps.shape[1], CB), 0)
    cols = lax.broadcasted_iota(jnp.int32, (taps.shape[1], CB), 1)
    spread = (rows == ((block * CB + cols) >> 4)).astype(f32)
    return jnp.dot(taps, spread, precision=lax.Precision.HIGHEST, preferred_element_type=f32)


def to_channels(value):
    return value.T.reshape(CB // (2 * GROUP), 2, GROUP, BLK).astype(bf16)


def to_positions(value):
    return value.astype(f32).reshape(CB, BLK).T


def featurize_kernel(taps_ref, halo_ref, q_ref, k_ref, v_ref, prod_ref, qf_ref, kf_ref, vf_ref):
    taps = spread_taps(taps_ref[...], pl.program_id(0))
    for b in range(2):
        feats = []
        for i, (src, dst) in enumerate(((q_ref, qf_ref), (k_ref, kf_ref), (v_ref, vf_ref))):
            ext = jnp.concatenate([halo_ref[i, b].astype(f32), src[b].astype(f32)], axis=0)
            total = taps[7 * i : 7 * i + 1] * ext[HALO:]
            for j in range(1, TAPS):
                total = total + taps[7 * i + j : 7 * i + j + 1] * ext[HALO - j : HALO - j + BLK]
            dst[b] = total
            feats.append(total)
        prod_ref[:, :, b] = to_channels(feats[1] * feats[2])


chan_spec = pl.BlockSpec((CB // (2 * GROUP), 2, 2, GROUP, BLK), lambda c: (c, 0, 0, 0, 0))
pos_spec = pl.BlockSpec((2, BLK, CB), lambda c: (0, 0, c))
taps_spec = pl.BlockSpec((24, 64), lambda c: (0, 0))
halo_spec = pl.BlockSpec((3, 2, HALO, CB), lambda c: (0, 0, 0, c))


def chan_shape():
    return jax.ShapeDtypeStruct((NCTX, 2, 2, GROUP, BLK), bf16)


def pos_shape(kind):
    return jax.ShapeDtypeStruct((2, BLK, 1024), kind)


def featurize(taps, halo, q, k, v):
    return pl.pallas_call(
        featurize_kernel,
        grid=(1024 // CB,),
        in_specs=[taps_spec, halo_spec, pos_spec, pos_spec, pos_spec],
        out_specs=[chan_spec, pos_spec, pos_spec, pos_spec],
        out_shape=[chan_shape(), pos_shape(f32), pos_shape(f32), pos_shape(f32)],
        compiler_params=params("arbitrary"),
        cost_estimate=pl.CostEstimate(flops=12_000_000, bytes_accessed=5_500_000, transcendentals=0),
        name="featurize",
    )(taps, halo, q, k, v)


def fold(src_ref, dst_ref):
    for i in range(NCTX // 2):
        dst_ref[32 * i : 32 * i + 32, :BLK] = src_ref[2 * i, 0].reshape(32, BLK)
        dst_ref[32 * i : 32 * i + 32, BLK:] = src_ref[2 * i + 1, 0].reshape(32, BLK)


def unfold(acc_ref, dst_ref):
    for i in range(NCTX // 2):
        rows = acc_ref[32 * i : 32 * i + 32].astype(bf16)
        dst_ref[2 * i, 0] = rows[:, :BLK].reshape(2, GROUP, BLK)
        dst_ref[2 * i + 1, 0] = rows[:, BLK:].reshape(2, GROUP, BLK)


def conv_kernel(x_ref, tile_ref, out_ref, x_s, acc_s):
    fold(x_ref, x_s)
    rows = x_s.shape[0]
    for d in range(rows // 32):
        term = jnp.dot(x_s[: rows - 32 * d], tile_ref[0, d], preferred_element_type=f32)
        if d == 0:
            acc_s[...] = term
        else:
            acc_s[32 * d :] += term
    unfold(acc_s, out_ref)


def corr_kernel(x_ref, tile_ref, out_ref, x_s, acc_s):
    fold(x_ref, x_s)
    rows = x_s.shape[0]
    for d in range(rows // 32):
        term = lax.dot_general(
            x_s[32 * d :], tile_ref[0, d], (((1,), (1,)), ((), ())), preferred_element_type=f32
        )
        if d == 0:
            acc_s[...] = term
        else:
            acc_s[: rows - 32 * d] += term
    unfold(acc_s, out_ref)


group_spec = pl.BlockSpec((NCTX, 1, 2, GROUP, BLK), lambda g: (0, g, 0, 0, 0))
tile_spec = pl.BlockSpec((1, 16, 2 * BLK, 2 * BLK), lambda g: (g, 0, 0, 0))


def convolve(kernel, name, x, tiles):
    return pl.pallas_call(
        kernel,
        grid=(2,),
        in_specs=[group_spec, tile_spec],
        out_specs=group_spec,
        out_shape=chan_shape(),
        scratch_shapes=[pltpu.VMEM((512, 256), bf16), pltpu.VMEM((512, 256), f32)],
        compiler_params=params("arbitrary"),
        cost_estimate=pl.CostEstimate(flops=1_100_000_000, bytes_accessed=5_300_000, transcendentals=0),
        name=name,
    )(x, tiles)


def grad_long_kernel(scale, p_ref, g_ref, out_ref, p_s, g_s):
    fold(p_ref, p_s)
    fold(g_ref, g_s)
    g_s[512:] = jnp.zeros((512, 256), bf16)
    rows = lax.broadcasted_iota(jnp.int32, (256, 256), 0)
    cols = lax.broadcasted_iota(jnp.int32, (256, 256), 1)
    flip = (rows + cols == 255).astype(bf16)
    back = lax.dot_general(
        flip, p_s[...], (((1,), (1,)), ((), ())), preferred_element_type=f32
    ).astype(bf16)

    def diagonals(block):
        padded = jnp.concatenate([block, jnp.zeros((BLK, BLK), f32)], axis=1)
        rolled = pltpu.roll(padded, 1, 1, stride=1, stride_axis=0)
        return jnp.sum(rolled, axis=0, keepdims=True)

    def gram(d):
        return jnp.dot(back, g_s[32 * d : 32 * d + 512], preferred_element_type=f32)

    here = gram(0)
    lag = diagonals(here[BLK:, :BLK] + here[:BLK, BLK:])
    for d in range(16):
        later = gram(d + 1) if d < 15 else None
        cross = here[BLK:, BLK:]
        if later is not None:
            cross = cross + later[:BLK, :BLK]
        odd = diagonals(cross)
        out_ref[0, :, 256 * d : 256 * d + BLK] = scale * (lag[:, BLK:] + odd[:, :BLK])
        if later is not None:
            lag = diagonals(later[BLK:, :BLK] + later[:BLK, BLK:])
            out_ref[0, :, 256 * d + BLK : 256 * d + 256] = scale * (odd[:, BLK:] + lag[:, :BLK])
        else:
            out_ref[0, :, 256 * d + BLK : 256 * d + 256] = scale * odd[:, BLK:]
        here = later


def grad_long_call(scale, prod, grad_conv):
    return pl.pallas_call(
        functools.partial(grad_long_kernel, scale),
        grid=(2,),
        in_specs=[group_spec, group_spec],
        out_specs=pl.BlockSpec((1, 1, NCTX * BLK), lambda g: (g, 0, 0)),
        out_shape=jax.ShapeDtypeStruct((2, 1, NCTX * BLK), f32),
        scratch_shapes=[pltpu.VMEM((512, 256), bf16), pltpu.VMEM((1024, 256), bf16)],
        compiler_params=params("arbitrary"),
        cost_estimate=pl.CostEstimate(flops=2_200_000_000, bytes_accessed=1_200_000, transcendentals=0),
        name="grad_long",
    )(prod, grad_conv)[:, 0]


def gate_kernel(conv_ref, qf_ref, gated_ref, convp_ref):
    for b in range(2):
        conv = to_positions(conv_ref[:, :, b])
        convp_ref[b] = conv.astype(bf16)
        gated_ref[b] = (qf_ref[b] * conv).astype(bf16)


def gate(conv, qf):
    return pl.pallas_call(
        gate_kernel,
        grid=(1024 // CB,),
        in_specs=[chan_spec, pos_spec],
        out_specs=[pos_spec, pos_spec],
        out_shape=[pos_shape(bf16), pos_shape(bf16)],
        compiler_params=params("arbitrary"),
        cost_estimate=pl.CostEstimate(flops=1_000_000, bytes_accessed=2_500_000, transcendentals=0),
        name="gate",
    )(conv, qf)


def grad_conv_kernel(own_ref, other_ref, qf_ref, gc_ref, gg_ref):
    for b in range(2):
        total = own_ref[b] + other_ref[b].astype(f32)
        gg_ref[b] = total
        gc_ref[:, :, b] = to_channels(total * qf_ref[b])


def grad_conv_call(own, other, qf):
    return pl.pallas_call(
        grad_conv_kernel,
        grid=(1024 // CB,),
        in_specs=[pos_spec, pos_spec, pos_spec],
        out_specs=[chan_spec, pos_spec],
        out_shape=[chan_shape(), pos_shape(f32)],
        compiler_params=params("arbitrary"),
        cost_estimate=pl.CostEstimate(flops=1_000_000, bytes_accessed=4_000_000, transcendentals=0),
        name="grad_conv",
    )(own, other, qf)


def unpack_kernel(gp_ref, kf_ref, vf_ref, gpp_ref, first_ref):
    for b in range(2):
        grad = to_positions(gp_ref[:, :, b])
        gpp_ref[b] = grad.astype(bf16)
        first_ref[0, b] = (grad[:HALO] * vf_ref[b]).astype(bf16)
        first_ref[1, b] = (grad[:HALO] * kf_ref[b]).astype(bf16)


def unpack(gp, kf, vf):
    rows_spec = pl.BlockSpec((2, HALO, CB), lambda c: (0, 0, c))
    return pl.pallas_call(
        unpack_kernel,
        grid=(1024 // CB,),
        in_specs=[chan_spec, rows_spec, rows_spec],
        out_specs=[pos_spec, pl.BlockSpec((2, 2, HALO, CB), lambda c: (0, 0, 0, c))],
        out_shape=[pos_shape(bf16), jax.ShapeDtypeStruct((2, 2, HALO, 1024), bf16)],
        compiler_params=params("arbitrary"),
        cost_estimate=pl.CostEstimate(flops=500_000, bytes_accessed=1_200_000, transcendentals=0),
        name="unpack",
    )(gp, kf, vf)


def backward_taps(grad, halo, taps, first):
    ext = jnp.concatenate([grad, halo.astype(f32)], axis=0)
    total = taps[first : first + 1] * grad
    for j in range(1, TAPS):
        total = total + taps[first + j : first + j + 1] * ext[j : j + BLK]
    return total.astype(bf16)


def grad_query_kernel(taps_ref, halo_ref, gg_ref, conv_ref, out_ref):
    taps = spread_taps(taps_ref[...], pl.program_id(0))
    for b in range(2):
        out_ref[b] = backward_taps(
            gg_ref[b] * conv_ref[b].astype(f32), halo_ref[0, b], taps, 0
        )


def grad_query_call(taps, halo, gg, conv):
    return pl.pallas_call(
        grad_query_kernel,
        grid=(1024 // CB,),
        in_specs=[
            taps_spec,
            pl.BlockSpec((1, 2, HALO, CB), lambda c: (0, 0, 0, c)),
            pos_spec,
            pos_spec,
        ],
        out_specs=pos_spec,
        out_shape=pos_shape(bf16),
        compiler_params=params("arbitrary"),
        cost_estimate=pl.CostEstimate(flops=4_000_000, bytes_accessed=2_100_000, transcendentals=0),
        name="grad_query",
    )(taps, halo, gg, conv)


def grad_kv_kernel(taps_ref, halo_ref, gp_ref, kf_ref, vf_ref, gk_ref, gv_ref):
    taps = spread_taps(taps_ref[...], pl.program_id(0))
    for b in range(2):
        grad = gp_ref[b].astype(f32)
        gk_ref[b] = backward_taps(grad * vf_ref[b], halo_ref[0, b], taps, TAPS)
        gv_ref[b] = backward_taps(grad * kf_ref[b], halo_ref[1, b], taps, 2 * TAPS)


def grad_kv_call(taps, halo, gp, kf, vf):
    return pl.pallas_call(
        grad_kv_kernel,
        grid=(1024 // CB,),
        in_specs=[
            taps_spec,
            pl.BlockSpec((2, 2, HALO, CB), lambda c: (0, 0, 0, c)),
            pos_spec,
            pos_spec,
            pos_spec,
        ],
        out_specs=[pos_spec, pos_spec],
        out_shape=[pos_shape(bf16), pos_shape(bf16)],
        compiler_params=params("arbitrary"),
        cost_estimate=pl.CostEstimate(flops=8_000_000, bytes_accessed=4_000_000, transcendentals=0),
        name="grad_kv",
    )(taps, halo, gp, kf, vf)


def vmem(count=1):
    return [pl.BlockSpec(memory_space=pltpu.VMEM)] * count


smem = pl.BlockSpec(memory_space=pltpu.SMEM)


def whole(kernel, name, ins, outs, flops=0, scratch=(), index=True):
    size = sum(a.size * a.dtype.itemsize for a in ins)
    size += sum(a.size * jnp.dtype(a.dtype).itemsize for a in outs)
    return pl.pallas_call(
        kernel,
        in_specs=([smem] if index else []) + vmem(len(ins) - int(index)),
        out_specs=vmem(len(outs)),
        out_shape=list(outs),
        scratch_shapes=list(scratch),
        compiler_params=pltpu.CompilerParams(vmem_limit_bytes=48 * 1024 * 1024),
        cost_estimate=pl.CostEstimate(flops=flops, bytes_accessed=size, transcendentals=0),
        name=name,
    )(*ins)


def shape(dims, kind=bf16):
    return jax.ShapeDtypeStruct(dims, kind)


def prep_kernel(at, q_ref, k_ref, v_ref, w_ref, g_ref, last_ref, wa_ref, wb_ref, mine_ref, theirs_ref):
    first_core = at[3] == 0
    for i, src in enumerate((q_ref, k_ref, v_ref)):
        last_ref[i] = src[...]
    wa_ref[...] = w_ref[:, :512]
    wb_ref[...] = w_ref[:, 512:]
    for x in range(NX):
        lo = g_ref[:, 256 * x : 256 * x + BLK]
        hi = g_ref[:, 256 * x + BLK : 256 * x + 256]
        mine_ref[:, BLK * x : BLK * x + BLK] = jnp.where(first_core, lo, hi)
        theirs_ref[:, BLK * x : BLK * x + BLK] = jnp.where(first_core, hi, lo)


def prep(at, q, k, v, weight, grad_out):
    rows = pl.BlockSpec((2, HALO, 1024), lambda i: (0, BLK // HALO - 1, 0))
    full = lambda dims: pl.BlockSpec(dims, lambda i: (0,) * len(dims))
    return pl.pallas_call(
        prep_kernel,
        grid=(1,),
        in_specs=[smem, rows, rows, rows, full((BLK, 1024)), full((256, 1024))],
        out_specs=[full((3, 2, HALO, 1024)), full((BLK, 512)), full((BLK, 512)), full((256, 512)), full((256, 512))],
        out_shape=[
            shape((3, 2, HALO, 1024)),
            shape((BLK, 512)),
            shape((BLK, 512)),
            shape((256, 512)),
            shape((256, 512)),
        ],
        compiler_params=params("arbitrary"),
        name="prep",
    )(at, q, k, v, weight, grad_out)


def grad_gated_kernel(at, *refs):
    cols, part_a, part_b = refs[:4], refs[4:8], refs[8:12]
    own_ref, other_ref, cols_ref, w_ref = refs[12:]
    for d in range(4):
        cols_ref[(at[2] + 4 - d) & 3] = cols[d][...]
        for e in range(4):
            w_ref[(at[0] + 4 - d) & 3, (at[1] + 4 - e) & 3, :, :512] = part_a[d][e]
            w_ref[(at[0] + 4 - e) & 3, (at[1] + 4 - d) & 3, :, 512:] = part_b[d][e]

    def step(n, carry):
        lanes = pl.ds(pl.multiple_of(n * 256, 256), 256)
        total = jnp.zeros((512, 256), f32)
        for y in range(NY):
            total = total + jnp.dot(
                cols_ref[y], w_ref[y, :, :, lanes].reshape(512, 256), preferred_element_type=f32
            )
        own_ref[:, lanes] = total[:256]
        other_ref[:, lanes] = total[256:].astype(bf16)
        return carry

    lax.fori_loop(0, 4, step, 0)


def mixed_kernel(at, own_g, other_g, w_ref, *outs):
    for d in range(4):
        block = w_ref[(at[2] + d) & 3].reshape(512, 1024)
        for i, src in enumerate((own_g, other_g)):
            part = lax.dot_general(
                src[...], block, (((1,), (1,)), ((), ())), preferred_element_type=f32
            )
            outs[d][256 * i : 256 * i + 256] = part.astype(outs[d].dtype)


def mixed_sum_kernel(own, a_ref, b_ref, c_ref, keep_ref, send_ref):
    total = own[...] + a_ref[...].astype(f32) + b_ref[...].astype(f32) + c_ref[...].astype(f32)
    keep_ref[...] = total[:256].astype(bf16)
    send_ref[...] = total[256:].astype(bf16)


def mixed_out_kernel(at, keep_ref, came_ref, out_ref):
    first_core = at[3] == 0
    for x in range(NX):
        keep = keep_ref[:, BLK * x : BLK * x + BLK]
        came = came_ref[:, BLK * x : BLK * x + BLK]
        out_ref[:, 256 * x : 256 * x + BLK] = jnp.where(first_core, keep, came)
        out_ref[:, 256 * x + BLK : 256 * x + 256] = jnp.where(first_core, came, keep)


def weight_grad_kernel(at, cols_ref, own_g, other_g, *refs):
    outs_a, outs_b, held_b = refs[:4], refs[4:8], refs[8]
    for d in range(4):
        cols = cols_ref[(at[0] + d) & 3]
        for n in range(2):
            lanes = slice(512 * n, 512 * n + 512)
            total = lax.dot_general(
                cols[:256], own_g[:, lanes], (((0,), (0,)), ((), ())), preferred_element_type=f32
            ) + lax.dot_general(
                cols[256:], other_g[:, lanes], (((0,), (0,)), ((), ())), preferred_element_type=f32
            )
            total = total.astype(bf16)
            for x in range(NX):
                block = total[BLK * x : BLK * x + BLK]
                if n == 0:
                    outs_a[d][(x + 4 - at[1]) & 3] = block
                else:
                    held_b[(x + 4 - at[1]) & 3, d] = block
    for e in range(4):
        outs_b[e][...] = held_b[e]


def sum_split_kernel(*refs):
    parts, outs = refs[:4], refs[4:]
    for e in range(4):
        total = parts[0][e].astype(f32)
        for part in parts[1:]:
            total = total + part[e].astype(f32)
        outs[e][...] = total.astype(outs[e].dtype)


def weight_out_kernel(*refs):
    out_ref = refs[8]
    for n in range(2):
        total = refs[4 * n][...]
        for part in refs[4 * n + 1 : 4 * n + 4]:
            total = total + part[...].astype(f32)
        out_ref[:, 512 * n : 512 * n + 512] = total


def exchange(value):
    return lax.all_to_all(value, "context", split_axis=0, concat_axis=0, tiled=True)


def body(query_in, key_in, value_in, short_filter, long_filter, out_weight, grad_out):
    batches, rows, channels = query_in.shape
    scale = float(batches * rows * NCTX * GROUP) ** (-0.5)
    ctx = lax.axis_index("context")
    at_y = lax.axis_index("tensor")
    at = jnp.stack([ctx // (NC * NX), (ctx // NC) % NX, at_y, ctx % NC]).astype(jnp.int32)
    positions = batches * rows
    half = channels // 2

    taps = jnp.pad(short_filter.reshape(3 * TAPS, channels // GROUP), ((0, 3), (0, 0)))
    last, w_a, w_b, mine, theirs = prep(
        at, query_in, key_in, value_in, out_weight, grad_out.reshape(positions, channels)
    )
    before = next_context(last, 1)

    w_a = jnp.stack(around(w_a, move_x))
    w_b = jnp.stack(around(w_b, move_z))
    w_a = around(w_a, move_z)
    w_b = around(w_b, move_x)

    columns = around(jnp.concatenate([mine, swap_core(theirs)]), move_y)

    tiles = toeplitz_tiles(long_filter)
    prod, qf, kf, vf = featurize(taps, before, query_in, key_in, value_in)
    prod = exchange(prod)
    conv = exchange(convolve(conv_kernel, "conv", prod, tiles))
    gated, conv = gate(conv, qf)
    gated_own = gated.reshape(positions, channels)
    gated_other = swap_core(gated_own)

    own, other, columns, weights = whole(
        grad_gated_kernel,
        "grad_gated",
        [at, *columns, *w_a, *w_b],
        [
            shape((positions, channels), f32),
            shape((positions, channels)),
            shape((NY, 2 * positions, half)),
            shape((NZ, NX, BLK, channels)),
        ],
        flops=2_200_000_000,
    )
    other = swap_core(other)
    grad_conv, grad_gated = grad_conv_call(
        own.reshape(query_in.shape), other.reshape(query_in.shape), qf
    )
    grad_conv = exchange(grad_conv)

    part = shape((4, BLK, half))
    sums = whole(
        weight_grad_kernel,
        "grad_weight",
        [at, columns, gated_own, gated_other],
        [part] * 8,
        flops=2_200_000_000,
        scratch=[pltpu.VMEM((4, 4, BLK, half), bf16)],
    )
    sums_a = deliver(sums[:4], move_z)
    sums_b = deliver(sums[4:], move_x)

    mixed = whole(
        mixed_kernel,
        "mixed",
        [at, gated_own, gated_other, weights],
        [shape((2 * positions, half), f32)] + [shape((2 * positions, half))] * 3,
        flops=2_200_000_000,
    )
    mixed = deliver(mixed, move_y)
    pieces = [shape((BLK, half), f32)] + [shape((BLK, half))] * 3
    sums_a = deliver(whole(sum_split_kernel, "sum_a", sums_a, pieces, index=False), move_x)
    sums_b = deliver(whole(sum_split_kernel, "sum_b", sums_b, pieces, index=False), move_z)
    keep, send = whole(
        mixed_sum_kernel, "mixed_sum", mixed, [shape((positions, half))] * 2, index=False
    )
    (mixed_out,) = whole(
        mixed_out_kernel, "mixed_out", [at, keep, swap_core(send)], [shape((positions, channels))]
    )
    mixed_out = mixed_out.reshape(query_in.shape)
    (grad_weight,) = whole(
        weight_out_kernel,
        "weight_out",
        [*sums_a, *sums_b],
        [shape((BLK, channels), f32)],
        index=False,
    )

    first_q = (grad_gated[:, :HALO] * conv[:, :HALO].astype(f32)).astype(bf16)[None]
    after_q = next_context(first_q, -1)
    grad_query = grad_query_call(taps, after_q, grad_gated, conv)

    grad_product = exchange(convolve(corr_kernel, "corr", grad_conv, tiles))
    grad_long = grad_long_call(scale, prod, grad_conv)
    grad_product, first_kv = unpack(grad_product, kf, vf)
    after_kv = next_context(first_kv, -1)
    grad_key, grad_value = grad_kv_call(taps, after_kv, grad_product, kf, vf)
    return (mixed_out, grad_query, grad_key, grad_value, grad_weight, grad_long)


def solution(mesh):
    act = P(None, "context", "tensor")
    in_specs = (
        act,
        act,
        act,
        P(None, None, "tensor"),
        P(("tensor", "context"), None),
        P("context", "tensor"),
        act,
    )
    out_specs = (act, act, act, act, P("context", "tensor"), P(("tensor", "context"), None))
    return jax.shard_map(body, mesh=mesh, in_specs=in_specs, out_specs=out_specs, check_vma=False)
```

time: 457 us -> 215 us (0.47)
  waiting for transfers between devices: 202 us -> 40.7 us
  matrix products: 73.3 us -> 0 us
  starting transfers between devices: 13.1 us -> 76.7 us
  local copies, waits for them, and re-layouts: 90.6 us -> 35.1 us
  Pallas kernels: 0 us -> 53.6 us
  blocking collectives: 30.9 us -> 0 us
  other arithmetic: 23.9 us -> 3.82 us
  between operations: 14.7 us -> 1.06 us
    all_gather x2 -> x0, waiting for transfers between devices: 82.6 us -> none  [the longest x1 55.3 us: body(): weight_rows = lax.all_gather(out_weight, 'context', axis=0, tiled=True)]
    dot_general x39 -> x0, matrix products: 73.3 us -> none  [the longest x1 8.36 us: body(): jnp.einsum('blo,oc->blc', columns, weight_rows, preferred_element_type=jn...]
    unnamed x5 -> x0, waiting for transfers between devices: 69.2 us -> none
    pallas_call x0 -> x19, Pallas kernels: none -> 53.6 us  [the longest x8 28.4 us: whole(): pl.pallas_call(kernel, in_specs=([smem] if index else []) + vmem(len(ins)...]
    ppermute x2 -> x37, starting transfers between devices: 2.84 us -> 54.2 us  [the longest x28 41.9 us: move_ctx(): return lax.ppermute(value, 'context', pairs)]
    ppermute x2 -> x37, waiting for transfers between devices: 1.01 us -> 40.7 us  [the longest x28 26.6 us: move_ctx(): return lax.ppermute(value, 'context', pairs)]
    all_to_all x2 -> x0, blocking collectives: 30.9 us -> none  [the longest x1 15.6 us: body(): lax.all_to_all(product, 'context', split_axis=2, concat_axis=1, tiled=True)]
    reduce_scatter x1 -> x0, waiting for transfers between devices: 29.9 us -> none  [body(): lax.psum_scatter(block_out.astype(jnp.bfloat16), 'tensor', scatter_dimens...]
  transfers between devices with their start and end apart: 8 -> 41, of which waited for: 7 -> 10; matrix products, arithmetic and copies ran while one was open for 7% -> 4% of each run, Pallas kernels for 0% -> 24%
where the time goes in v1:
time: 215 us; the launch traced here: 211 us
  starting transfers between devices  76.7 us (36%)
  Pallas kernels  53.6 us (25%)
  waiting for transfers between devices  40.7 us (19%)
  local copies, waits for them, and re-layouts  35.1 us (16%)
  other arithmetic  3.82 us (2%)
    ppermute x28, starting transfers between devices, move_ctx(): return lax.ppermute(value, 'context', pairs)  41.9 us
    unnamed x86, local copies, waits for them, and re-layouts  31.9 us
    pallas_call x8, Pallas kernels, whole(): pl.pallas_call(kernel, in_specs=([smem] if index else []) + vmem(len(ins)...  28.4 us
    ppermute x28, waiting for transfers between devices, move_ctx(): return lax.ppermute(value, 'context', pairs)  26.6 us
    all_to_all x4, starting transfers between devices, exchange(): lax.all_to_all(value, 'context', split_axis=0, concat_axis=0, tiled=True)  22.5 us
    ppermute x6, waiting for transfers between devices, move_y(): return lax.ppermute(value, 'tensor', [(i, (i + d) % NY) for i in range(NY)])  12.2 us
    ppermute x6, starting transfers between devices, move_y(): return lax.ppermute(value, 'tensor', [(i, (i + d) % NY) for i in range(NY)])  8.45 us
    pallas_call x1, Pallas kernels, featurize(): pl.pallas_call(featurize_kernel, grid=(1024 // CB,), in_specs=[taps_spec,...  4.65 us
  transfers between devices with their start and end apart: 41, of which 10 were waited for; matrix products, arithmetic and copies ran while one was open for 4% of the time, Pallas kernels for 24%

profile of v1, /device:TPU:0, one launch (start us, length us, event | category | flops | bytes accessed | tf_op | source)
XLA Modules:
  0.0 211.0 jit_solution(8799368454190842872)
XLA Ops:
  9.2 4.8 %collective-permute-start.14 = (bf16[128,512]{1,0:T(8,128)(2,1)}, bf16[128,512]{1,0:T(8,128)(2,1)}, u32[]{:S(2)}, u32[]{:S(2)}) collective-permute-start(bf16[128,512]{1,0:T(8,128)(2,1)} %get-tuple-element.56), channel_id=1, source_target_pairs={{0,96},{4,100},{8,104},{12,108},{16,112},{20,116},{24,120},{28,124... | collective-permute-start | bytes 393224 | tf_op jit(solution)/shard_map/ppermute | solution.py:29
  20.7 4.7 %featurize.1 = (bf16[32,2,2,16,128]{4,3,2,1,0:T(8,128)(2,1)S(1)}, f32[2,128,1024]{2,1,0:T(8,128)S(1)}, f32[2,128,1024]{2,1,0:T(8,128)S(1)}, f32[2,128,1024]{2,1,0:T(8,128)S(1)}) custom-call(f32[24,64]{1,0:T(8,128)S(1)} %pad.4.taps_ref, bf16[3,2,16,1024]{3,2,1,0:T(8,128)(2,1)S(1)} %copy-done.31, bf16[2,128,1024]{2,1,0:T(8,128)(2,1)S(1)} %copy-done.4, ...), custom_call_target="tpu_custom_call" | custom-call | flops 12000000 | bytes 5500000 | tf_op jit(solution)/shard_map/featurize/pallas_call | solution.py:141
  26.2 7.3 %all-to-all-start = ((bf16[32,2,2,16,128]{4,3,2,1,0:T(8,128)(2,1)}), bf16[32,2,2,16,128]{4,3,2,1,0:T(8,128)(2,1)}, u32[]{:S(2)}, u32[]{:S(2)}) async-start(bf16[32,2,2,16,128]{4,3,2,1,0:T(8,128)(2,1)} %copy-done.19), calls=%async_computation | async-start | bytes 1048576 | tf_op jit(solution)/shard_map/all_to_all | solution.py:531
  33.4 3.0 %collective-permute-start.8 = (bf16[128,512]{1,0:T(8,128)(2,1)S(1)}, bf16[128,512]{1,0:T(8,128)(2,1)S(1)}, u32[]{:S(2)}, u32[]{:S(2)}) collective-permute-start(bf16[128,512]{1,0:T(8,128)(2,1)S(1)} %get-tuple-element.55), channel_id=1, source_target_pairs={{0,24},{4,28},{8,0},{12,4},{16,8},{20,12},{24,16},{28,20},{32,56},... | collective-permute-start | bytes 393224 | tf_op jit(solution)/shard_map/ppermute | solution.py:29
  45.1 2.7 %collective-permute-start.16 = (bf16[4,128,512]{2,1,0:T(8,128)(2,1)}, bf16[4,128,512]{2,1,0:T(8,128)(2,1)}, u32[]{:S(2)}, u32[]{:S(2)}) collective-permute-start(bf16[4,128,512]{2,1,0:T(8,128)(2,1)} %pad_maximum_fusion.1.refs_8_), channel_id=1, source_target_pairs={{0,16},{4,20},{8,24},{12,28},{16,0},{20,4},{24,8},{28,12},{32,48},... | collective-permute-start | bytes 1572872 | tf_op jit(solution)/shard_map/ppermute | solution.py:29
  50.9 2.8 %collective-permute-start.11 = (bf16[4,128,512]{2,1,0:T(8,128)(2,1)}, bf16[4,128,512]{2,1,0:T(8,128)(2,1)}, u32[]{:S(2)}, u32[]{:S(2)}) collective-permute-start(bf16[4,128,512]{2,1,0:T(8,128)(2,1)} %pad_maximum_fusion.refs_4_), channel_id=1, source_target_pairs={{0,96},{4,100},{8,104},{12,108},{16,112},{20,116},{24,120},{28,124... | collective-permute-start | bytes 1572872 | tf_op jit(solution)/shard_map/ppermute | solution.py:29
  63.5 6.0 %all-to-all-start.1 = ((bf16[32,2,2,16,128]{4,3,2,1,0:T(8,128)(2,1)}), bf16[32,2,2,16,128]{4,3,2,1,0:T(8,128)(2,1)}, u32[]{:S(2)}, u32[]{:S(2)}) async-start(bf16[32,2,2,16,128]{4,3,2,1,0:T(8,128)(2,1)} %copy-done.10), calls=%async_computation.1 | async-start | bytes 1048576 | tf_op jit(solution)/shard_map/all_to_all | solution.py:531
  73.7 3.0 %collective-permute-start.5 = (bf16[512,512]{1,0:T(8,128)(2,1)}, bf16[512,512]{1,0:T(8,128)(2,1)}, u32[]{:S(2)}, u32[]{:S(2)}) collective-permute-start(bf16[512,512]{1,0:T(8,128)(2,1)} %constant_dynamic-update-slice_fusion.refs_0_), channel_id=1, source_target_pairs={{0,3},{1,0},{2,1},{3,2},{4,7},{5,4},{6,5},{7,6},{8,11},{9,8},{10,9... | collective-permute-start | bytes 1572872 | tf_op jit(solution)/shard_map/ppermute | solution.py:45
  77.3 3.4 %collective-permute-done.11.refs_7_ = bf16[4,128,512]{2,1,0:T(8,128)(2,1)} collective-permute-done((bf16[4,128,512]{2,1,0:T(8,128)(2,1)}, bf16[4,128,512]{2,1,0:T(8,128)(2,1)}, u32[]{:S(2)}, u32[]{:S(2)}) %collective-permute-start.11) | collective-permute-done | bytes 524320 | tf_op jit(solution)/shard_map/ppermute | solution.py:29
  85.4 5.5 %collective-permute-done.9.refs_5_ = bf16[4,128,512]{2,1,0:T(8,128)(2,1)} collective-permute-done((bf16[4,128,512]{2,1,0:T(8,128)(2,1)}, bf16[4,128,512]{2,1,0:T(8,128)(2,1)}, u32[]{:S(2)}, u32[]{:S(2)}) %collective-permute-start.9) | collective-permute-done | bytes 524320 | tf_op jit(solution)/shard_map/ppermute | solution.py:29
  90.9 8.5 %collective-permute-done.5.refs_3_ = bf16[512,512]{1,0:T(8,128)(2,1)} collective-permute-done((bf16[512,512]{1,0:T(8,128)(2,1)}, bf16[512,512]{1,0:T(8,128)(2,1)}, u32[]{:S(2)}, u32[]{:S(2)}) %collective-permute-start.5) | collective-permute-done | bytes 524320 | tf_op jit(solution)/shard_map/ppermute | solution.py:45
  99.5 3.7 %collective-permute-done.3.refs_1_ = bf16[512,512]{1,0:T(8,128)(2,1)} collective-permute-done((bf16[512,512]{1,0:T(8,128)(2,1)}, bf16[512,512]{1,0:T(8,128)(2,1)}, u32[]{:S(2)}, u32[]{:S(2)}) %collective-permute-start.3) | collective-permute-done | bytes 524320 | tf_op jit(solution)/shard_map/ppermute | solution.py:45
  103.2 8.3 %grad_gated.1 = (f32[256,1024]{1,0:T(8,128)}, bf16[256,1024]{1,0:T(8,128)(2,1)S(1)}, bf16[4,512,512]{2,1,0:T(8,128)(2,1)}, bf16[4,4,128,1024]{3,2,1,0:T(8,128)(2,1)}) custom-call(s32[4]{0:T(128)S(1)} %pad_add_fusion.at, bf16[512,512]{1,0:T(8,128)(2,1)} %constant_dynamic-update-slice_fusion.refs_0_, bf16[512,512]{1,0:T(8,128)(2,1)} %collective-permute-done.3.refs_1_, ...), custom_call_target="tpu_custom_call" | custom-call | flops 2200000000 | bytes 14155792 | tf_op jit(solution)/shard_map/grad_gated/pallas_call | solution.py:393
  111.5 5.0 %mixed.1 = (f32[512,512]{1,0:T(8,128)S(1)}, bf16[512,512]{1,0:T(8,128)(2,1)}, bf16[512,512]{1,0:T(8,128)(2,1)S(1)}, bf16[512,512]{1,0:T(8,128)(2,1)S(1)}) custom-call(s32[4]{0:T(128)S(1)} %pad_add_fusion.at, bf16[256,1024]{1,0:T(8,128)(2,1)S(1)} %bitcast.27, bf16[256,1024]{1,0:T(8,128)(2,1)S(1)} %collective-permute-done.1.other_g, ...), custom_call_target="tpu_custom_call" | custom-call | flops 2200000000 | bytes 7864336 | tf_op jit(solution)/shard_map/mixed/pallas_call | solution.py:393
  119.1 4.8 %grad_weight.1 = (bf16[4,128,512]{2,1,0:T(8,128)(2,1)S(1)}, bf16[4,128,512]{2,1,0:T(8,128)(2,1)}, bf16[4,128,512]{2,1,0:T(8,128)(2,1)}, bf16[4,128,512]{2,1,0:T(...) custom-call(s32[4]{0:T(128)S(1)} %pad_add_fusion.at, ...), custom_call_target="tpu_custom_call" | custom-call | flops 2200000000 | bytes 7340048 | tf_op jit(solution)/shard_map/grad_weight/pallas_call | solution.py:393
  132.7 4.9 %all-to-all-start.2 = ((bf16[32,2,2,16,128]{4,3,2,1,0:T(8,128)(2,1)}), bf16[32,2,2,16,128]{4,3,2,1,0:T(8,128)(2,1)S(1)}, u32[]{:S(2)}, u32[]{:S(2)}) async-start(bf16[32,2,2,16,128]{4,3,2,1,0:T(8,128)(2,1)} %copy-done.20), calls=%async_computation.2 | async-start | bytes 1048576 | tf_op jit(solution)/shard_map/all_to_all | solution.py:531
  144.9 10.9 %collective-permute-done.25.refs_1_ = bf16[4,128,512]{2,1,0:T(8,128)(2,1)} collective-permute-done((bf16[4,128,512]{2,1,0:T(8,128)(2,1)}, bf16[4,128,512]{2,1,0:T(8,128)(2,1)}, u32[]{:S(2)}, u32[]{:S(2)}) %collective-permute-start.25) | collective-permute-done | bytes 524320 | tf_op jit(solution)/shard_map/ppermute | solution.py:29
  156.4 3.1 %collective-permute-start.32 = (bf16[4,128,512]{2,1,0:T(8,128)(2,1)}, bf16[4,128,512]{2,1,0:T(8,128)(2,1)}, u32[]{:S(2)}, u32[]{:S(2)}) collective-permute-start(bf16[4,128,512]{2,1,0:T(8,128)(2,1)} %copy-done.35), channel_id=1, source_target_pairs={{0,16},{4,20},{8,24},{12,28},{16,0},{20,4},{24,8},{28,12},{32,48},... | collective-permute-start | bytes 1572872 | tf_op jit(solution)/shard_map/ppermute | solution.py:29
  165.8 4.4 %all-to-all-start.3 = ((bf16[32,2,2,16,128]{4,3,2,1,0:T(8,128)(2,1)}), bf16[32,2,2,16,128]{4,3,2,1,0:T(8,128)(2,1)S(1)}, u32[]{:S(2)}, u32[]{:S(2)}) async-start(bf16[32,2,2,16,128]{4,3,2,1,0:T(8,128)(2,1)} %copy-done.9), calls=%async_computation.3 | async-start | bytes 1048576 | tf_op jit(solution)/shard_map/all_to_all | solution.py:531
  175.4 2.7 %collective-permute-start.29 = (bf16[128,512]{1,0:T(8,128)(2,1)}, bf16[128,512]{1,0:T(8,128)(2,1)}, u32[]{:S(2)}, u32[]{:S(2)}) collective-permute-start(bf16[128,512]{1,0:T(8,128)(2,1)} %get-tuple-element.82), channel_id=1, source_target_pairs={{0,16},{4,20},{8,24},{12,28},{16,0},{20,4},{24,8},{28,12},{32,48},... | collective-permute-start | bytes 393224 | tf_op jit(solution)/shard_map/ppermute | solution.py:29
  178.0 3.0 %collective-permute-done.31.refs_1_ = bf16[4,128,512]{2,1,0:T(8,128)(2,1)} collective-permute-done((bf16[4,128,512]{2,1,0:T(8,128)(2,1)}, bf16[4,128,512]{2,1,0:T(8,128)(2,1)}, u32[]{:S(2)}, u32[]{:S(2)}) %collective-permute-start.31) | collective-permute-done | bytes 524320 | tf_op jit(solution)/shard_map/ppermute | solution.py:29
  192.8 2.7 %collective-permute-start.35 = (bf16[128,512]{1,0:T(8,128)(2,1)}, bf16[128,512]{1,0:T(8,128)(2,1)S(1)}, u32[]{:S(2)}, u32[]{:S(2)}) collective-permute-start(bf16[128,512]{1,0:T(8,128)(2,1)} %copy-done.41), channel_id=1, source_target_pairs={{0,64},{4,68},{8,72},{12,76},{16,80},{20,84},{24,88},{28,92},{32,9... | collective-permute-start | bytes 393224 | tf_op jit(solution)/shard_map/ppermute | solution.py:29
  198.2 4.1 %grad_long.1 = f32[2,1,4096]{2,1,0:T(1,128)S(1)} custom-call(bf16[32,2,2,16,128]{4,3,2,1,0:T(8,128)(2,1)} %all-to-all-done.x_ref.p_ref, bf16[32,2,2,16,128]{4,3,2,1,0:T(8,128)(2,1)S(1)} %all-to-all-done.2.x_ref.g_ref), custom_call_target="tpu_custom_call" | custom-call | flops 2200000000 | bytes 1200000 | tf_op jit(solution)/shard_map/grad_long/pallas_call | solution.py:247
  205.5 3.6 %grad_kv.1 = (bf16[2,128,1024]{2,1,0:T(8,128)(2,1)}, bf16[2,128,1024]{2,1,0:T(8,128)(2,1)}) custom-call(f32[24,64]{1,0:T(8,128)S(1)} %pad.4.taps_ref, bf16[2,2,16,1024]{3,2,1,0:T(8,128)(2,1)S(1)} %collective-permute-done.24.halo_ref, bf16[2,128,1024]{2,1,0:T(8,128)(2,1)S(1)} %get-tuple-element.72.gp_ref, f32[2,128,1024]{2,1,0:T(8,128)S(1)} %get-tuple-element.69.kf_ref, ...), custom_call_target="tpu_custom_call" | custom-call | flops 8000000 | bytes 4000000 | tf_op jit(solution)/shard_map/grad_kv/pallas_call | solution.py:365
  (171 shorter events, 97.0 us)
Async XLA Ops:
  9.2 28.1 %collective-permute-start.14 = (bf16[128,512]{1,0:T(8,128)(2,1)}, bf16[128,512]{1,0:T(8,128)(2,1)}, u32[]{:S(2)}, u32[]{:S(2)}) collective-permute-start(bf16[128,512]{1,0:T(8,128)(2,1)} %get-tuple-element.56), channel_id=1, source_target_pairs={{0,96},{4,100},{8,104},{12,108},{16,112},{20,116},{24,120},{28,124... | collective-permute-start | bytes 393224 | tf_op jit(solution)/shard_map/ppermute | solution.py:29
  14.0 24.2 %collective-permute-start.13 = (bf16[128,512]{1,0:T(8,128)(2,1)}, bf16[128,512]{1,0:T(8,128)(2,1)}, u32[]{:S(2)}, u32[]{:S(2)}) collective-permute-start(bf16[128,512]{1,0:T(8,128)(2,1)} %get-tuple-element.56), channel_id=1, source_target_pairs={{0,64},{4,68},{8,72},{12,76},{16,80},{20,84},{24,88},{28,92},{32,9... | collective-permute-start | bytes 393224 | tf_op jit(solution)/shard_map/ppermute | solution.py:29
  14.0 24.2 %collective-permute-start.12 = (bf16[128,512]{1,0:T(8,128)(2,1)}, bf16[128,512]{1,0:T(8,128)(2,1)}, u32[]{:S(2)}, u32[]{:S(2)}) collective-permute-start(bf16[128,512]{1,0:T(8,128)(2,1)} %get-tuple-element.56), channel_id=1, source_target_pairs={{0,32},{4,36},{8,40},{12,44},{16,48},{20,52},{24,56},{28,60},{32,6... | collective-permute-start | bytes 393224 | tf_op jit(solution)/shard_map/ppermute | solution.py:29
  26.2 31.9 %all-to-all-start = ((bf16[32,2,2,16,128]{4,3,2,1,0:T(8,128)(2,1)}), bf16[32,2,2,16,128]{4,3,2,1,0:T(8,128)(2,1)}, u32[]{:S(2)}, u32[]{:S(2)}) async-start(bf16[32,2,2,16,128]{4,3,2,1,0:T(8,128)(2,1)} %copy-done.19), calls=%async_computation | async-start | bytes 1048576 | tf_op jit(solution)/shard_map/all_to_all | solution.py:531
  40.1 31.8 %collective-permute-start.17 = (bf16[4,128,512]{2,1,0:T(8,128)(2,1)}, bf16[4,128,512]{2,1,0:T(8,128)(2,1)}, u32[]{:S(2)}, u32[]{:S(2)}) collective-permute-start(bf16[4,128,512]{2,1,0:T(8,128)(2,1)} %pad_maximum_fusion.1.refs_8_), channel_id=1, source_target_pairs={{0,24},{4,28},{8,0},{12,4},{16,8},{20,12},{24,16},{28,20},{32,56},... | collective-permute-start | bytes 1572872 | tf_op jit(solution)/shard_map/ppermute | solution.py:29
  45.1 28.6 %collective-permute-start.16 = (bf16[4,128,512]{2,1,0:T(8,128)(2,1)}, bf16[4,128,512]{2,1,0:T(8,128)(2,1)}, u32[]{:S(2)}, u32[]{:S(2)}) collective-permute-start(bf16[4,128,512]{2,1,0:T(8,128)(2,1)} %pad_maximum_fusion.1.refs_8_), channel_id=1, source_target_pairs={{0,16},{4,20},{8,24},{12,28},{16,0},{20,4},{24,8},{28,12},{32,48},... | collective-permute-start | bytes 1572872 | tf_op jit(solution)/shard_map/ppermute | solution.py:29
  47.8 28.9 %collective-permute-start.15 = (bf16[4,128,512]{2,1,0:T(8,128)(2,1)}, bf16[4,128,512]{2,1,0:T(8,128)(2,1)}, u32[]{:S(2)}, u32[]{:S(2)}) collective-permute-start(bf16[4,128,512]{2,1,0:T(8,128)(2,1)} %pad_maximum_fusion.1.refs_8_), channel_id=1, source_target_pairs={{0,8},{4,12},{8,16},{12,20},{16,24},{20,28},{24,0},{28,4},{32,40},... | collective-permute-start | bytes 1572872 | tf_op jit(solution)/shard_map/ppermute | solution.py:29
  50.9 29.8 %collective-permute-start.11 = (bf16[4,128,512]{2,1,0:T(8,128)(2,1)}, bf16[4,128,512]{2,1,0:T(8,128)(2,1)}, u32[]{:S(2)}, u32[]{:S(2)}) collective-permute-start(bf16[4,128,512]{2,1,0:T(8,128)(2,1)} %pad_maximum_fusion.refs_4_), channel_id=1, source_target_pairs={{0,96},{4,100},{8,104},{12,108},{16,112},{20,116},{24,120},{28,124... | collective-permute-start | bytes 1572872 | tf_op jit(solution)/shard_map/ppermute | solution.py:29
  57.2 28.1 %collective-permute-start.10 = (bf16[4,128,512]{2,1,0:T(8,128)(2,1)}, bf16[4,128,512]{2,1,0:T(8,128)(2,1)}, u32[]{:S(2)}, u32[]{:S(2)}) collective-permute-start(bf16[4,128,512]{2,1,0:T(8,128)(2,1)} %pad_maximum_fusion.refs_4_), channel_id=1, source_target_pairs={{0,64},{4,68},{8,72},{12,76},{16,80},{20,84},{24,88},{28,92},{32,9... | collective-permute-start | bytes 1572872 | tf_op jit(solution)/shard_map/ppermute | solution.py:29
  73.7 25.8 %collective-permute-start.5 = (bf16[512,512]{1,0:T(8,128)(2,1)}, bf16[512,512]{1,0:T(8,128)(2,1)}, u32[]{:S(2)}, u32[]{:S(2)}) collective-permute-start(bf16[512,512]{1,0:T(8,128)(2,1)} %constant_dynamic-update-slice_fusion.refs_0_), channel_id=1, source_target_pairs={{0,3},{1,0},{2,1},{3,2},{4,7},{5,4},{6,5},{7,6},{8,11},{9,8},{10,9... | collective-permute-start | bytes 1572872 | tf_op jit(solution)/shard_map/ppermute | solution.py:45
  76.7 22.8 %collective-permute-start.4 = (bf16[512,512]{1,0:T(8,128)(2,1)}, bf16[512,512]{1,0:T(8,128)(2,1)}, u32[]{:S(2)}, u32[]{:S(2)}) collective-permute-start(bf16[512,512]{1,0:T(8,128)(2,1)} %constant_dynamic-update-slice_fusion.refs_0_), channel_id=1, source_target_pairs={{0,2},{1,3},{2,0},{3,1},{4,6},{5,7},{6,4},{7,5},{8,10},{9,11},{10,... | collective-permute-start | bytes 1572872 | tf_op jit(solution)/shard_map/ppermute | solution.py:45
  85.4 26.2 %collective-permute-start.1 = (bf16[256,1024]{1,0:T(8,128)(2,1)S(1)}, bf16[256,1024]{1,0:T(8,128)(2,1)S(1)}, u32[]{:S(2)}, u32[]{:S(2)}) collective-permute-start(bf16[256,1024]{1,0:T(8,128)(2,1)S(1)} %bitcast.26), channel_id=1, source_target_pairs={{0,4},{4,0},{8,12},{12,8},{16,20},{20,16},{24,28},{28,24},{32,36},... | collective-permute-start | bytes 1572872 | tf_op jit(solution)/shard_map/ppermute | solution.py:29
  119.1 24.5 %collective-permute-start.18 = (bf16[512,512]{1,0:T(8,128)(2,1)}, bf16[512,512]{1,0:T(8,128)(2,1)}, u32[]{:S(2)}, u32[]{:S(2)}) collective-permute-start(bf16[512,512]{1,0:T(8,128)(2,1)} %get-tuple-element.59), channel_id=1, source_target_pairs={{0,1},{1,2},{2,3},{3,0},{4,5},{5,6},{6,7},{7,4},{8,9},{9,10},{10,1... | collective-permute-start | bytes 1572872 | tf_op jit(solution)/shard_map/ppermute | solution.py:45
  124.8 31.1 %collective-permute-start.25 = (bf16[4,128,512]{2,1,0:T(8,128)(2,1)}, bf16[4,128,512]{2,1,0:T(8,128)(2,1)}, u32[]{:S(2)}, u32[]{:S(2)}) collective-permute-start(bf16[4,128,512]{2,1,0:T(8,128)(2,1)} %get-tuple-element.77), channel_id=1, source_target_pairs={{0,32},{4,36},{8,40},{12,44},{16,48},{20,52},{24,56},{28,60},{32,6... | collective-permute-start | bytes 1572872 | tf_op jit(solution)/shard_map/ppermute | solution.py:29
  126.3 30.1 %collective-permute-start.26 = (bf16[4,128,512]{2,1,0:T(8,128)(2,1)}, bf16[4,128,512]{2,1,0:T(8,128)(2,1)}, u32[]{:S(2)}, u32[]{:S(2)}) collective-permute-start(bf16[4,128,512]{2,1,0:T(8,128)(2,1)} %get-tuple-element.78), channel_id=1, source_target_pairs={{0,64},{4,68},{8,72},{12,76},{16,80},{20,84},{24,88},{28,92},{32,9... | collective-permute-start | bytes 1572872 | tf_op jit(solution)/shard_map/ppermute | solution.py:29
  127.9 31.6 %collective-permute-start.27 = (bf16[4,128,512]{2,1,0:T(8,128)(2,1)}, bf16[4,128,512]{2,1,0:T(8,128)(2,1)}, u32[]{:S(2)}, u32[]{:S(2)}) collective-permute-start(bf16[4,128,512]{2,1,0:T(8,128)(2,1)} %get-tuple-element.79), channel_id=1, source_target_pairs={{0,96},{4,100},{8,104},{12,108},{16,112},{20,116},{24,120},{28,124... | collective-permute-start | bytes 1572872 | tf_op jit(solution)/shard_map/ppermute | solution.py:29
  132.7 28.2 %all-to-all-start.2 = ((bf16[32,2,2,16,128]{4,3,2,1,0:T(8,128)(2,1)}), bf16[32,2,2,16,128]{4,3,2,1,0:T(8,128)(2,1)S(1)}, u32[]{:S(2)}, u32[]{:S(2)}) async-start(bf16[32,2,2,16,128]{4,3,2,1,0:T(8,128)(2,1)} %copy-done.20), calls=%async_computation.2 | async-start | bytes 1048576 | tf_op jit(solution)/shard_map/all_to_all | solution.py:531
  141.7 31.9 %collective-permute-start.19 = (bf16[512,512]{1,0:T(8,128)(2,1)}, bf16[512,512]{1,0:T(8,128)(2,1)}, u32[]{:S(2)}, u32[]{:S(2)}) collective-permute-start(bf16[512,512]{1,0:T(8,128)(2,1)} %copy-done.38), channel_id=1, source_target_pairs={{0,2},{1,3},{2,0},{3,1},{4,6},{5,7},{6,4},{7,5},{8,10},{9,11},{10,... | collective-permute-start | bytes 1572872 | tf_op jit(solution)/shard_map/ppermute | solution.py:45
  143.7 31.7 %collective-permute-start.20 = (bf16[512,512]{1,0:T(8,128)(2,1)}, bf16[512,512]{1,0:T(8,128)(2,1)}, u32[]{:S(2)}, u32[]{:S(2)}) collective-permute-start(bf16[512,512]{1,0:T(8,128)(2,1)} %copy-done.36), channel_id=1, source_target_pairs={{0,3},{1,0},{2,1},{3,2},{4,7},{5,4},{6,5},{7,6},{8,11},{9,8},{10,9... | collective-permute-start | bytes 1572872 | tf_op jit(solution)/shard_map/ppermute | solution.py:45
  155.8 25.2 %collective-permute-start.31 = (bf16[4,128,512]{2,1,0:T(8,128)(2,1)}, bf16[4,128,512]{2,1,0:T(8,128)(2,1)}, u32[]{:S(2)}, u32[]{:S(2)}) collective-permute-start(bf16[4,128,512]{2,1,0:T(8,128)(2,1)} %copy-done.37), channel_id=1, source_target_pairs={{0,8},{4,12},{8,16},{12,20},{16,24},{20,28},{24,0},{28,4},{32,40},... | collective-permute-start | bytes 1572872 | tf_op jit(solution)/shard_map/ppermute | solution.py:29
  156.4 28.0 %collective-permute-start.32 = (bf16[4,128,512]{2,1,0:T(8,128)(2,1)}, bf16[4,128,512]{2,1,0:T(8,128)(2,1)}, u32[]{:S(2)}, u32[]{:S(2)}) collective-permute-start(bf16[4,128,512]{2,1,0:T(8,128)(2,1)} %copy-done.35), channel_id=1, source_target_pairs={{0,16},{4,20},{8,24},{12,28},{16,0},{20,4},{24,8},{28,12},{32,48},... | collective-permute-start | bytes 1572872 | tf_op jit(solution)/shard_map/ppermute | solution.py:29
  159.5 28.5 %collective-permute-start.33 = (bf16[4,128,512]{2,1,0:T(8,128)(2,1)}, bf16[4,128,512]{2,1,0:T(8,128)(2,1)}, u32[]{:S(2)}, u32[]{:S(2)}) collective-permute-start(bf16[4,128,512]{2,1,0:T(8,128)(2,1)} %copy-done.34), channel_id=1, source_target_pairs={{0,24},{4,28},{8,0},{12,4},{16,8},{20,12},{24,16},{28,20},{32,56},... | collective-permute-start | bytes 1572872 | tf_op jit(solution)/shard_map/ppermute | solution.py:29
  165.8 26.4 %all-to-all-start.3 = ((bf16[32,2,2,16,128]{4,3,2,1,0:T(8,128)(2,1)}), bf16[32,2,2,16,128]{4,3,2,1,0:T(8,128)(2,1)S(1)}, u32[]{:S(2)}, u32[]{:S(2)}) async-start(bf16[32,2,2,16,128]{4,3,2,1,0:T(8,128)(2,1)} %copy-done.9), calls=%async_computation.3 | async-start | bytes 1048576 | tf_op jit(solution)/shard_map/all_to_all | solution.py:531
  184.5 24.7 %collective-permute-start.21 = (bf16[256,512]{1,0:T(8,128)(2,1)}, bf16[256,512]{1,0:T(8,128)(2,1)}, u32[]{:S(2)}, u32[]{:S(2)}) collective-permute-start(bf16[256,512]{1,0:T(8,128)(2,1)} %get-tuple-element.63), channel_id=1, source_target_pairs={{0,4},{4,0},{8,12},{12,8},{16,20},{20,16},{24,28},{28,24},{32,36},... | collective-permute-start | bytes 786440 | tf_op jit(solution)/shard_map/ppermute | solution.py:29
  (59 other events, 400.0 us)

commit v2 on v1

--- a/solution.py
+++ b/solution.py
@@ -14,6 +14,7 @@
 NCTX = NZ * NX * NC
 BLK = 128
 CB = 256
+VMEM_BYTES = 48 * 1024 * 1024
 f32 = jnp.float32
 bf16 = jnp.bfloat16
 
@@ -59,7 +60,7 @@
 
 
 def params(*sem):
-    return pltpu.CompilerParams(dimension_semantics=sem, vmem_limit_bytes=48 * 1024 * 1024)
+    return pltpu.CompilerParams(dimension_semantics=sem, vmem_limit_bytes=VMEM_BYTES)
 
 
 def toeplitz_kernel(filter_ref, tile_ref):
@@ -144,7 +145,7 @@
         in_specs=[taps_spec, halo_spec, pos_spec, pos_spec, pos_spec],
         out_specs=[chan_spec, pos_spec, pos_spec, pos_spec],
         out_shape=[chan_shape(), pos_shape(f32), pos_shape(f32), pos_shape(f32)],
-        compiler_params=params("arbitrary"),
+        compiler_params=pltpu.CompilerParams(vmem_limit_bytes=62 * 1024 * 1024),
         cost_estimate=pl.CostEstimate(flops=12_000_000, bytes_accessed=5_500_000, transcendentals=0),
         name="featurize",
     )(taps, halo, q, k, v)
@@ -396,7 +397,7 @@
         out_specs=vmem(len(outs)),
         out_shape=list(outs),
         scratch_shapes=list(scratch),
-        compiler_params=pltpu.CompilerParams(vmem_limit_bytes=48 * 1024 * 1024),
+        compiler_params=pltpu.CompilerParams(vmem_limit_bytes=VMEM_BYTES),
         cost_estimate=pl.CostEstimate(flops=flops, bytes_accessed=size, transcendentals=0),
         name=name,
     )(*ins)
@@ -406,12 +407,10 @@
     return jax.ShapeDtypeStruct(dims, kind)
 
 
-def prep_kernel(at, q_ref, k_ref, v_ref, w_ref, g_ref, last_ref, wa_ref, wb_ref, mine_ref, theirs_ref):
+def prep_kernel(at, q_ref, k_ref, v_ref, g_ref, last_ref, mine_ref, theirs_ref):
     first_core = at[3] == 0
     for i, src in enumerate((q_ref, k_ref, v_ref)):
         last_ref[i] = src[...]
-    wa_ref[...] = w_ref[:, :512]
-    wb_ref[...] = w_ref[:, 512:]
     for x in range(NX):
         lo = g_ref[:, 256 * x : 256 * x + BLK]
         hi = g_ref[:, 256 * x + BLK : 256 * x + 256]
@@ -419,57 +418,70 @@
         theirs_ref[:, BLK * x : BLK * x + BLK] = jnp.where(first_core, hi, lo)
 
 
-def prep(at, q, k, v, weight, grad_out):
+def prep(at, q, k, v, grad_out):
     rows = pl.BlockSpec((2, HALO, 1024), lambda i: (0, BLK // HALO - 1, 0))
     full = lambda dims: pl.BlockSpec(dims, lambda i: (0,) * len(dims))
     return pl.pallas_call(
         prep_kernel,
         grid=(1,),
-        in_specs=[smem, rows, rows, rows, full((BLK, 1024)), full((256, 1024))],
-        out_specs=[full((3, 2, HALO, 1024)), full((BLK, 512)), full((BLK, 512)), full((256, 512)), full((256, 512))],
+        in_specs=[smem, rows, rows, rows, full((256, 1024))],
+        out_specs=[full((3, 2, HALO, 1024)), full((256, 512)), full((256, 512))],
         out_shape=[
             shape((3, 2, HALO, 1024)),
-            shape((BLK, 512)),
-            shape((BLK, 512)),
             shape((256, 512)),
             shape((256, 512)),
         ],
-        compiler_params=params("arbitrary"),
+        compiler_params=pltpu.CompilerParams(vmem_limit_bytes=62 * 1024 * 1024),
         name="prep",
-    )(at, q, k, v, weight, grad_out)
-
-
-def grad_gated_kernel(at, *refs):
-    cols, part_a, part_b = refs[:4], refs[4:8], refs[8:12]
-    own_ref, other_ref, cols_ref, w_ref = refs[12:]
-    for d in range(4):
-        cols_ref[(at[2] + 4 - d) & 3] = cols[d][...]
-        for e in range(4):
-            w_ref[(at[0] + 4 - d) & 3, (at[1] + 4 - e) & 3, :, :512] = part_a[d][e]
-            w_ref[(at[0] + 4 - e) & 3, (at[1] + 4 - d) & 3, :, 512:] = part_b[d][e]
-
-    def step(n, carry):
-        lanes = pl.ds(pl.multiple_of(n * 256, 256), 256)
-        total = jnp.zeros((512, 256), f32)
-        for y in range(NY):
-            total = total + jnp.dot(
-                cols_ref[y], w_ref[y, :, :, lanes].reshape(512, 256), preferred_element_type=f32
-            )
-        own_ref[:, lanes] = total[:256]
-        other_ref[:, lanes] = total[256:].astype(bf16)
-        return carry
-
-    lax.fori_loop(0, 4, step, 0)
+    )(at, q, k, v, grad_out)
+
+
+def grad_gated_kernel(at, c0, c1, c2, c3, w_ref, own_ref, other_ref):
+    total = jnp.zeros((512, 256), f32)
+    for d, cols in enumerate((c0, c1, c2, c3)):
+        total = total + jnp.dot(
+            cols[...], w_ref[(at[2] + 4 - d) & 3], preferred_element_type=f32
+        )
+    own_ref[...] = total[:256]
+    other_ref[...] = total[256:].astype(bf16)
+
+
+def grad_gated_call(at, columns, weights):
+    fixed = pl.BlockSpec((512, 512), lambda n: (0, 0))
+    return pl.pallas_call(
+        grad_gated_kernel,
+        grid=(4,),
+        in_specs=[smem] + [fixed] * 4 + [pl.BlockSpec((4, 512, 256), lambda n: (0, 0, n))],
+        out_specs=[pl.BlockSpec((256, 256), lambda n: (0, n))] * 2,
+        out_shape=[shape((256, 1024), f32), shape((256, 1024))],
+        compiler_params=params("arbitrary"),
+        cost_estimate=pl.CostEstimate(flops=2_200_000_000, bytes_accessed=7_800_000, transcendentals=0),
+        name="grad_gated",
+    )(at, *columns, weights)
 
 
 def mixed_kernel(at, own_g, other_g, w_ref, *outs):
     for d in range(4):
-        block = w_ref[(at[2] + d) & 3].reshape(512, 1024)
+        block = w_ref[(at[2] + d) & 3]
         for i, src in enumerate((own_g, other_g)):
             part = lax.dot_general(
                 src[...], block, (((1,), (1,)), ((), ())), preferred_element_type=f32
             )
             outs[d][256 * i : 256 * i + 256] = part.astype(outs[d].dtype)
+
+
+def mixed_call(at, own, other, weights):
+    fixed = pl.BlockSpec((256, 1024), lambda n: (0, 0))
+    return pl.pallas_call(
+        mixed_kernel,
+        grid=(2,),
+        in_specs=[smem, fixed, fixed, pl.BlockSpec((4, 256, 1024), lambda n: (0, n, 0))],
+        out_specs=[pl.BlockSpec((512, 256), lambda n: (0, n))] * 4,
+        out_shape=[shape((512, 512), f32)] + [shape((512, 512))] * 3,
+        compiler_params=params("arbitrary"),
+        cost_estimate=pl.CostEstimate(flops=2_200_000_000, bytes_accessed=7_800_000, transcendentals=0),
+        name="mixed",
+    )(at, own, other, weights)
 
 
 def mixed_sum_kernel(own, a_ref, b_ref, c_ref, keep_ref, send_ref):
@@ -487,44 +499,31 @@
         out_ref[:, 256 * x + BLK : 256 * x + 256] = jnp.where(first_core, came, keep)
 
 
-def weight_grad_kernel(at, cols_ref, own_g, other_g, *refs):
-    outs_a, outs_b, held_b = refs[:4], refs[4:8], refs[8]
-    for d in range(4):
-        cols = cols_ref[(at[0] + d) & 3]
-        for n in range(2):
-            lanes = slice(512 * n, 512 * n + 512)
-            total = lax.dot_general(
-                cols[:256], own_g[:, lanes], (((0,), (0,)), ((), ())), preferred_element_type=f32
-            ) + lax.dot_general(
-                cols[256:], other_g[:, lanes], (((0,), (0,)), ((), ())), preferred_element_type=f32
+def weight_grad_kernel(at, c0, c1, c2, c3, own_g, other_g, out_ref):
+    for d, cols in enumerate((c0, c1, c2, c3)):
+        total = 0.0
+        for i, src in enumerate((own_g, other_g)):
+            total = total + lax.dot_general(
+                cols[256 * i : 256 * i + 256],
+                src[...],
+                (((0,), (0,)), ((), ())),
+                preferred_element_type=f32,
             )
-            total = total.astype(bf16)
-            for x in range(NX):
-                block = total[BLK * x : BLK * x + BLK]
-                if n == 0:
-                    outs_a[d][(x + 4 - at[1]) & 3] = block
-                else:
-                    held_b[(x + 4 - at[1]) & 3, d] = block
-    for e in range(4):
-        outs_b[e][...] = held_b[e]
-
-
-def sum_split_kernel(*refs):
-    parts, outs = refs[:4], refs[4:]
-    for e in range(4):
-        total = parts[0][e].astype(f32)
-        for part in parts[1:]:
-            total = total + part[e].astype(f32)
-        outs[e][...] = total.astype(outs[e].dtype)
-
-
-def weight_out_kernel(*refs):
-    out_ref = refs[8]
-    for n in range(2):
-        total = refs[4 * n][...]
-        for part in refs[4 * n + 1 : 4 * n + 4]:
-            total = total + part[...].astype(f32)
-        out_ref[:, 512 * n : 512 * n + 512] = total
+        out_ref[(at[2] + 4 - d) & 3] = total.astype(bf16)
+
+
+def weight_grad_call(at, columns, own, other):
+    fixed = pl.BlockSpec((512, 512), lambda n: (0, 0))
+    return pl.pallas_call(
+        weight_grad_kernel,
+        grid=(2,),
+        in_specs=[smem] + [fixed] * 4 + [pl.BlockSpec((256, 512), lambda n: (0, n))] * 2,
+        out_specs=pl.BlockSpec((4, 512, 512), lambda n: (0, 0, n)),
+        out_shape=shape((4, 512, 1024)),
+        compiler_params=params("arbitrary"),
+        cost_estimate=pl.CostEstimate(flops=2_200_000_000, bytes_accessed=7_800_000, transcendentals=0),
+        name="grad_weight",
+    )(at, *columns, own, other)
 
 
 def exchange(value):
@@ -541,15 +540,18 @@
     half = channels // 2
 
     taps = jnp.pad(short_filter.reshape(3 * TAPS, channels // GROUP), ((0, 3), (0, 0)))
-    last, w_a, w_b, mine, theirs = prep(
-        at, query_in, key_in, value_in, out_weight, grad_out.reshape(positions, channels)
+    same_core = [list(range(c, NCTX, NC)) for c in range(NC)]
+    weights = lax.all_gather(
+        out_weight,
+        "context",
+        axis=0,
+        tiled=True,
+        axis_index_groups=same_core,
+    ).reshape(NY, half, channels)
+    last, mine, theirs = prep(
+        at, query_in, key_in, value_in, grad_out.reshape(positions, channels)
     )
     before = next_context(last, 1)
-
-    w_a = jnp.stack(around(w_a, move_x))
-    w_b = jnp.stack(around(w_b, move_z))
-    w_a = around(w_a, move_z)
-    w_b = around(w_b, move_x)
 
     columns = around(jnp.concatenate([mine, swap_core(theirs)]), move_y)
 
@@ -561,47 +563,21 @@
     gated_own = gated.reshape(positions, channels)
     gated_other = swap_core(gated_own)
 
-    own, other, columns, weights = whole(
-        grad_gated_kernel,
-        "grad_gated",
-        [at, *columns, *w_a, *w_b],
-        [
-            shape((positions, channels), f32),
-            shape((positions, channels)),
-            shape((NY, 2 * positions, half)),
-            shape((NZ, NX, BLK, channels)),
-        ],
-        flops=2_200_000_000,
-    )
+    own, other = grad_gated_call(at, columns, weights)
     other = swap_core(other)
     grad_conv, grad_gated = grad_conv_call(
         own.reshape(query_in.shape), other.reshape(query_in.shape), qf
     )
-    grad_conv = exchange(grad_conv)
-
-    part = shape((4, BLK, half))
-    sums = whole(
-        weight_grad_kernel,
-        "grad_weight",
-        [at, columns, gated_own, gated_other],
-        [part] * 8,
-        flops=2_200_000_000,
-        scratch=[pltpu.VMEM((4, 4, BLK, half), bf16)],
-    )
-    sums_a = deliver(sums[:4], move_z)
-    sums_b = deliver(sums[4:], move_x)
-
-    mixed = whole(
-        mixed_kernel,
-        "mixed",
-        [at, gated_own, gated_other, weights],
-        [shape((2 * positions, half), f32)] + [shape((2 * positions, half))] * 3,
-        flops=2_200_000_000,
-    )
+    grad_conv, gated_own = lax.optimization_barrier((grad_conv, gated_own))
+    grad_conv_all = exchange(grad_conv)
+
+    sums = weight_grad_call(at, columns, gated_own, gated_other).reshape(-1, channels)
+    grad_weight = lax.psum_scatter(
+        sums, "context", scatter_dimension=0, axis_index_groups=same_core, tiled=True
+    ).astype(f32)
+
+    mixed = mixed_call(at, gated_own, gated_other, weights)
     mixed = deliver(mixed, move_y)
-    pieces = [shape((BLK, half), f32)] + [shape((BLK, half))] * 3
-    sums_a = deliver(whole(sum_split_kernel, "sum_a", sums_a, pieces, index=False), move_x)
-    sums_b = deliver(whole(sum_split_kernel, "sum_b", sums_b, pieces, index=False), move_z)
     keep, send = whole(
         mixed_sum_kernel, "mixed_sum", mixed, [shape((positions, half))] * 2, index=False
     )
@@ -609,20 +585,15 @@
         mixed_out_kernel, "mixed_out", [at, keep, swap_core(send)], [shape((positions, channels))]
     )
     mixed_out = mixed_out.reshape(query_in.shape)
-    (grad_weight,) = whole(
-        weight_out_kernel,
-        "weight_out",
-        [*sums_a, *sums_b],
-        [shape((BLK, channels), f32)],
-        index=False,
-    )
-
     first_q = (grad_gated[:, :HALO] * conv[:, :HALO].astype(f32)).astype(bf16)[None]
     after_q = next_context(first_q, -1)
     grad_query = grad_query_call(taps, after_q, grad_gated, conv)
 
-    grad_product = exchange(convolve(corr_kernel, "corr", grad_conv, tiles))
-    grad_long = grad_long_call(scale, prod, grad_conv)
+    grad_product = exchange(convolve(corr_kernel, "corr", grad_conv_all, tiles))
+    grad_long = grad_long_call(scale, prod, grad_conv_all)
+    grad_product, grad_long, grad_query = lax.optimization_barrier(
+        (grad_product, grad_long, grad_query)
+    )
     grad_product, first_kv = unpack(grad_product, kf, vf)
     after_kv = next_context(first_kv, -1)
     grad_key, grad_value = grad_kv_call(taps, after_kv, grad_product, kf, vf)

time: 215 us -> 179 us (0.83); the launches traced: 211 us -> 178 us
  starting transfers between devices: 76.7 us -> 53 us
  local copies, waits for them, and re-layouts: 35.1 us -> 16.3 us
  between operations: 1.06 us -> 14.3 us
  Pallas kernels: 53.6 us -> 48.6 us
    ppermute x28 -> x4, starting transfers between devices: 41.9 us -> 7.36 us  [move_ctx(): return lax.ppermute(value, 'context', pairs)]
    ppermute x28 -> x4, waiting for transfers between devices: 26.6 us -> 0.59 us  [move_ctx(): return lax.ppermute(value, 'context', pairs)]
    pallas_call x8 -> x2, Pallas kernels: 28.4 us -> 4.04 us  [whole(): pl.pallas_call(kernel, in_specs=([smem] if index else []) + vmem(len(ins)...]
    reduce_scatter x0 -> x1, waiting for transfers between devices: none -> 19.3 us  [body(): lax.psum_scatter(sums, 'context', scatter_dimension=0, axis_index_groups=...]
    unnamed x86 -> x46, local copies, waits for them, and re-layouts: 31.9 us -> 14.9 us
    pallas_call x0 -> x3, Pallas kernels: none -> 16.4 us  [the longest x1 5.78 us: grad_gated_call(): pl.pallas_call(grad_gated_kernel, grid=(4,), in_specs=[smem] + [fixed] *...]
    all_to_all x4, starting transfers between devices: 22.5 us -> 31.3 us  [exchange(): lax.all_to_all(value, 'context', split_axis=0, concat_axis=0, tiled=True)]
    all_gather x0 -> x1, waiting for transfers between devices: none -> 5.14 us  [body(): lax.all_gather(out_weight, 'context', axis=0, tiled=True, axis_index_grou...]
  transfers between devices with their start and end apart: 41 -> 19, of which waited for: 10 -> 11; matrix products, arithmetic and copies ran while one was open for 4% -> 2% of each run, Pallas kernels for 24% -> 24%
where the time goes in v2:
time: 179 us; the launch traced here: 178 us
  starting transfers between devices  53 us (30%)
  Pallas kernels  48.6 us (27%)
  waiting for transfers between devices  42.1 us (24%)
  local copies, waits for them, and re-layouts  16.3 us (9%)
  between operations  14.3 us (8%)
  other arithmetic  3.24 us (2%)
    all_to_all x4, starting transfers between devices, exchange(): lax.all_to_all(value, 'context', split_axis=0, concat_axis=0, tiled=True)  31.3 us
    reduce_scatter x1, waiting for transfers between devices, body(): lax.psum_scatter(sums, 'context', scatter_dimension=0, axis_index_groups=...  19.3 us
    unnamed x46, local copies, waits for them, and re-layouts  14.9 us
    ppermute x6, waiting for transfers between devices, move_y(): return lax.ppermute(value, 'tensor', [(i, (i + d) % NY) for i in range(NY)])  12 us
    ppermute x6, starting transfers between devices, move_y(): return lax.ppermute(value, 'tensor', [(i, (i + d) % NY) for i in range(NY)])  10.3 us
    ppermute x4, starting transfers between devices, move_ctx(): return lax.ppermute(value, 'context', pairs)  7.36 us
    pallas_call x1, Pallas kernels, featurize(): pl.pallas_call(featurize_kernel, grid=(1024 // CB,), in_specs=[taps_spec,...  6.16 us
    pallas_call x1, Pallas kernels, grad_gated_call(): pl.pallas_call(grad_gated_kernel, grid=(4,), in_specs=[smem] + [fixed] *...  5.78 us
  transfers between devices with their start and end apart: 19, of which 11 were waited for; matrix products, arithmetic and copies ran while one was open for 2% of the time, Pallas kernels for 24%

profile of v2, /device:TPU:0, one launch (start us, length us, event | category | flops | bytes accessed | tf_op | source)
XLA Modules:
  0.0 177.7 jit_solution(7026545684410059996)
XLA Ops:
  13.9 6.2 %featurize.1 = (bf16[32,2,2,16,128]{4,3,2,1,0:T(8,128)(2,1)}, f32[2,128,1024]{2,1,0:T(8,128)}, f32[2,128,1024]{2,1,0:T(8,128)}, f32[2,128,1024]{2,1,0:T(8,128)}) custom-call(f32[24,64]{1,0:T(8,128)} %pad.4.taps_ref, bf16[3,2,16,1024]{3,2,1,0:T(8,128)(2,1)} %copy-done.20, bf16[2,128,1024]{2,1,0:T(8,128)(2,1)} %q_ref.3, bf16[2,128,1024]{2,1,0:T(8,128)(2,1)} %k_ref.3, ...), custom_call_target="tpu_custom_call" | custom-call | flops 12000000 | bytes 5500000 | tf_op jit(solution)/shard_map/featurize/pallas_call | solution.py:142
  20.1 12.9 %all-to-all-start = ((bf16[32,2,2,16,128]{4,3,2,1,0:T(8,128)(2,1)}), bf16[32,2,2,16,128]{4,3,2,1,0:T(8,128)(2,1)S(1)}, u32[]{:S(2)}, u32[]{:S(2)}) async-start(bf16[32,2,2,16,128]{4,3,2,1,0:T(8,128)(2,1)} %get-tuple-element.41), calls=%async_computation | async-start | bytes 1048576 | tf_op jit(solution)/shard_map/all_to_all | solution.py:530
  34.8 3.1 %collective-permute-start.3 = (bf16[512,512]{1,0:T(8,128)(2,1)S(1)}, bf16[512,512]{1,0:T(8,128)(2,1)S(1)}, u32[]{:S(2)}, u32[]{:S(2)}) collective-permute-start(bf16[512,512]{1,0:T(8,128)(2,1)S(1)} %constant_dynamic-update-slice_fusion.c0), channel_id=1, source_target_pairs={{0,3},{1,0},{2,1},{3,2},{4,7},{5,4},{6,5},{7,6},{8,11},{9,8},{10,9... | collective-permute-start | bytes 1572872 | tf_op jit(solution)/shard_map/ppermute | solution.py:46
  42.4 2.4 %all-to-all-done.x_ref.p_ref = bf16[32,2,2,16,128]{4,3,2,1,0:T(8,128)(2,1)S(1)} async-done(((bf16[32,2,2,16,128]{4,3,2,1,0:T(8,128)(2,1)}), bf16[32,2,2,16,128]{4,3,2,1,0:T(8,128)(2,1)S(1)}, u32[]{:S(2)}, u32[]{:S(2)}) %all-to-all-start) | async-done | bytes 524320 | tf_op jit(solution)/shard_map/all_to_all | solution.py:530
  44.7 2.2 %copy-done.1 = bf16[2,16,256,256]{3,2,1,0:T(8,128)(2,1)S(1)} copy-done((bf16[2,16,256,256]{3,2,1,0:T(8,128)(2,1)S(1)}, bf16[2,16,256,256]{3,2,1,0:T(8,128)(2,1)}, u32[]{:S(2)}) %copy-start.1) | copy-done | bytes 4194328
  46.9 2.3 %conv.1 = bf16[32,2,2,16,128]{4,3,2,1,0:T(8,128)(2,1)} custom-call(bf16[32,2,2,16,128]{4,3,2,1,0:T(8,128)(2,1)S(1)} %all-to-all-done.x_ref.p_ref, bf16[2,16,256,256]{3,2,1,0:T(8,128)(2,1)S(1)} %copy-done.1), custom_call_target="tpu_custom_call" | custom-call | flops 1100000000 | bytes 5300000 | tf_op jit(solution)/shard_map/conv/pallas_call | solution.py:198
  49.2 5.4 %all-to-all-start.1 = ((bf16[32,2,2,16,128]{4,3,2,1,0:T(8,128)(2,1)}), bf16[32,2,2,16,128]{4,3,2,1,0:T(8,128)(2,1)S(1)}, u32[]{:S(2)}, u32[]{:S(2)}) async-start(bf16[32,2,2,16,128]{4,3,2,1,0:T(8,128)(2,1)} %conv.1), calls=%async_computation.1 | async-start | bytes 1048576 | tf_op jit(solution)/shard_map/all_to_all | solution.py:530
  54.7 6.1 %collective-permute-done.3.c3 = bf16[512,512]{1,0:T(8,128)(2,1)S(1)} collective-permute-done((bf16[512,512]{1,0:T(8,128)(2,1)S(1)}, bf16[512,512]{1,0:T(8,128)(2,1)S(1)}, u32[]{:S(2)}, u32[]{:S(2)}) %collective-permute-start.3) | collective-permute-done | bytes 524320 | tf_op jit(solution)/shard_map/ppermute | solution.py:46
  60.8 3.8 %collective-permute-done.1.c1 = bf16[512,512]{1,0:T(8,128)(2,1)} collective-permute-done((bf16[512,512]{1,0:T(8,128)(2,1)S(1)}, bf16[512,512]{1,0:T(8,128)(2,1)}, u32[]{:S(2)}, u32[]{:S(2)}) %collective-permute-start.1) | collective-permute-done | bytes 524320 | tf_op jit(solution)/shard_map/ppermute | solution.py:46
  64.6 5.1 %all-gather.2.cloned.1.call-done = bf16[2048,1024]{1,0:T(8,128)(2,1)} async-done(((bf16[128,1024]{1,0:T(8,128)(2,1)}), bf16[2048,1024]{1,0:T(8,128)(2,1)}) %all-gather.2.cloned.1.call-update) | async-done | bytes 4194320 | tf_op jit(solution)/shard_map/all_gather | solution.py:544
  69.7 5.8 %grad_gated.1 = (f32[256,1024]{1,0:T(8,128)S(1)}, bf16[256,1024]{1,0:T(8,128)(2,1)}) custom-call(s32[4]{0:T(128)S(1)} %copy-done.13, bf16[512,512]{1,0:T(8,128)(2,1)S(1)} %constant_dynamic-update-slice_fusion.c0, bf16[512,512]{1,0:T(8,128)(2,1)} %collective-permute-done.1.c1, bf16[512,512]{1,0:T(8,128)(2,1)} %collective-permute-done.2.c2, ...), custom_call_target="tpu_custom_call" | custom-call | flops 2200000000 | bytes 7800000 | tf_op jit(solution)/shard_map/grad_gated/pallas_call | solution.py:451
  81.7 5.4 %grad_weight.1 = bf16[4,512,1024]{2,1,0:T(8,128)(2,1)} custom-call(s32[4]{0:T(128)S(1)} %copy-done.13, bf16[512,512]{1,0:T(8,128)(2,1)S(1)} %copy-done.12, bf16[512,512]{1,0:T(8,128)(2,1)} %collective-permute-done.1.c1, bf16[512,512]{1,0:T(8,128)(2,1)} %collective-permute-done.2.c2, bf16[512,512]{1,0:T(8,128)(2,1)S(1)} %copy-done.15, ...), custom_call_target="tpu_custom_call" | custom-call | flops 2200000000 | bytes 7800000 | tf_op jit(solution)/shard_map/grad_weight/pallas_call | solution.py:517
  87.1 5.8 %all-to-all-start.2 = ((bf16[32,2,2,16,128]{4,3,2,1,0:T(8,128)(2,1)}), bf16[32,2,2,16,128]{4,3,2,1,0:T(8,128)(2,1)S(1)}, u32[]{:S(2)}, u32[]{:S(2)}) async-start(bf16[32,2,2,16,128]{4,3,2,1,0:T(8,128)(2,1)} %get-tuple-element.50), calls=%async_computation.2 | async-start | bytes 1048576 | tf_op jit(solution)/shard_map/all_to_all | solution.py:530
  95.0 5.2 %mixed.1 = (f32[512,512]{1,0:T(8,128)S(1)}, bf16[512,512]{1,0:T(8,128)(2,1)}, bf16[512,512]{1,0:T(8,128)(2,1)}, bf16[512,512]{1,0:T(8,128)(2,1)}) custom-call(s32[4]{0:T(128)S(1)} %copy-done.13, bf16[256,1024]{1,0:T(8,128)(2,1)S(1)} %bitcast.20, bf16[256,1024]{1,0:T(8,128)(2,1)S(1)} %copy-done.19, bf16[4,512,1024]{2,1,0:T(8,128)(2,1)} %bitcast.26), custom_call_target="tpu_custom_call" | custom-call | flops 2200000000 | bytes 7800000 | tf_op jit(solution)/shard_map/mixed/pallas_call | solution.py:475
  101.5 2.8 %collective-permute-start.8 = (bf16[512,512]{1,0:T(8,128)(2,1)}, bf16[512,512]{1,0:T(8,128)(2,1)}, u32[]{:S(2)}, u32[]{:S(2)}) collective-permute-start(bf16[512,512]{1,0:T(8,128)(2,1)} %get-tuple-element.46), channel_id=1, source_target_pairs={{0,2},{1,3},{2,0},{3,1},{4,6},{5,7},{6,4},{7,5},{8,10},{9,11},{10,... | collective-permute-start | bytes 1572872 | tf_op jit(solution)/shard_map/ppermute | solution.py:46
  106.2 2.2 %copy-done.2 = bf16[2,16,256,256]{3,2,1,0:T(8,128)(2,1)S(1)} copy-done((bf16[2,16,256,256]{3,2,1,0:T(8,128)(2,1)S(1)}, bf16[2,16,256,256]{3,2,1,0:T(8,128)(2,1)}, u32[]{:S(2)}) %copy-start.2) | copy-done | bytes 4194328
  108.4 2.5 %corr.1 = bf16[32,2,2,16,128]{4,3,2,1,0:T(8,128)(2,1)} custom-call(bf16[32,2,2,16,128]{4,3,2,1,0:T(8,128)(2,1)S(1)} %all-to-all-done.2.x_ref.g_ref, bf16[2,16,256,256]{3,2,1,0:T(8,128)(2,1)S(1)} %copy-done.2), custom_call_target="tpu_custom_call" | custom-call | flops 1100000000 | bytes 5300000 | tf_op jit(solution)/shard_map/corr/pallas_call | solution.py:198
  110.9 7.3 %all-to-all-start.3 = ((bf16[32,2,2,16,128]{4,3,2,1,0:T(8,128)(2,1)}), bf16[32,2,2,16,128]{4,3,2,1,0:T(8,128)(2,1)}, u32[]{:S(2)}, u32[]{:S(2)}) async-start(bf16[32,2,2,16,128]{4,3,2,1,0:T(8,128)(2,1)} %corr.1), calls=%async_computation.3 | async-start | bytes 1048576 | tf_op jit(solution)/shard_map/all_to_all | solution.py:530
  123.3 2.7 %grad_query.1 = bf16[2,128,1024]{2,1,0:T(8,128)(2,1)} custom-call(f32[24,64]{1,0:T(8,128)S(1)} %copy-done.10, bf16[1,2,16,1024]{3,2,1,0:T(8,128)(2,1)S(1)} %collective-permute-done.11.halo_ref, f32[2,128,1024]{2,1,0:T(8,128)S(1)} %get-tuple-element.51.gg_ref, bf16[2,128,1024]{2,1,0:T(8,128)(2,1)S(1)} %copy-done.9), custom_call_target="tpu_custom_call" | custom-call | flops 4000000 | bytes 2100000 | tf_op jit(solution)/shard_map/grad_query/pallas_call | solution.py:340
  130.3 6.5 %collective-permute-start.10 = (bf16[256,512]{1,0:T(8,128)(2,1)}, bf16[256,512]{1,0:T(8,128)(2,1)}, u32[]{:S(2)}, u32[]{:S(2)}) collective-permute-start(bf16[256,512]{1,0:T(8,128)(2,1)} %get-tuple-element.49), channel_id=1, source_target_pairs={{0,4},{4,0},{8,12},{12,8},{16,20},{20,16},{24,28},{28,24},{32,36},... | collective-permute-start | bytes 786440 | tf_op jit(solution)/shard_map/ppermute | solution.py:30
  136.8 3.2 %grad_long.1 = f32[2,1,4096]{2,1,0:T(1,128)S(1)} custom-call(bf16[32,2,2,16,128]{4,3,2,1,0:T(8,128)(2,1)S(1)} %all-to-all-done.x_ref.p_ref, bf16[32,2,2,16,128]{4,3,2,1,0:T(8,128)(2,1)S(1)} %all-to-all-done.2.x_ref.g_ref), custom_call_target="tpu_custom_call" | custom-call | flops 2200000000 | bytes 1200000 | tf_op jit(solution)/shard_map/grad_long/pallas_call | solution.py:248
  140.6 2.2 %unpack.1 = (bf16[2,128,1024]{2,1,0:T(8,128)(2,1)S(1)}, bf16[2,2,16,1024]{3,2,1,0:T(8,128)(2,1)S(1)}) custom-call(bf16[32,2,2,16,128]{4,3,2,1,0:T(8,128)(2,1)} %all-to-all-done.3.gp_ref, f32[2,128,1024]{2,1,0:T(8,128)S(1)} %copy-done.3, f32[2,128,1024]{2,1,0:T(8,128)S(1)} %copy-done.4), custom_call_target="tpu_custom_call" | custom-call | flops 500000 | bytes 1200000 | tf_op jit(solution)/shard_map/unpack/pallas_call | solution.py:311
  146.1 3.6 %grad_kv.1 = (bf16[2,128,1024]{2,1,0:T(8,128)(2,1)}, bf16[2,128,1024]{2,1,0:T(8,128)(2,1)}) custom-call(f32[24,64]{1,0:T(8,128)S(1)} %copy-done.10, bf16[2,2,16,1024]{3,2,1,0:T(8,128)(2,1)S(1)} %collective-permute-done.12.halo_ref, bf16[2,128,1024]{2,1,0:T(8,128)(2,1)S(1)} %get-tuple-element.58.gp_ref, f32[2,128,1024]{2,1,0:T(8,128)S(1)} %copy-done.3, ...), custom_call_target="tpu_custom_call" | custom-call | flops 8000000 | bytes 4000000 | tf_op jit(solution)/shard_map/grad_kv/pallas_call | solution.py:366
  149.8 19.3 %reduce-scatter.2.cloned.1.call-done = bf16[128,1024]{1,0:T(8,128)(2,1)} async-done(((bf16[2048,1024]{1,0:T(8,128)(2,1)}), bf16[128,1024]{1,0:T(8,128)(2,1)}) %reduce-scatter.2.cloned.1.call-update) | async-done | bytes 262160 | tf_op jit(solution)/shard_map/reduce_scatter | solution.py:575
  (85 shorter events, 39.5 us)
Async XLA Ops:
  7.2 32.3 %copy-start.21 = (f32[2,4096]{1,0:T(2,128)S(1)}, f32[2,4096]{1,0:T(2,128)}, u32[]{:S(2)}) copy-start(f32[2,4096]{1,0:T(2,128)} %param.11) | copy-start | bytes 98308
  7.2 62.5 %all-gather.2.cloned.1.call-start = ((), (), s32[]{:S(2)}) async-start(), calls=%async_computation.5 | async-start | bytes 4456448 | tf_op jit(solution)/shard_map/all_gather | solution.py:544
  10.6 2.6 %collective-permute-start.5 = (bf16[3,2,16,1024]{3,2,1,0:T(8,128)(2,1)}, bf16[3,2,16,1024]{3,2,1,0:T(8,128)(2,1)S(1)}, u32[]{:S(2)}, u32[]{:S(2)}) collective-permute-start(bf16[3,2,16,1024]{3,2,1,0:T(8,128)(2,1)} %get-tuple-element.38), channel_id=1, source_target_pairs={{0,4},{4,8},{8,12},{12,16},{16,20},{20,24},{24,28},{28,32},{32,36}... | collective-permute-start | bytes 589832 | tf_op jit(solution)/shard_map/ppermute | solution.py:51
  20.1 24.6 %all-to-all-start = ((bf16[32,2,2,16,128]{4,3,2,1,0:T(8,128)(2,1)}), bf16[32,2,2,16,128]{4,3,2,1,0:T(8,128)(2,1)S(1)}, u32[]{:S(2)}, u32[]{:S(2)}) async-start(bf16[32,2,2,16,128]{4,3,2,1,0:T(8,128)(2,1)} %get-tuple-element.41), calls=%async_computation | async-start | bytes 1048576 | tf_op jit(solution)/shard_map/all_to_all | solution.py:530
  33.0 1.8 %collective-permute-start = (bf16[256,512]{1,0:T(8,128)(2,1)}, bf16[256,512]{1,0:T(8,128)(2,1)S(1)}, u32[]{:S(2)}, u32[]{:S(2)}) collective-permute-start(bf16[256,512]{1,0:T(8,128)(2,1)} %get-tuple-element.35), channel_id=1, source_target_pairs={{0,4},{4,0},{8,12},{12,8},{16,20},{20,16},{24,28},{28,24},{32,36},... | collective-permute-start | bytes 786440 | tf_op jit(solution)/shard_map/ppermute | solution.py:30
  34.8 34.9 %copy-start.11 = (bf16[512,512]{1,0:T(8,128)(2,1)}, bf16[512,512]{1,0:T(8,128)(2,1)S(1)}, u32[]{:S(2)}) copy-start(bf16[512,512]{1,0:T(8,128)(2,1)S(1)} %constant_dynamic-update-slice_fusion.c0) | copy-start | bytes 1572868
  34.8 25.9 %collective-permute-start.3 = (bf16[512,512]{1,0:T(8,128)(2,1)S(1)}, bf16[512,512]{1,0:T(8,128)(2,1)S(1)}, u32[]{:S(2)}, u32[]{:S(2)}) collective-permute-start(bf16[512,512]{1,0:T(8,128)(2,1)S(1)} %constant_dynamic-update-slice_fusion.c0), channel_id=1, source_target_pairs={{0,3},{1,0},{2,1},{3,2},{4,7},{5,4},{6,5},{7,6},{8,11},{9,8},{10,9... | collective-permute-start | bytes 1572872 | tf_op jit(solution)/shard_map/ppermute | solution.py:46
  37.9 22.9 %collective-permute-start.2 = (bf16[512,512]{1,0:T(8,128)(2,1)S(1)}, bf16[512,512]{1,0:T(8,128)(2,1)}, u32[]{:S(2)}, u32[]{:S(2)}) collective-permute-start(bf16[512,512]{1,0:T(8,128)(2,1)S(1)} %constant_dynamic-update-slice_fusion.c0), channel_id=1, source_target_pairs={{0,2},{1,3},{2,0},{3,1},{4,6},{5,7},{6,4},{7,5},{8,10},{9,11},{10,... | collective-permute-start | bytes 1572872 | tf_op jit(solution)/shard_map/ppermute | solution.py:46
  38.5 26.0 %collective-permute-start.1 = (bf16[512,512]{1,0:T(8,128)(2,1)S(1)}, bf16[512,512]{1,0:T(8,128)(2,1)}, u32[]{:S(2)}, u32[]{:S(2)}) collective-permute-start(bf16[512,512]{1,0:T(8,128)(2,1)S(1)} %constant_dynamic-update-slice_fusion.c0), channel_id=1, source_target_pairs={{0,1},{1,2},{2,3},{3,0},{4,5},{5,6},{6,7},{7,4},{8,9},{9,10},{10,1... | collective-permute-start | bytes 1572872 | tf_op jit(solution)/shard_map/ppermute | solution.py:46
  46.9 22.8 %copy-start.13 = (s32[4]{0:T(128)S(1)}, s32[4]{0:T(128)}, u32[]{:S(2)}) copy-start(s32[4]{0:T(128)} %pad_add_fusion.at) | copy-start | bytes 52
  49.2 27.2 %all-to-all-start.1 = ((bf16[32,2,2,16,128]{4,3,2,1,0:T(8,128)(2,1)}), bf16[32,2,2,16,128]{4,3,2,1,0:T(8,128)(2,1)S(1)}, u32[]{:S(2)}, u32[]{:S(2)}) async-start(bf16[32,2,2,16,128]{4,3,2,1,0:T(8,128)(2,1)} %conv.1), calls=%async_computation.1 | async-start | bytes 1048576 | tf_op jit(solution)/shard_map/all_to_all | solution.py:530
  54.6 21.9 %copy-start.5 = (f32[2,128,1024]{2,1,0:T(8,128)S(1)}, f32[2,128,1024]{2,1,0:T(8,128)}, u32[]{:S(2)}) copy-start(f32[2,128,1024]{2,1,0:T(8,128)} %get-tuple-element.39.qf_ref) | copy-start | bytes 3145732
  54.6 114.4 %reduce-scatter.2.cloned.1.call-start = ((), (), s32[]{:S(2)}) async-start(), calls=%async_computation.6 | async-start | bytes 4456448 | tf_op jit(solution)/shard_map/reduce_scatter | solution.py:575
  76.5 2.1 %collective-permute-start.4 = (bf16[256,1024]{1,0:T(8,128)(2,1)}, bf16[256,1024]{1,0:T(8,128)(2,1)S(1)}, u32[]{:S(2)}, u32[]{:S(2)}) collective-permute-start(bf16[256,1024]{1,0:T(8,128)(2,1)} %get-tuple-element.37), channel_id=1, source_target_pairs={{0,4},{4,0},{8,12},{12,8},{16,20},{20,16},{24,28},{28,24},{32,36},... | collective-permute-start | bytes 1572872 | tf_op jit(solution)/shard_map/ppermute | solution.py:30
  78.0 3.7 %collective-permute-start.6 = (bf16[256,1024]{1,0:T(8,128)(2,1)S(1)}, bf16[256,1024]{1,0:T(8,128)(2,1)S(1)}, u32[]{:S(2)}, u32[]{:S(2)}) collective-permute-start(bf16[256,1024]{1,0:T(8,128)(2,1)S(1)} %bitcast.18), channel_id=1, source_target_pairs={{0,4},{4,0},{8,12},{12,8},{16,20},{20,16},{24,28},{28,24},{32,36},... | collective-permute-start | bytes 1572872 | tf_op jit(solution)/shard_map/ppermute | solution.py:30
  87.1 19.1 %all-to-all-start.2 = ((bf16[32,2,2,16,128]{4,3,2,1,0:T(8,128)(2,1)}), bf16[32,2,2,16,128]{4,3,2,1,0:T(8,128)(2,1)S(1)}, u32[]{:S(2)}, u32[]{:S(2)}) async-start(bf16[32,2,2,16,128]{4,3,2,1,0:T(8,128)(2,1)} %get-tuple-element.50), calls=%async_computation.2 | async-start | bytes 1048576 | tf_op jit(solution)/shard_map/all_to_all | solution.py:530
  95.0 27.2 %copy-start.10 = (f32[24,64]{1,0:T(8,128)S(1)}, f32[24,64]{1,0:T(8,128)}, u32[]{:S(2)}) copy-start(f32[24,64]{1,0:T(8,128)} %pad.4.taps_ref) | copy-start | bytes 18436
  100.2 25.7 %collective-permute-start.7 = (bf16[512,512]{1,0:T(8,128)(2,1)}, bf16[512,512]{1,0:T(8,128)(2,1)}, u32[]{:S(2)}, u32[]{:S(2)}) collective-permute-start(bf16[512,512]{1,0:T(8,128)(2,1)} %get-tuple-element.45), channel_id=1, source_target_pairs={{0,1},{1,2},{2,3},{3,0},{4,5},{5,6},{6,7},{7,4},{8,9},{9,10},{10,1... | collective-permute-start | bytes 1572872 | tf_op jit(solution)/shard_map/ppermute | solution.py:46
  101.5 26.5 %collective-permute-start.8 = (bf16[512,512]{1,0:T(8,128)(2,1)}, bf16[512,512]{1,0:T(8,128)(2,1)}, u32[]{:S(2)}, u32[]{:S(2)}) collective-permute-start(bf16[512,512]{1,0:T(8,128)(2,1)} %get-tuple-element.46), channel_id=1, source_target_pairs={{0,2},{1,3},{2,0},{3,1},{4,6},{5,7},{6,4},{7,5},{8,10},{9,11},{10,... | collective-permute-start | bytes 1572872 | tf_op jit(solution)/shard_map/ppermute | solution.py:46
  104.4 23.7 %collective-permute-start.9 = (bf16[512,512]{1,0:T(8,128)(2,1)}, bf16[512,512]{1,0:T(8,128)(2,1)}, u32[]{:S(2)}, u32[]{:S(2)}) collective-permute-start(bf16[512,512]{1,0:T(8,128)(2,1)} %get-tuple-element.47), channel_id=1, source_target_pairs={{0,3},{1,0},{2,1},{3,2},{4,7},{5,4},{6,5},{7,6},{8,11},{9,8},{10,9... | collective-permute-start | bytes 1572872 | tf_op jit(solution)/shard_map/ppermute | solution.py:46
  110.9 29.7 %all-to-all-start.3 = ((bf16[32,2,2,16,128]{4,3,2,1,0:T(8,128)(2,1)}), bf16[32,2,2,16,128]{4,3,2,1,0:T(8,128)(2,1)}, u32[]{:S(2)}, u32[]{:S(2)}) async-start(bf16[32,2,2,16,128]{4,3,2,1,0:T(8,128)(2,1)} %corr.1), calls=%async_computation.3 | async-start | bytes 1048576 | tf_op jit(solution)/shard_map/all_to_all | solution.py:530
  119.0 3.1 %collective-permute-start.11 = (bf16[1,2,16,1024]{3,2,1,0:T(8,128)(2,1)S(1)}, bf16[1,2,16,1024]{3,2,1,0:T(8,128)(2,1)S(1)}, u32[]{:S(2)}, u32[]{:S(2)}) collective-permute-start(bf16[1,2,16,1024]{3,2,1,0:T(8,128)(2,1)S(1)} %fusion), channel_id=1, source_target_pairs={{4,0},{8,4},{12,8},{16,12},{20,16},{24,20},{28,24},{32,28},{36,32}... | collective-permute-start | bytes 196616 | tf_op jit(solution)/shard_map/ppermute | solution.py:51
  130.3 13.9 %collective-permute-start.10 = (bf16[256,512]{1,0:T(8,128)(2,1)}, bf16[256,512]{1,0:T(8,128)(2,1)}, u32[]{:S(2)}, u32[]{:S(2)}) collective-permute-start(bf16[256,512]{1,0:T(8,128)(2,1)} %get-tuple-element.49), channel_id=1, source_target_pairs={{0,4},{4,0},{8,12},{12,8},{16,20},{20,16},{24,28},{28,24},{32,36},... | collective-permute-start | bytes 786440 | tf_op jit(solution)/shard_map/ppermute | solution.py:30
  142.9 3.2 %collective-permute-start.12 = (bf16[2,2,16,1024]{3,2,1,0:T(8,128)(2,1)S(1)}, bf16[2,2,16,1024]{3,2,1,0:T(8,128)(2,1)S(1)}, u32[]{:S(2)}, u32[]{:S(2)}) collective-permute-start(bf16[2,2,16,1024]{3,2,1,0:T(8,128)(2,1)S(1)} %get-tuple-element.57), channel_id=1, source_target_pairs={{4,0},{8,4},{12,8},{16,12},{20,16},{24,20},{28,24},{32,28},{36,32}... | collective-permute-start | bytes 393224 | tf_op jit(solution)/shard_map/ppermute | solution.py:51
  (17 other events, 74.6 us)
Sparse Core Ops, SparseCore 0:
  10.2 59.5 all-gather.1
  87.2 81.7 reduce-scatter.1

commit v3 on v2

--- a/solution.py
+++ b/solution.py
@@ -14,7 +14,7 @@
 NCTX = NZ * NX * NC
 BLK = 128
 CB = 256
-VMEM_BYTES = 48 * 1024 * 1024
+VMEM_BYTES = 32 * 1024 * 1024
 f32 = jnp.float32
 bf16 = jnp.bfloat16
 
@@ -95,11 +95,14 @@
     )(long_filter[:, None, :])
 
 
-def spread_taps(taps, block):
-    rows = lax.broadcasted_iota(jnp.int32, (taps.shape[1], CB), 0)
-    cols = lax.broadcasted_iota(jnp.int32, (taps.shape[1], CB), 1)
+def spread_taps(taps_ref, stream, block):
+    groups = taps_ref.shape[2]
+    rows = lax.broadcasted_iota(jnp.int32, (groups, CB), 0)
+    cols = lax.broadcasted_iota(jnp.int32, (groups, CB), 1)
     spread = (rows == ((block * CB + cols) >> 4)).astype(f32)
-    return jnp.dot(taps, spread, precision=lax.Precision.HIGHEST, preferred_element_type=f32)
+    return jnp.dot(
+        taps_ref[stream], spread, precision=lax.Precision.HIGHEST, preferred_element_type=f32
+    )
 
 
 def to_channels(value):
@@ -111,14 +114,15 @@
 
 
 def featurize_kernel(taps_ref, halo_ref, q_ref, k_ref, v_ref, prod_ref, qf_ref, kf_ref, vf_ref):
-    taps = spread_taps(taps_ref[...], pl.program_id(0))
+    spread = [spread_taps(taps_ref, i, pl.program_id(0)) for i in range(3)]
     for b in range(2):
         feats = []
         for i, (src, dst) in enumerate(((q_ref, qf_ref), (k_ref, kf_ref), (v_ref, vf_ref))):
             ext = jnp.concatenate([halo_ref[i, b].astype(f32), src[b].astype(f32)], axis=0)
-            total = taps[7 * i : 7 * i + 1] * ext[HALO:]
+            taps = spread[i]
+            total = taps[:1] * ext[HALO:]
             for j in range(1, TAPS):
-                total = total + taps[7 * i + j : 7 * i + j + 1] * ext[HALO - j : HALO - j + BLK]
+                total = total + taps[j : j + 1] * ext[HALO - j : HALO - j + BLK]
             dst[b] = total
             feats.append(total)
         prod_ref[:, :, b] = to_channels(feats[1] * feats[2])
@@ -126,7 +130,7 @@
 
 chan_spec = pl.BlockSpec((CB // (2 * GROUP), 2, 2, GROUP, BLK), lambda c: (c, 0, 0, 0, 0))
 pos_spec = pl.BlockSpec((2, BLK, CB), lambda c: (0, 0, c))
-taps_spec = pl.BlockSpec((24, 64), lambda c: (0, 0))
+taps_spec = pl.BlockSpec((3, TAPS, 64), lambda c: (0, 0, 0))
 halo_spec = pl.BlockSpec((3, 2, HALO, CB), lambda c: (0, 0, 0, c))
 
 
@@ -320,20 +324,18 @@
     )(gp, kf, vf)
 
 
-def backward_taps(grad, halo, taps, first):
+def backward_taps(grad, halo, taps):
     ext = jnp.concatenate([grad, halo.astype(f32)], axis=0)
-    total = taps[first : first + 1] * grad
+    total = taps[:1] * grad
     for j in range(1, TAPS):
-        total = total + taps[first + j : first + j + 1] * ext[j : j + BLK]
+        total = total + taps[j : j + 1] * ext[j : j + BLK]
     return total.astype(bf16)
 
 
 def grad_query_kernel(taps_ref, halo_ref, gg_ref, conv_ref, out_ref):
-    taps = spread_taps(taps_ref[...], pl.program_id(0))
+    taps = spread_taps(taps_ref, 0, pl.program_id(0))
     for b in range(2):
-        out_ref[b] = backward_taps(
-            gg_ref[b] * conv_ref[b].astype(f32), halo_ref[0, b], taps, 0
-        )
+        out_ref[b] = backward_taps(gg_ref[b] * conv_ref[b].astype(f32), halo_ref[0, b], taps)
 
 
 def grad_query_call(taps, halo, gg, conv):
@@ -355,11 +357,12 @@
 
 
 def grad_kv_kernel(taps_ref, halo_ref, gp_ref, kf_ref, vf_ref, gk_ref, gv_ref):
-    taps = spread_taps(taps_ref[...], pl.program_id(0))
+    key_taps = spread_taps(taps_ref, 1, pl.program_id(0))
+    value_taps = spread_taps(taps_ref, 2, pl.program_id(0))
     for b in range(2):
         grad = gp_ref[b].astype(f32)
-        gk_ref[b] = backward_taps(grad * vf_ref[b], halo_ref[0, b], taps, TAPS)
-        gv_ref[b] = backward_taps(grad * kf_ref[b], halo_ref[1, b], taps, 2 * TAPS)
+        gk_ref[b] = backward_taps(grad * vf_ref[b], halo_ref[0, b], key_taps)
+        gv_ref[b] = backward_taps(grad * kf_ref[b], halo_ref[1, b], value_taps)
 
 
 def grad_kv_call(taps, halo, gp, kf, vf):
@@ -539,7 +542,7 @@
     positions = batches * rows
     half = channels // 2
 
-    taps = jnp.pad(short_filter.reshape(3 * TAPS, channels // GROUP), ((0, 3), (0, 0)))
+    taps = short_filter
     same_core = [list(range(c, NCTX, NC)) for c in range(NC)]
     weights = lax.all_gather(
         out_weight,
@@ -553,30 +556,34 @@
     )
     before = next_context(last, 1)
 
-    columns = around(jnp.concatenate([mine, swap_core(theirs)]), move_y)
+    columns = jnp.concatenate([mine, swap_core(theirs)])
+    columns, before = lax.optimization_barrier((columns, before))
+    columns = around(columns, move_y)
 
     tiles = toeplitz_tiles(long_filter)
     prod, qf, kf, vf = featurize(taps, before, query_in, key_in, value_in)
     prod = exchange(prod)
+    prod, *columns = lax.optimization_barrier((prod, *columns))
     conv = exchange(convolve(conv_kernel, "conv", prod, tiles))
     gated, conv = gate(conv, qf)
     gated_own = gated.reshape(positions, channels)
     gated_other = swap_core(gated_own)
 
+    sums = weight_grad_call(at, columns, gated_own, gated_other).reshape(-1, channels)
+    weights, sums = lax.optimization_barrier((weights, sums))
     own, other = grad_gated_call(at, columns, weights)
     other = swap_core(other)
     grad_conv, grad_gated = grad_conv_call(
         own.reshape(query_in.shape), other.reshape(query_in.shape), qf
     )
-    grad_conv, gated_own = lax.optimization_barrier((grad_conv, gated_own))
+    grad_conv, gated_late = lax.optimization_barrier((grad_conv, gated_own))
     grad_conv_all = exchange(grad_conv)
 
-    sums = weight_grad_call(at, columns, gated_own, gated_other).reshape(-1, channels)
     grad_weight = lax.psum_scatter(
         sums, "context", scatter_dimension=0, axis_index_groups=same_core, tiled=True
     ).astype(f32)
 
-    mixed = mixed_call(at, gated_own, gated_other, weights)
+    mixed = mixed_call(at, gated_late, gated_other, weights)
     mixed = deliver(mixed, move_y)
     keep, send = whole(
         mixed_sum_kernel, "mixed_sum", mixed, [shape((positions, half))] * 2, index=False

time: 179 us -> 173 us (0.966)
  blocking collectives: 0 us -> 18.1 us
  waiting for transfers between devices: 42.1 us -> 26.5 us
  starting transfers between devices: 53 us -> 44.6 us
  Pallas kernels: 48.6 us -> 43.7 us
  local copies, waits for them, and re-layouts: 16.3 us -> 19.9 us
    all_to_all x0 -> x1, blocking collectives: none -> 18.1 us  [exchange(): lax.all_to_all(value, 'context', split_axis=0, concat_axis=0, tiled=True)]
    reduce_scatter x1, waiting for transfers between devices: 19.3 us -> 8.58 us  [body(): lax.psum_scatter(sums, 'context', scatter_dimension=0, axis_index_groups=...]
    ppermute x6, waiting for transfers between devices: 12 us -> 2.13 us  [move_y(): return lax.ppermute(value, 'tensor', [(i, (i + d) % NY) for i in range(NY)])]
    all_to_all x4 -> x3, starting transfers between devices: 31.3 us -> 22.6 us  [exchange(): lax.all_to_all(value, 'context', split_axis=0, concat_axis=0, tiled=True)]
    all_to_all x4 -> x3, waiting for transfers between devices: 2.68 us -> 9.42 us  [exchange(): lax.all_to_all(value, 'context', split_axis=0, concat_axis=0, tiled=True)]
    all_gather x1, waiting for transfers between devices: 5.14 us -> 0.01 us  [body(): lax.all_gather(out_weight, 'context', axis=0, tiled=True, axis_index_grou...]
    unnamed x46 -> x47, local copies, waits for them, and re-layouts: 14.9 us -> 19.9 us
    ppermute x4, waiting for transfers between devices: 0.59 us -> 3.67 us  [move_ctx(): return lax.ppermute(value, 'context', pairs)]
  transfers between devices with their start and end apart: 19 -> 18, of which waited for: 11 -> 9; matrix products, arithmetic and copies ran while one was open for 2% -> 2% of each run, Pallas kernels for 24% -> 25%
where the time goes in v3:
time: 173 us; the launch traced here: 171 us
  starting transfers between devices  44.6 us (26%)
  Pallas kernels  43.7 us (25%)
  waiting for transfers between devices  26.5 us (15%)
  local copies, waits for them, and re-layouts  19.9 us (12%)
  blocking collectives  18.1 us (10%)
  between operations  14.4 us (8%)
  other arithmetic  4.23 us (2%)
    all_to_all x3, starting transfers between devices, exchange(): lax.all_to_all(value, 'context', split_axis=0, concat_axis=0, tiled=True)  22.6 us
    unnamed x47, local copies, waits for them, and re-layouts  19.9 us
    all_to_all x1, blocking collectives, exchange(): lax.all_to_all(value, 'context', split_axis=0, concat_axis=0, tiled=True)  18.1 us
    ppermute x6, starting transfers between devices, move_y(): return lax.ppermute(value, 'tensor', [(i, (i + d) % NY) for i in range(NY)])  10.3 us
    all_to_all x3, waiting for transfers between devices, exchange(): lax.all_to_all(value, 'context', split_axis=0, concat_axis=0, tiled=True)  9.42 us
    reduce_scatter x1, waiting for transfers between devices, body(): lax.psum_scatter(sums, 'context', scatter_dimension=0, axis_index_groups=...  8.58 us
    ppermute x4, starting transfers between devices, move_ctx(): return lax.ppermute(value, 'context', pairs)  6.45 us
    pallas_call x1, Pallas kernels, featurize(): pl.pallas_call(featurize_kernel, grid=(1024 // CB,), in_specs=[taps_spec,...  6.31 us
  transfers between devices with their start and end apart: 18, of which 9 were waited for; matrix products, arithmetic and copies ran while one was open for 2% of the time, Pallas kernels for 25%

profile of v3, /device:TPU:0, one launch (start us, length us, event | category | flops | bytes accessed | tf_op | source)
XLA Modules:
  0.0 171.4 jit_solution(11878340429798472896)
XLA Ops:
  10.7 2.4 %collective-permute-start.1 = (bf16[3,2,16,1024]{3,2,1,0:T(8,128)(2,1)}, bf16[3,2,16,1024]{3,2,1,0:T(8,128)(2,1)S(1)}, u32[]{:S(2)}, u32[]{:S(2)}) collective-permute-start(bf16[3,2,16,1024]{3,2,1,0:T(8,128)(2,1)} %get-tuple-element.45), channel_id=1, source_target_pairs={{0,4},{4,8},{8,12},{12,16},{16,20},{20,24},{24,28},{28,32},{32,36}... | collective-permute-start | bytes 589832 | tf_op jit(solution)/shard_map/ppermute | solution.py:51
  14.3 3.1 %collective-permute-start.4 = (bf16[512,512]{1,0:T(8,128)(2,1)S(1)}, bf16[512,512]{1,0:T(8,128)(2,1)S(1)}, u32[]{:S(2)}, u32[]{:S(2)}) collective-permute-start(bf16[512,512]{1,0:T(8,128)(2,1)S(1)} %pad_maximum_fusion.c0), channel_id=1, source_target_pairs={{0,3},{1,0},{2,1},{3,2},{4,7},{5,4},{6,5},{7,6},{8,11},{9,8},{10,9... | collective-permute-start | bytes 1572872 | tf_op jit(solution)/shard_map/ppermute | solution.py:46
  19.0 6.3 %featurize.1 = (bf16[32,2,2,16,128]{4,3,2,1,0:T(8,128)(2,1)}, f32[2,128,1024]{2,1,0:T(8,128)}, f32[2,128,1024]{2,1,0:T(8,128)}, f32[2,128,1024]{2,1,0:T(8,128)}) custom-call(f32[3,7,64]{2,1,0:T(8,128)} %taps_ref.5, bf16[3,2,16,1024]{3,2,1,0:T(8,128)(2,1)} %copy-done.21, bf16[2,128,1024]{2,1,0:T(8,128)(2,1)} %q_ref.3, bf16[2,128,1024]{2,1,0:T(8,128)(2,1)} %k_ref.3, ...), custom_call_target="tpu_custom_call" | custom-call | flops 12000000 | bytes 5500000 | tf_op jit(solution)/shard_map/featurize/pallas_call | solution.py:146
  25.3 11.7 %all-to-all-start = ((bf16[32,2,2,16,128]{4,3,2,1,0:T(8,128)(2,1)}), bf16[32,2,2,16,128]{4,3,2,1,0:T(8,128)(2,1)S(1)}, u32[]{:S(2)}, u32[]{:S(2)}) async-start(bf16[32,2,2,16,128]{4,3,2,1,0:T(8,128)(2,1)} %get-tuple-element.47), calls=%async_computation | async-start | bytes 1048576 | tf_op jit(solution)/shard_map/all_to_all | solution.py:533
  40.0 8.8 %all-to-all-done.x_ref.p_ref = bf16[32,2,2,16,128]{4,3,2,1,0:T(8,128)(2,1)S(1)} async-done(((bf16[32,2,2,16,128]{4,3,2,1,0:T(8,128)(2,1)}), bf16[32,2,2,16,128]{4,3,2,1,0:T(8,128)(2,1)S(1)}, u32[]{:S(2)}, u32[]{:S(2)}) %all-to-all-start) | async-done | bytes 524320 | tf_op jit(solution)/shard_map/all_to_all | solution.py:533
  49.6 2.3 %copy-done.1 = bf16[2,16,256,256]{3,2,1,0:T(8,128)(2,1)S(1)} copy-done((bf16[2,16,256,256]{3,2,1,0:T(8,128)(2,1)S(1)}, bf16[2,16,256,256]{3,2,1,0:T(8,128)(2,1)}, u32[]{:S(2)}) %copy-start.1) | copy-done | bytes 4194328
  53.5 18.1 %all_to_all.20.conv_ref = bf16[32,2,2,16,128]{4,3,2,1,0:T(8,128)(2,1)S(1)} all-to-all(bf16[32,2,2,16,128]{4,3,2,1,0:T(8,128)(2,1)S(1)} %conv.1), channel_id=1, replica_groups=mesh['context'=32,'tensor'=4] {'context'}, dimensions={0} | all-to-all | bytes 1048576 | tf_op jit(solution)/shard_map/all_to_all | solution.py:533
  74.4 4.2 %grad_weight.1 = bf16[4,512,1024]{2,1,0:T(8,128)(2,1)S(1)} custom-call(s32[4]{0:T(128)S(1)} %copy-done.11, bf16[512,512]{1,0:T(8,128)(2,1)S(1)} %pad_maximum_fusion.c0, bf16[512,512]{1,0:T(8,128)(2,1)} %collective-permute-done.2.c1, bf16[512,512]{1,0:T(8,128)(2,1)} %collective-permute-done.3.c2, bf16[512,512]{1,0:T(8,128)(2,1)S(1)} %copy-done.15, ...), custom_call_target="tpu_custom_call" | custom-call | flops 2200000000 | bytes 7800000 | tf_op jit(solution)/shard_map/grad_weight/pallas_call | solution.py:520
  82.2 2.2 %copy-done.12 = bf16[2048,1024]{1,0:T(8,128)(2,1)S(1)} copy-done((bf16[2048,1024]{1,0:T(8,128)(2,1)S(1)}, bf16[2048,1024]{1,0:T(8,128)(2,1)}, u32[]{:S(2)}) %copy-start.12) | copy-done | bytes 4194328
  84.4 4.6 %grad_gated.1 = (f32[256,1024]{1,0:T(8,128)S(1)}, bf16[256,1024]{1,0:T(8,128)(2,1)S(1)}) custom-call(s32[4]{0:T(128)S(1)} %copy-done.11, bf16[512,512]{1,0:T(8,128)(2,1)S(1)} %pad_maximum_fusion.c0, bf16[512,512]{1,0:T(8,128)(2,1)} %collective-permute-done.2.c1, bf16[512,512]{1,0:T(8,128)(2,1)} %collective-permute-done.3.c2, ...), custom_call_target="tpu_custom_call" | custom-call | flops 2200000000 | bytes 7800000 | tf_op jit(solution)/shard_map/grad_gated/pallas_call | solution.py:454
  92.6 3.9 %all-to-all-start.2 = ((bf16[32,2,2,16,128]{4,3,2,1,0:T(8,128)(2,1)}), bf16[32,2,2,16,128]{4,3,2,1,0:T(8,128)(2,1)S(1)}, u32[]{:S(2)}, u32[]{:S(2)}) async-start(bf16[32,2,2,16,128]{4,3,2,1,0:T(8,128)(2,1)} %copy-done.9), calls=%async_computation.2 | async-start | bytes 1048576 | tf_op jit(solution)/shard_map/all_to_all | solution.py:533
  96.5 2.2 %copy-done.13 = bf16[2048,1024]{1,0:T(8,128)(2,1)S(1)} copy-done((bf16[2048,1024]{1,0:T(8,128)(2,1)S(1)}, bf16[2048,1024]{1,0:T(8,128)(2,1)}, u32[]{:S(2)}) %copy-start.13) | copy-done | bytes 4194328
  100.8 4.2 %mixed.1 = (f32[512,512]{1,0:T(8,128)S(1)}, bf16[512,512]{1,0:T(8,128)(2,1)}, bf16[512,512]{1,0:T(8,128)(2,1)}, bf16[512,512]{1,0:T(8,128)(2,1)}) custom-call(s32[4]{0:T(128)S(1)} %copy-done.11, bf16[256,1024]{1,0:T(8,128)(2,1)S(1)} %bitcast.23, bf16[256,1024]{1,0:T(8,128)(2,1)S(1)} %copy-done.20, bf16[4,512,1024]{2,1,0:T(8,128)(2,1)S(1)} %bitcast.20), custom_call_target="tpu_custom_call" | custom-call | flops 2200000000 | bytes 7800000 | tf_op jit(solution)/shard_map/mixed/pallas_call | solution.py:478
  106.7 2.5 %collective-permute-start.8 = (bf16[512,512]{1,0:T(8,128)(2,1)}, bf16[512,512]{1,0:T(8,128)(2,1)}, u32[]{:S(2)}, u32[]{:S(2)}) collective-permute-start(bf16[512,512]{1,0:T(8,128)(2,1)} %get-tuple-element.63), channel_id=1, source_target_pairs={{0,2},{1,3},{2,0},{3,1},{4,6},{5,7},{6,4},{7,5},{8,10},{9,11},{10,... | collective-permute-start | bytes 1572872 | tf_op jit(solution)/shard_map/ppermute | solution.py:46
  111.2 2.2 %copy-done.2 = bf16[2,16,256,256]{3,2,1,0:T(8,128)(2,1)S(1)} copy-done((bf16[2,16,256,256]{3,2,1,0:T(8,128)(2,1)S(1)}, bf16[2,16,256,256]{3,2,1,0:T(8,128)(2,1)}, u32[]{:S(2)}) %copy-start.2) | copy-done | bytes 4194328
  113.5 2.5 %corr.1 = bf16[32,2,2,16,128]{4,3,2,1,0:T(8,128)(2,1)} custom-call(bf16[32,2,2,16,128]{4,3,2,1,0:T(8,128)(2,1)S(1)} %all-to-all-done.2.x_ref.g_ref, bf16[2,16,256,256]{3,2,1,0:T(8,128)(2,1)S(1)} %copy-done.2), custom_call_target="tpu_custom_call" | custom-call | flops 1100000000 | bytes 5300000 | tf_op jit(solution)/shard_map/corr/pallas_call | solution.py:202
  116.0 7.0 %all-to-all-start.3 = ((bf16[32,2,2,16,128]{4,3,2,1,0:T(8,128)(2,1)}), bf16[32,2,2,16,128]{4,3,2,1,0:T(8,128)(2,1)}, u32[]{:S(2)}, u32[]{:S(2)}) async-start(bf16[32,2,2,16,128]{4,3,2,1,0:T(8,128)(2,1)} %corr.1), calls=%async_computation.3 | async-start | bytes 1048576 | tf_op jit(solution)/shard_map/all_to_all | solution.py:533
  128.0 2.6 %grad_query.1 = bf16[2,128,1024]{2,1,0:T(8,128)(2,1)} custom-call(f32[3,7,64]{2,1,0:T(8,128)S(1)} %copy-done.10, bf16[1,2,16,1024]{3,2,1,0:T(8,128)(2,1)S(1)} %collective-permute-done.11.halo_ref, f32[2,128,1024]{2,1,0:T(8,128)S(1)} %get-tuple-element.68.gg_ref, bf16[2,128,1024]{2,1,0:T(8,128)(2,1)S(1)} %copy-done.8), custom_call_target="tpu_custom_call" | custom-call | flops 4000000 | bytes 2100000 | tf_op jit(solution)/shard_map/grad_query/pallas_call | solution.py:342
  132.8 2.2 %mixed_sum.1 = (bf16[256,512]{1,0:T(8,128)(2,1)S(1)}, bf16[256,512]{1,0:T(8,128)(2,1)}) custom-call(f32[512,512]{1,0:T(8,128)S(1)} %get-tuple-element.61.own, bf16[512,512]{1,0:T(8,128)(2,1)} %collective-permute-done.7.a_ref, bf16[512,512]{1,0:T(8,128)(2,1)} %collective-permute-done.8.b_ref, bf16[512,512]{1,0:T(8,128)(2,1)} %collective-permute-done.9.c_ref), custom_call_target="tpu_custom_call" | custom-call | bytes 3145728 | tf_op jit(solution)/shard_map/mixed_sum/pallas_call | solution.py:397
  135.0 6.1 %collective-permute-start.10 = (bf16[256,512]{1,0:T(8,128)(2,1)}, bf16[256,512]{1,0:T(8,128)(2,1)}, u32[]{:S(2)}, u32[]{:S(2)}) collective-permute-start(bf16[256,512]{1,0:T(8,128)(2,1)} %get-tuple-element.66), channel_id=1, source_target_pairs={{0,4},{4,0},{8,12},{12,8},{16,20},{20,16},{24,28},{28,24},{32,36},... | collective-permute-start | bytes 786440 | tf_op jit(solution)/shard_map/ppermute | solution.py:30
  141.1 3.2 %grad_long.1 = f32[2,1,4096]{2,1,0:T(1,128)S(1)} custom-call(bf16[32,2,2,16,128]{4,3,2,1,0:T(8,128)(2,1)S(1)} %all-to-all-done.x_ref.p_ref, bf16[32,2,2,16,128]{4,3,2,1,0:T(8,128)(2,1)S(1)} %all-to-all-done.2.x_ref.g_ref), custom_call_target="tpu_custom_call" | custom-call | flops 2200000000 | bytes 1200000 | tf_op jit(solution)/shard_map/grad_long/pallas_call | solution.py:252
  145.0 2.2 %unpack.1 = (bf16[2,128,1024]{2,1,0:T(8,128)(2,1)S(1)}, bf16[2,2,16,1024]{3,2,1,0:T(8,128)(2,1)S(1)}) custom-call(bf16[32,2,2,16,128]{4,3,2,1,0:T(8,128)(2,1)} %all-to-all-done.3.gp_ref, f32[2,128,1024]{2,1,0:T(8,128)S(1)} %copy-done.4, f32[2,128,1024]{2,1,0:T(8,128)S(1)} %copy-done.5), custom_call_target="tpu_custom_call" | custom-call | flops 500000 | bytes 1200000 | tf_op jit(solution)/shard_map/unpack/pallas_call | solution.py:315
  150.5 3.7 %grad_kv.1 = (bf16[2,128,1024]{2,1,0:T(8,128)(2,1)}, bf16[2,128,1024]{2,1,0:T(8,128)(2,1)}) custom-call(f32[3,7,64]{2,1,0:T(8,128)S(1)} %copy-done.10, bf16[2,2,16,1024]{3,2,1,0:T(8,128)(2,1)S(1)} %collective-permute-done.12.halo_ref, bf16[2,128,1024]{2,1,0:T(8,128)(2,1)S(1)} %get-tuple-element.75.gp_ref, f32[2,128,1024]{2,1,0:T(8,128)S(1)} %copy-done.4, ...), custom_call_target="tpu_custom_call" | custom-call | flops 8000000 | bytes 4000000 | tf_op jit(solution)/shard_map/grad_kv/pallas_call | solution.py:369
  154.2 8.6 %reduce-scatter.2.cloned.1.call-done = bf16[128,1024]{1,0:T(8,128)(2,1)} async-done(((bf16[2048,1024]{1,0:T(8,128)(2,1)}), bf16[128,1024]{1,0:T(8,128)(2,1)}) %reduce-scatter.2.cloned.1.call-update) | async-done | bytes 262160 | tf_op jit(solution)/shard_map/reduce_scatter | solution.py:582
  (83 shorter events, 40.1 us)
Async XLA Ops:
  7.2 29.9 %copy-start.22 = (f32[2,4096]{1,0:T(2,128)S(1)}, f32[2,4096]{1,0:T(2,128)}, u32[]{:S(2)}) copy-start(f32[2,4096]{1,0:T(2,128)} %param.11) | copy-start | bytes 98308
  7.2 75.0 %all-gather.2.cloned.1.call-start = ((), (), s32[]{:S(2)}) async-start(), calls=%async_computation.5 | async-start | bytes 4456448 | tf_op jit(solution)/shard_map/all_gather | solution.py:547
  10.6 2.4 %collective-permute-start = (bf16[256,512]{1,0:T(8,128)(2,1)}, bf16[256,512]{1,0:T(8,128)(2,1)S(1)}, u32[]{:S(2)}, u32[]{:S(2)}) collective-permute-start(bf16[256,512]{1,0:T(8,128)(2,1)} %get-tuple-element.44), channel_id=1, source_target_pairs={{0,4},{4,0},{8,12},{12,8},{16,20},{20,16},{24,28},{28,24},{32,36},... | collective-permute-start | bytes 786440 | tf_op jit(solution)/shard_map/ppermute | solution.py:30
  10.7 3.7 %collective-permute-start.1 = (bf16[3,2,16,1024]{3,2,1,0:T(8,128)(2,1)}, bf16[3,2,16,1024]{3,2,1,0:T(8,128)(2,1)S(1)}, u32[]{:S(2)}, u32[]{:S(2)}) collective-permute-start(bf16[3,2,16,1024]{3,2,1,0:T(8,128)(2,1)} %get-tuple-element.45), channel_id=1, source_target_pairs={{0,4},{4,8},{8,12},{12,16},{16,20},{20,24},{24,28},{28,32},{32,36}... | collective-permute-start | bytes 589832 | tf_op jit(solution)/shard_map/ppermute | solution.py:51
  14.3 34.5 %collective-permute-start.4 = (bf16[512,512]{1,0:T(8,128)(2,1)S(1)}, bf16[512,512]{1,0:T(8,128)(2,1)S(1)}, u32[]{:S(2)}, u32[]{:S(2)}) collective-permute-start(bf16[512,512]{1,0:T(8,128)(2,1)S(1)} %pad_maximum_fusion.c0), channel_id=1, source_target_pairs={{0,3},{1,0},{2,1},{3,2},{4,7},{5,4},{6,5},{7,6},{8,11},{9,8},{10,9... | collective-permute-start | bytes 1572872 | tf_op jit(solution)/shard_map/ppermute | solution.py:46
  17.4 32.2 %collective-permute-start.3 = (bf16[512,512]{1,0:T(8,128)(2,1)S(1)}, bf16[512,512]{1,0:T(8,128)(2,1)}, u32[]{:S(2)}, u32[]{:S(2)}) collective-permute-start(bf16[512,512]{1,0:T(8,128)(2,1)S(1)} %pad_maximum_fusion.c0), channel_id=1, source_target_pairs={{0,2},{1,3},{2,0},{3,1},{4,6},{5,7},{6,4},{7,5},{8,10},{9,11},{10,... | collective-permute-start | bytes 1572872 | tf_op jit(solution)/shard_map/ppermute | solution.py:46
  18.1 31.6 %collective-permute-start.2 = (bf16[512,512]{1,0:T(8,128)(2,1)S(1)}, bf16[512,512]{1,0:T(8,128)(2,1)}, u32[]{:S(2)}, u32[]{:S(2)}) collective-permute-start(bf16[512,512]{1,0:T(8,128)(2,1)S(1)} %pad_maximum_fusion.c0), channel_id=1, source_target_pairs={{0,1},{1,2},{2,3},{3,0},{4,5},{5,6},{6,7},{7,4},{8,9},{9,10},{10,1... | collective-permute-start | bytes 1572872 | tf_op jit(solution)/shard_map/ppermute | solution.py:46
  25.3 23.5 %all-to-all-start = ((bf16[32,2,2,16,128]{4,3,2,1,0:T(8,128)(2,1)}), bf16[32,2,2,16,128]{4,3,2,1,0:T(8,128)(2,1)S(1)}, u32[]{:S(2)}, u32[]{:S(2)}) async-start(bf16[32,2,2,16,128]{4,3,2,1,0:T(8,128)(2,1)} %get-tuple-element.47), calls=%async_computation | async-start | bytes 1048576 | tf_op jit(solution)/shard_map/all_to_all | solution.py:533
  37.0 125.7 %reduce-scatter.2.cloned.1.call-start = ((), (), s32[]{:S(2)}) async-start(), calls=%async_computation.6 | async-start | bytes 4456448 | tf_op jit(solution)/shard_map/reduce_scatter | solution.py:582
  37.1 34.5 %copy-start.6 = (f32[2,128,1024]{2,1,0:T(8,128)S(1)}, f32[2,128,1024]{2,1,0:T(8,128)}, u32[]{:S(2)}) copy-start(f32[2,128,1024]{2,1,0:T(8,128)} %get-tuple-element.54.qf_ref) | copy-start | bytes 3145732
  37.1 37.2 %copy-start.11 = (s32[4]{0:T(128)S(1)}, s32[4]{0:T(128)}, u32[]{:S(2)}) copy-start(s32[4]{0:T(128)} %pad_add_fusion.at) | copy-start | bytes 52
  51.9 22.5 %copy-start.15 = (bf16[512,512]{1,0:T(8,128)(2,1)S(1)}, bf16[512,512]{1,0:T(8,128)(2,1)}, u32[]{:S(2)}) copy-start(bf16[512,512]{1,0:T(8,128)(2,1)} %copy-done.14) | copy-start | bytes 1572868
  72.3 18.7 %copy-start.7 = (bf16[2,128,1024]{2,1,0:T(8,128)(2,1)}, bf16[2,128,1024]{2,1,0:T(8,128)(2,1)S(1)}, u32[]{:S(2)}) copy-start(bf16[2,128,1024]{2,1,0:T(8,128)(2,1)S(1)} %get-tuple-element.69.conv_ref) | copy-start | bytes 1572868
  72.4 2.0 %collective-permute-start.5 = (bf16[256,1024]{1,0:T(8,128)(2,1)S(1)}, bf16[256,1024]{1,0:T(8,128)(2,1)S(1)}, u32[]{:S(2)}, u32[]{:S(2)}) collective-permute-start(bf16[256,1024]{1,0:T(8,128)(2,1)S(1)} %bitcast.21), channel_id=1, source_target_pairs={{0,4},{4,0},{8,12},{12,8},{16,20},{20,16},{24,28},{28,24},{32,36},... | collective-permute-start | bytes 1572872 | tf_op jit(solution)/shard_map/ppermute | solution.py:30
  89.0 2.0 %collective-permute-start.6 = (bf16[256,1024]{1,0:T(8,128)(2,1)S(1)}, bf16[256,1024]{1,0:T(8,128)(2,1)S(1)}, u32[]{:S(2)}, u32[]{:S(2)}) collective-permute-start(bf16[256,1024]{1,0:T(8,128)(2,1)S(1)} %get-tuple-element.58), channel_id=1, source_target_pairs={{0,4},{4,0},{8,12},{12,8},{16,20},{20,16},{24,28},{28,24},{32,36},... | collective-permute-start | bytes 1572872 | tf_op jit(solution)/shard_map/ppermute | solution.py:30
  92.6 18.7 %all-to-all-start.2 = ((bf16[32,2,2,16,128]{4,3,2,1,0:T(8,128)(2,1)}), bf16[32,2,2,16,128]{4,3,2,1,0:T(8,128)(2,1)S(1)}, u32[]{:S(2)}, u32[]{:S(2)}) async-start(bf16[32,2,2,16,128]{4,3,2,1,0:T(8,128)(2,1)} %copy-done.9), calls=%async_computation.2 | async-start | bytes 1048576 | tf_op jit(solution)/shard_map/all_to_all | solution.py:533
  100.8 26.2 %copy-start.10 = (f32[3,7,64]{2,1,0:T(8,128)S(1)}, f32[3,7,64]{2,1,0:T(8,128)}, u32[]{:S(2)}) copy-start(f32[3,7,64]{2,1,0:T(8,128)} %taps_ref.5) | copy-start | bytes 16132
  105.0 25.7 %collective-permute-start.7 = (bf16[512,512]{1,0:T(8,128)(2,1)}, bf16[512,512]{1,0:T(8,128)(2,1)}, u32[]{:S(2)}, u32[]{:S(2)}) collective-permute-start(bf16[512,512]{1,0:T(8,128)(2,1)} %get-tuple-element.62), channel_id=1, source_target_pairs={{0,1},{1,2},{2,3},{3,0},{4,5},{5,6},{6,7},{7,4},{8,9},{9,10},{10,1... | collective-permute-start | bytes 1572872 | tf_op jit(solution)/shard_map/ppermute | solution.py:46
  106.7 26.1 %collective-permute-start.8 = (bf16[512,512]{1,0:T(8,128)(2,1)}, bf16[512,512]{1,0:T(8,128)(2,1)}, u32[]{:S(2)}, u32[]{:S(2)}) collective-permute-start(bf16[512,512]{1,0:T(8,128)(2,1)} %get-tuple-element.63), channel_id=1, source_target_pairs={{0,2},{1,3},{2,0},{3,1},{4,6},{5,7},{6,4},{7,5},{8,10},{9,11},{10,... | collective-permute-start | bytes 1572872 | tf_op jit(solution)/shard_map/ppermute | solution.py:46
  109.2 23.6 %collective-permute-start.9 = (bf16[512,512]{1,0:T(8,128)(2,1)}, bf16[512,512]{1,0:T(8,128)(2,1)}, u32[]{:S(2)}, u32[]{:S(2)}) collective-permute-start(bf16[512,512]{1,0:T(8,128)(2,1)} %get-tuple-element.64), channel_id=1, source_target_pairs={{0,3},{1,0},{2,1},{3,2},{4,7},{5,4},{6,5},{7,6},{8,11},{9,8},{10,9... | collective-permute-start | bytes 1572872 | tf_op jit(solution)/shard_map/ppermute | solution.py:46
  116.0 29.0 %all-to-all-start.3 = ((bf16[32,2,2,16,128]{4,3,2,1,0:T(8,128)(2,1)}), bf16[32,2,2,16,128]{4,3,2,1,0:T(8,128)(2,1)}, u32[]{:S(2)}, u32[]{:S(2)}) async-start(bf16[32,2,2,16,128]{4,3,2,1,0:T(8,128)(2,1)} %corr.1), calls=%async_computation.3 | async-start | bytes 1048576 | tf_op jit(solution)/shard_map/all_to_all | solution.py:533
  123.8 3.1 %collective-permute-start.11 = (bf16[1,2,16,1024]{3,2,1,0:T(8,128)(2,1)S(1)}, bf16[1,2,16,1024]{3,2,1,0:T(8,128)(2,1)S(1)}, u32[]{:S(2)}, u32[]{:S(2)}) collective-permute-start(bf16[1,2,16,1024]{3,2,1,0:T(8,128)(2,1)S(1)} %fusion), channel_id=1, source_target_pairs={{4,0},{8,4},{12,8},{16,12},{20,16},{24,20},{28,24},{32,28},{36,32}... | collective-permute-start | bytes 196616 | tf_op jit(solution)/shard_map/ppermute | solution.py:51
  135.0 13.6 %collective-permute-start.10 = (bf16[256,512]{1,0:T(8,128)(2,1)}, bf16[256,512]{1,0:T(8,128)(2,1)}, u32[]{:S(2)}, u32[]{:S(2)}) collective-permute-start(bf16[256,512]{1,0:T(8,128)(2,1)} %get-tuple-element.66), channel_id=1, source_target_pairs={{0,4},{4,0},{8,12},{12,8},{16,20},{20,16},{24,28},{28,24},{32,36},... | collective-permute-start | bytes 786440 | tf_op jit(solution)/shard_map/ppermute | solution.py:30
  147.2 3.2 %collective-permute-start.12 = (bf16[2,2,16,1024]{3,2,1,0:T(8,128)(2,1)S(1)}, bf16[2,2,16,1024]{3,2,1,0:T(8,128)(2,1)S(1)}, u32[]{:S(2)}, u32[]{:S(2)}) collective-permute-start(bf16[2,2,16,1024]{3,2,1,0:T(8,128)(2,1)S(1)} %get-tuple-element.74), channel_id=1, source_target_pairs={{4,0},{8,4},{12,8},{16,12},{20,16},{24,20},{28,24},{32,28},{36,32}... | collective-permute-start | bytes 393224 | tf_op jit(solution)/shard_map/ppermute | solution.py:51
  (17 other events, 53.8 us)
Sparse Core Ops, SparseCore 0:
  10.2 59.4 all-gather.1
  82.3 80.4 reduce-scatter.1

commit v4 on v3

--- a/solution.py
+++ b/solution.py
@@ -14,7 +14,7 @@
 NCTX = NZ * NX * NC
 BLK = 128
 CB = 256
-VMEM_BYTES = 32 * 1024 * 1024
+VMEM_BYTES = 48 * 1024 * 1024
 f32 = jnp.float32
 bf16 = jnp.bfloat16
 

time: 173 us -> 172 us (level)
  local copies, waits for them, and re-layouts: 19.9 us -> 13.6 us
  waiting for transfers between devices: 26.5 us -> 30.3 us
  Pallas kernels: 43.7 us -> 46.2 us
    unnamed x47 -> x41, local copies, waits for them, and re-layouts: 19.9 us -> 13.5 us
    reduce_scatter x1, waiting for transfers between devices: 8.58 us -> 11.8 us  [body(): lax.psum_scatter(sums, 'context', scatter_dimension=0, axis_index_groups=...]
  transfers between devices with their start and end apart: 18 -> 18, of which waited for: 9 -> 9; matrix products, arithmetic and copies ran while one was open for 2% -> 2% of each run, Pallas kernels for 25% -> 27%
where the time goes in v4:
time: 172 us; the launch traced here: 171 us
  Pallas kernels  46.2 us (27%)
  starting transfers between devices  43.9 us (26%)
  waiting for transfers between devices  30.3 us (18%)
  blocking collectives  18.1 us (11%)
  between operations  14.3 us (8%)
  local copies, waits for them, and re-layouts  13.6 us (8%)
  other arithmetic  4.23 us (2%)
    all_to_all x3, starting transfers between devices, exchange(): lax.all_to_all(value, 'context', split_axis=0, concat_axis=0, tiled=True)  21.9 us
    all_to_all x1, blocking collectives, exchange(): lax.all_to_all(value, 'context', split_axis=0, concat_axis=0, tiled=True)  18.1 us
    unnamed x41, local copies, waits for them, and re-layouts  13.5 us
    reduce_scatter x1, waiting for transfers between devices, body(): lax.psum_scatter(sums, 'context', scatter_dimension=0, axis_index_groups=...  11.8 us
    ppermute x6, starting transfers between devices, move_y(): return lax.ppermute(value, 'tensor', [(i, (i + d) % NY) for i in range(NY)])  10.3 us
    all_to_all x3, waiting for transfers between devices, exchange(): lax.all_to_all(value, 'context', split_axis=0, concat_axis=0, tiled=True)  9.99 us
    ppermute x4, starting transfers between devices, move_ctx(): return lax.ppermute(value, 'context', pairs)  6.43 us
    pallas_call x1, Pallas kernels, featurize(): pl.pallas_call(featurize_kernel, grid=(1024 // CB,), in_specs=[taps_spec,...  6.3 us
  transfers between devices with their start and end apart: 18, of which 9 were waited for; matrix products, arithmetic and copies ran while one was open for 2% of the time, Pallas kernels for 27%

profile of v4, /device:TPU:0, one launch (start us, length us, event | category | flops | bytes accessed | tf_op | source)
XLA Modules:
  0.0 170.8 jit_solution(17922557363169011844)
XLA Ops:
  8.5 2.1 %prep.1 = (bf16[3,2,16,1024]{3,2,1,0:T(8,128)(2,1)}, bf16[256,512]{1,0:T(8,128)(2,1)}, bf16[256,512]{1,0:T(8,128)(2,1)}) custom-call(s32[4]{0:T(128)} %pad_add_fusion.at, bf16[2,128,1024]{2,1,0:T(8,128)(2,1)} %q_ref.3, bf16[2,128,1024]{2,1,0:T(8,128)(2,1)} %k_ref.3, bf16[2,128,1024]{2,1,0:T(8,128)(2,1)} %v_ref.3, bf16[256,1024]{1,0:T(8,128)(2,1)} %bitcast.22), custom_call_target="tpu_custom_call" | custom-call | tf_op jit(solution)/shard_map/prep/pallas_call | solution.py:427
  10.7 2.4 %collective-permute-start.1 = (bf16[3,2,16,1024]{3,2,1,0:T(8,128)(2,1)}, bf16[3,2,16,1024]{3,2,1,0:T(8,128)(2,1)S(1)}, u32[]{:S(2)}, u32[]{:S(2)}) collective-permute-start(bf16[3,2,16,1024]{3,2,1,0:T(8,128)(2,1)} %get-tuple-element.45), channel_id=1, source_target_pairs={{0,4},{4,8},{8,12},{12,16},{16,20},{20,24},{24,28},{28,32},{32,36}... | collective-permute-start | bytes 589832 | tf_op jit(solution)/shard_map/ppermute | solution.py:51
  14.3 3.1 %collective-permute-start.4 = (bf16[512,512]{1,0:T(8,128)(2,1)S(1)}, bf16[512,512]{1,0:T(8,128)(2,1)S(1)}, u32[]{:S(2)}, u32[]{:S(2)}) collective-permute-start(bf16[512,512]{1,0:T(8,128)(2,1)S(1)} %pad_maximum_fusion.c0), channel_id=1, source_target_pairs={{0,3},{1,0},{2,1},{3,2},{4,7},{5,4},{6,5},{7,6},{8,11},{9,8},{10,9... | collective-permute-start | bytes 1572872 | tf_op jit(solution)/shard_map/ppermute | solution.py:46
  19.0 6.3 %featurize.1 = (bf16[32,2,2,16,128]{4,3,2,1,0:T(8,128)(2,1)}, f32[2,128,1024]{2,1,0:T(8,128)}, f32[2,128,1024]{2,1,0:T(8,128)}, f32[2,128,1024]{2,1,0:T(8,128)}) custom-call(f32[3,7,64]{2,1,0:T(8,128)} %taps_ref.5, bf16[3,2,16,1024]{3,2,1,0:T(8,128)(2,1)} %copy-done.18, bf16[2,128,1024]{2,1,0:T(8,128)(2,1)} %q_ref.3, bf16[2,128,1024]{2,1,0:T(8,128)(2,1)} %k_ref.3, ...), custom_call_target="tpu_custom_call" | custom-call | flops 12000000 | bytes 5500000 | tf_op jit(solution)/shard_map/featurize/pallas_call | solution.py:146
  25.3 11.7 %all-to-all-start = ((bf16[32,2,2,16,128]{4,3,2,1,0:T(8,128)(2,1)}), bf16[32,2,2,16,128]{4,3,2,1,0:T(8,128)(2,1)S(1)}, u32[]{:S(2)}, u32[]{:S(2)}) async-start(bf16[32,2,2,16,128]{4,3,2,1,0:T(8,128)(2,1)} %get-tuple-element.47), calls=%async_computation | async-start | bytes 1048576 | tf_op jit(solution)/shard_map/all_to_all | solution.py:533
  40.0 8.8 %all-to-all-done.x_ref.p_ref = bf16[32,2,2,16,128]{4,3,2,1,0:T(8,128)(2,1)S(1)} async-done(((bf16[32,2,2,16,128]{4,3,2,1,0:T(8,128)(2,1)}), bf16[32,2,2,16,128]{4,3,2,1,0:T(8,128)(2,1)S(1)}, u32[]{:S(2)}, u32[]{:S(2)}) %all-to-all-start) | async-done | bytes 524320 | tf_op jit(solution)/shard_map/all_to_all | solution.py:533
  49.6 2.3 %copy-done.1 = bf16[2,16,256,256]{3,2,1,0:T(8,128)(2,1)S(1)} copy-done((bf16[2,16,256,256]{3,2,1,0:T(8,128)(2,1)S(1)}, bf16[2,16,256,256]{3,2,1,0:T(8,128)(2,1)}, u32[]{:S(2)}) %copy-start.1) | copy-done | bytes 4194328
  53.5 18.1 %all_to_all.20.conv_ref = bf16[32,2,2,16,128]{4,3,2,1,0:T(8,128)(2,1)S(1)} all-to-all(bf16[32,2,2,16,128]{4,3,2,1,0:T(8,128)(2,1)S(1)} %conv.1), channel_id=1, replica_groups=mesh['context'=32,'tensor'=4] {'context'}, dimensions={0} | all-to-all | bytes 1048576 | tf_op jit(solution)/shard_map/all_to_all | solution.py:533
  74.4 5.3 %grad_weight.1 = bf16[4,512,1024]{2,1,0:T(8,128)(2,1)} custom-call(s32[4]{0:T(128)S(1)} %copy-done.10, bf16[512,512]{1,0:T(8,128)(2,1)S(1)} %pad_maximum_fusion.c0, bf16[512,512]{1,0:T(8,128)(2,1)} %collective-permute-done.2.c1, bf16[512,512]{1,0:T(8,128)(2,1)} %collective-permute-done.3.c2, bf16[512,512]{1,0:T(8,128)(2,1)S(1)} %copy-done.12, ...), custom_call_target="tpu_custom_call" | custom-call | flops 2200000000 | bytes 7800000 | tf_op jit(solution)/shard_map/grad_weight/pallas_call | solution.py:520
  81.3 5.1 %grad_gated.1 = (f32[256,1024]{1,0:T(8,128)S(1)}, bf16[256,1024]{1,0:T(8,128)(2,1)S(1)}) custom-call(s32[4]{0:T(128)S(1)} %copy-done.10, bf16[512,512]{1,0:T(8,128)(2,1)S(1)} %pad_maximum_fusion.c0, bf16[512,512]{1,0:T(8,128)(2,1)} %collective-permute-done.2.c1, bf16[512,512]{1,0:T(8,128)(2,1)} %collective-permute-done.3.c2, ...), custom_call_target="tpu_custom_call" | custom-call | flops 2200000000 | bytes 7800000 | tf_op jit(solution)/shard_map/grad_gated/pallas_call | solution.py:454
  90.0 3.9 %all-to-all-start.2 = ((bf16[32,2,2,16,128]{4,3,2,1,0:T(8,128)(2,1)}), bf16[32,2,2,16,128]{4,3,2,1,0:T(8,128)(2,1)S(1)}, u32[]{:S(2)}, u32[]{:S(2)}) async-start(bf16[32,2,2,16,128]{4,3,2,1,0:T(8,128)(2,1)} %copy-done.8), calls=%async_computation.2 | async-start | bytes 1048576 | tf_op jit(solution)/shard_map/all_to_all | solution.py:533
  96.0 5.2 %mixed.1 = (f32[512,512]{1,0:T(8,128)S(1)}, bf16[512,512]{1,0:T(8,128)(2,1)}, bf16[512,512]{1,0:T(8,128)(2,1)}, bf16[512,512]{1,0:T(8,128)(2,1)}) custom-call(s32[4]{0:T(128)S(1)} %copy-done.10, bf16[256,1024]{1,0:T(8,128)(2,1)S(1)} %bitcast.20, bf16[256,1024]{1,0:T(8,128)(2,1)S(1)} %copy-done.17, bf16[4,512,1024]{2,1,0:T(8,128)(2,1)} %bitcast.26), custom_call_target="tpu_custom_call" | custom-call | flops 2200000000 | bytes 7800000 | tf_op jit(solution)/shard_map/mixed/pallas_call | solution.py:478
  102.9 2.5 %collective-permute-start.8 = (bf16[512,512]{1,0:T(8,128)(2,1)}, bf16[512,512]{1,0:T(8,128)(2,1)}, u32[]{:S(2)}, u32[]{:S(2)}) collective-permute-start(bf16[512,512]{1,0:T(8,128)(2,1)} %get-tuple-element.63), channel_id=1, source_target_pairs={{0,2},{1,3},{2,0},{3,1},{4,6},{5,7},{6,4},{7,5},{8,10},{9,11},{10,... | collective-permute-start | bytes 1572872 | tf_op jit(solution)/shard_map/ppermute | solution.py:46
  107.9 2.2 %copy-done.2 = bf16[2,16,256,256]{3,2,1,0:T(8,128)(2,1)S(1)} copy-done((bf16[2,16,256,256]{3,2,1,0:T(8,128)(2,1)S(1)}, bf16[2,16,256,256]{3,2,1,0:T(8,128)(2,1)}, u32[]{:S(2)}) %copy-start.2) | copy-done | bytes 4194328
  110.2 2.5 %corr.1 = bf16[32,2,2,16,128]{4,3,2,1,0:T(8,128)(2,1)} custom-call(bf16[32,2,2,16,128]{4,3,2,1,0:T(8,128)(2,1)S(1)} %all-to-all-done.2.x_ref.g_ref, bf16[2,16,256,256]{3,2,1,0:T(8,128)(2,1)S(1)} %copy-done.2), custom_call_target="tpu_custom_call" | custom-call | flops 1100000000 | bytes 5300000 | tf_op jit(solution)/shard_map/corr/pallas_call | solution.py:202
  112.7 6.3 %all-to-all-start.3 = ((bf16[32,2,2,16,128]{4,3,2,1,0:T(8,128)(2,1)}), bf16[32,2,2,16,128]{4,3,2,1,0:T(8,128)(2,1)}, u32[]{:S(2)}, u32[]{:S(2)}) async-start(bf16[32,2,2,16,128]{4,3,2,1,0:T(8,128)(2,1)} %corr.1), calls=%async_computation.3 | async-start | bytes 1048576 | tf_op jit(solution)/shard_map/all_to_all | solution.py:533
  124.1 2.6 %grad_query.1 = bf16[2,128,1024]{2,1,0:T(8,128)(2,1)} custom-call(f32[3,7,64]{2,1,0:T(8,128)S(1)} %copy-done.9, bf16[1,2,16,1024]{3,2,1,0:T(8,128)(2,1)S(1)} %collective-permute-done.11.halo_ref, f32[2,128,1024]{2,1,0:T(8,128)S(1)} %get-tuple-element.68.gg_ref, bf16[2,128,1024]{2,1,0:T(8,128)(2,1)S(1)} %copy-done.7), custom_call_target="tpu_custom_call" | custom-call | flops 4000000 | bytes 2100000 | tf_op jit(solution)/shard_map/grad_query/pallas_call | solution.py:342
  126.8 2.1 %collective-permute-done.8.b_ref = bf16[512,512]{1,0:T(8,128)(2,1)} collective-permute-done((bf16[512,512]{1,0:T(8,128)(2,1)}, bf16[512,512]{1,0:T(8,128)(2,1)}, u32[]{:S(2)}, u32[]{:S(2)}) %collective-permute-start.8) | collective-permute-done | bytes 524320 | tf_op jit(solution)/shard_map/ppermute | solution.py:46
  128.9 2.2 %mixed_sum.1 = (bf16[256,512]{1,0:T(8,128)(2,1)S(1)}, bf16[256,512]{1,0:T(8,128)(2,1)}) custom-call(f32[512,512]{1,0:T(8,128)S(1)} %get-tuple-element.61.own, bf16[512,512]{1,0:T(8,128)(2,1)} %collective-permute-done.7.a_ref, bf16[512,512]{1,0:T(8,128)(2,1)} %collective-permute-done.8.b_ref, bf16[512,512]{1,0:T(8,128)(2,1)} %collective-permute-done.9.c_ref), custom_call_target="tpu_custom_call" | custom-call | bytes 3145728 | tf_op jit(solution)/shard_map/mixed_sum/pallas_call | solution.py:397
  131.1 6.1 %collective-permute-start.10 = (bf16[256,512]{1,0:T(8,128)(2,1)}, bf16[256,512]{1,0:T(8,128)(2,1)}, u32[]{:S(2)}, u32[]{:S(2)}) collective-permute-start(bf16[256,512]{1,0:T(8,128)(2,1)} %get-tuple-element.66), channel_id=1, source_target_pairs={{0,4},{4,0},{8,12},{12,8},{16,20},{20,16},{24,28},{28,24},{32,36},... | collective-permute-start | bytes 786440 | tf_op jit(solution)/shard_map/ppermute | solution.py:30
  137.3 3.2 %grad_long.1 = f32[2,1,4096]{2,1,0:T(1,128)S(1)} custom-call(bf16[32,2,2,16,128]{4,3,2,1,0:T(8,128)(2,1)S(1)} %all-to-all-done.x_ref.p_ref, bf16[32,2,2,16,128]{4,3,2,1,0:T(8,128)(2,1)S(1)} %all-to-all-done.2.x_ref.g_ref), custom_call_target="tpu_custom_call" | custom-call | flops 2200000000 | bytes 1200000 | tf_op jit(solution)/shard_map/grad_long/pallas_call | solution.py:252
  141.1 2.2 %unpack.1 = (bf16[2,128,1024]{2,1,0:T(8,128)(2,1)S(1)}, bf16[2,2,16,1024]{3,2,1,0:T(8,128)(2,1)S(1)}) custom-call(bf16[32,2,2,16,128]{4,3,2,1,0:T(8,128)(2,1)} %all-to-all-done.3.gp_ref, f32[2,128,1024]{2,1,0:T(8,128)S(1)} %copy-done.3, f32[2,128,1024]{2,1,0:T(8,128)S(1)} %copy-done.4), custom_call_target="tpu_custom_call" | custom-call | flops 500000 | bytes 1200000 | tf_op jit(solution)/shard_map/unpack/pallas_call | solution.py:315
  146.6 3.7 %grad_kv.1 = (bf16[2,128,1024]{2,1,0:T(8,128)(2,1)}, bf16[2,128,1024]{2,1,0:T(8,128)(2,1)}) custom-call(f32[3,7,64]{2,1,0:T(8,128)S(1)} %copy-done.9, bf16[2,2,16,1024]{3,2,1,0:T(8,128)(2,1)S(1)} %collective-permute-done.12.halo_ref, bf16[2,128,1024]{2,1,0:T(8,128)(2,1)S(1)} %get-tuple-element.75.gp_ref, f32[2,128,1024]{2,1,0:T(8,128)S(1)} %copy-done.3, ...), custom_call_target="tpu_custom_call" | custom-call | flops 8000000 | bytes 4000000 | tf_op jit(solution)/shard_map/grad_kv/pallas_call | solution.py:369
  150.3 11.8 %reduce-scatter.2.cloned.1.call-done = bf16[128,1024]{1,0:T(8,128)(2,1)} async-done(((bf16[2048,1024]{1,0:T(8,128)(2,1)}), bf16[128,1024]{1,0:T(8,128)(2,1)}) %reduce-scatter.2.cloned.1.call-update) | async-done | bytes 262160 | tf_op jit(solution)/shard_map/reduce_scatter | solution.py:582
  (77 shorter events, 34.4 us)
Async XLA Ops:
  7.2 29.9 %copy-start.19 = (f32[2,4096]{1,0:T(2,128)S(1)}, f32[2,4096]{1,0:T(2,128)}, u32[]{:S(2)}) copy-start(f32[2,4096]{1,0:T(2,128)} %param.11) | copy-start | bytes 98308
  7.2 74.1 %all-gather.2.cloned.1.call-start = ((), (), s32[]{:S(2)}) async-start(), calls=%async_computation.5 | async-start | bytes 4456448 | tf_op jit(solution)/shard_map/all_gather | solution.py:547
  10.6 2.4 %collective-permute-start = (bf16[256,512]{1,0:T(8,128)(2,1)}, bf16[256,512]{1,0:T(8,128)(2,1)S(1)}, u32[]{:S(2)}, u32[]{:S(2)}) collective-permute-start(bf16[256,512]{1,0:T(8,128)(2,1)} %get-tuple-element.44), channel_id=1, source_target_pairs={{0,4},{4,0},{8,12},{12,8},{16,20},{20,16},{24,28},{28,24},{32,36},... | collective-permute-start | bytes 786440 | tf_op jit(solution)/shard_map/ppermute | solution.py:30
  10.7 3.7 %collective-permute-start.1 = (bf16[3,2,16,1024]{3,2,1,0:T(8,128)(2,1)}, bf16[3,2,16,1024]{3,2,1,0:T(8,128)(2,1)S(1)}, u32[]{:S(2)}, u32[]{:S(2)}) collective-permute-start(bf16[3,2,16,1024]{3,2,1,0:T(8,128)(2,1)} %get-tuple-element.45), channel_id=1, source_target_pairs={{0,4},{4,8},{8,12},{12,16},{16,20},{20,24},{24,28},{28,32},{32,36}... | collective-permute-start | bytes 589832 | tf_op jit(solution)/shard_map/ppermute | solution.py:51
  14.3 34.5 %collective-permute-start.4 = (bf16[512,512]{1,0:T(8,128)(2,1)S(1)}, bf16[512,512]{1,0:T(8,128)(2,1)S(1)}, u32[]{:S(2)}, u32[]{:S(2)}) collective-permute-start(bf16[512,512]{1,0:T(8,128)(2,1)S(1)} %pad_maximum_fusion.c0), channel_id=1, source_target_pairs={{0,3},{1,0},{2,1},{3,2},{4,7},{5,4},{6,5},{7,6},{8,11},{9,8},{10,9... | collective-permute-start | bytes 1572872 | tf_op jit(solution)/shard_map/ppermute | solution.py:46
  17.4 32.2 %collective-permute-start.3 = (bf16[512,512]{1,0:T(8,128)(2,1)S(1)}, bf16[512,512]{1,0:T(8,128)(2,1)}, u32[]{:S(2)}, u32[]{:S(2)}) collective-permute-start(bf16[512,512]{1,0:T(8,128)(2,1)S(1)} %pad_maximum_fusion.c0), channel_id=1, source_target_pairs={{0,2},{1,3},{2,0},{3,1},{4,6},{5,7},{6,4},{7,5},{8,10},{9,11},{10,... | collective-permute-start | bytes 1572872 | tf_op jit(solution)/shard_map/ppermute | solution.py:46
  18.1 31.6 %collective-permute-start.2 = (bf16[512,512]{1,0:T(8,128)(2,1)S(1)}, bf16[512,512]{1,0:T(8,128)(2,1)}, u32[]{:S(2)}, u32[]{:S(2)}) collective-permute-start(bf16[512,512]{1,0:T(8,128)(2,1)S(1)} %pad_maximum_fusion.c0), channel_id=1, source_target_pairs={{0,1},{1,2},{2,3},{3,0},{4,5},{5,6},{6,7},{7,4},{8,9},{9,10},{10,1... | collective-permute-start | bytes 1572872 | tf_op jit(solution)/shard_map/ppermute | solution.py:46
  25.3 23.5 %all-to-all-start = ((bf16[32,2,2,16,128]{4,3,2,1,0:T(8,128)(2,1)}), bf16[32,2,2,16,128]{4,3,2,1,0:T(8,128)(2,1)S(1)}, u32[]{:S(2)}, u32[]{:S(2)}) async-start(bf16[32,2,2,16,128]{4,3,2,1,0:T(8,128)(2,1)} %get-tuple-element.47), calls=%async_computation | async-start | bytes 1048576 | tf_op jit(solution)/shard_map/all_to_all | solution.py:533
  37.0 125.1 %reduce-scatter.2.cloned.1.call-start = ((), (), s32[]{:S(2)}) async-start(), calls=%async_computation.6 | async-start | bytes 4456448 | tf_op jit(solution)/shard_map/reduce_scatter | solution.py:582
  37.1 34.5 %copy-start.5 = (f32[2,128,1024]{2,1,0:T(8,128)S(1)}, f32[2,128,1024]{2,1,0:T(8,128)}, u32[]{:S(2)}) copy-start(f32[2,128,1024]{2,1,0:T(8,128)} %get-tuple-element.54.qf_ref) | copy-start | bytes 3145732
  37.1 37.2 %copy-start.10 = (s32[4]{0:T(128)S(1)}, s32[4]{0:T(128)}, u32[]{:S(2)}) copy-start(s32[4]{0:T(128)} %pad_add_fusion.at) | copy-start | bytes 52
  51.9 22.5 %copy-start.12 = (bf16[512,512]{1,0:T(8,128)(2,1)S(1)}, bf16[512,512]{1,0:T(8,128)(2,1)}, u32[]{:S(2)}) copy-start(bf16[512,512]{1,0:T(8,128)(2,1)} %copy-done.11) | copy-start | bytes 1572868
  72.3 16.1 %copy-start.6 = (bf16[2,128,1024]{2,1,0:T(8,128)(2,1)}, bf16[2,128,1024]{2,1,0:T(8,128)(2,1)S(1)}, u32[]{:S(2)}) copy-start(bf16[2,128,1024]{2,1,0:T(8,128)(2,1)S(1)} %get-tuple-element.69.conv_ref) | copy-start | bytes 1572868
  72.4 2.0 %collective-permute-start.5 = (bf16[256,1024]{1,0:T(8,128)(2,1)S(1)}, bf16[256,1024]{1,0:T(8,128)(2,1)S(1)}, u32[]{:S(2)}, u32[]{:S(2)}) collective-permute-start(bf16[256,1024]{1,0:T(8,128)(2,1)S(1)} %bitcast.18), channel_id=1, source_target_pairs={{0,4},{4,0},{8,12},{12,8},{16,20},{20,16},{24,28},{28,24},{32,36},... | collective-permute-start | bytes 1572872 | tf_op jit(solution)/shard_map/ppermute | solution.py:30
  86.4 2.0 %collective-permute-start.6 = (bf16[256,1024]{1,0:T(8,128)(2,1)S(1)}, bf16[256,1024]{1,0:T(8,128)(2,1)S(1)}, u32[]{:S(2)}, u32[]{:S(2)}) collective-permute-start(bf16[256,1024]{1,0:T(8,128)(2,1)S(1)} %get-tuple-element.58), channel_id=1, source_target_pairs={{0,4},{4,0},{8,12},{12,8},{16,20},{20,16},{24,28},{28,24},{32,36},... | collective-permute-start | bytes 1572872 | tf_op jit(solution)/shard_map/ppermute | solution.py:30
  90.0 18.0 %all-to-all-start.2 = ((bf16[32,2,2,16,128]{4,3,2,1,0:T(8,128)(2,1)}), bf16[32,2,2,16,128]{4,3,2,1,0:T(8,128)(2,1)S(1)}, u32[]{:S(2)}, u32[]{:S(2)}) async-start(bf16[32,2,2,16,128]{4,3,2,1,0:T(8,128)(2,1)} %copy-done.8), calls=%async_computation.2 | async-start | bytes 1048576 | tf_op jit(solution)/shard_map/all_to_all | solution.py:533
  96.0 27.1 %copy-start.9 = (f32[3,7,64]{2,1,0:T(8,128)S(1)}, f32[3,7,64]{2,1,0:T(8,128)}, u32[]{:S(2)}) copy-start(f32[3,7,64]{2,1,0:T(8,128)} %taps_ref.5) | copy-start | bytes 16132
  101.1 25.6 %collective-permute-start.7 = (bf16[512,512]{1,0:T(8,128)(2,1)}, bf16[512,512]{1,0:T(8,128)(2,1)}, u32[]{:S(2)}, u32[]{:S(2)}) collective-permute-start(bf16[512,512]{1,0:T(8,128)(2,1)} %get-tuple-element.62), channel_id=1, source_target_pairs={{0,1},{1,2},{2,3},{3,0},{4,5},{5,6},{6,7},{7,4},{8,9},{9,10},{10,1... | collective-permute-start | bytes 1572872 | tf_op jit(solution)/shard_map/ppermute | solution.py:46
  102.9 26.0 %collective-permute-start.8 = (bf16[512,512]{1,0:T(8,128)(2,1)}, bf16[512,512]{1,0:T(8,128)(2,1)}, u32[]{:S(2)}, u32[]{:S(2)}) collective-permute-start(bf16[512,512]{1,0:T(8,128)(2,1)} %get-tuple-element.63), channel_id=1, source_target_pairs={{0,2},{1,3},{2,0},{3,1},{4,6},{5,7},{6,4},{7,5},{8,10},{9,11},{10,... | collective-permute-start | bytes 1572872 | tf_op jit(solution)/shard_map/ppermute | solution.py:46
  105.3 23.5 %collective-permute-start.9 = (bf16[512,512]{1,0:T(8,128)(2,1)}, bf16[512,512]{1,0:T(8,128)(2,1)}, u32[]{:S(2)}, u32[]{:S(2)}) collective-permute-start(bf16[512,512]{1,0:T(8,128)(2,1)} %get-tuple-element.64), channel_id=1, source_target_pairs={{0,3},{1,0},{2,1},{3,2},{4,7},{5,4},{6,5},{7,6},{8,11},{9,8},{10,9... | collective-permute-start | bytes 1572872 | tf_op jit(solution)/shard_map/ppermute | solution.py:46
  112.7 28.4 %all-to-all-start.3 = ((bf16[32,2,2,16,128]{4,3,2,1,0:T(8,128)(2,1)}), bf16[32,2,2,16,128]{4,3,2,1,0:T(8,128)(2,1)}, u32[]{:S(2)}, u32[]{:S(2)}) async-start(bf16[32,2,2,16,128]{4,3,2,1,0:T(8,128)(2,1)} %corr.1), calls=%async_computation.3 | async-start | bytes 1048576 | tf_op jit(solution)/shard_map/all_to_all | solution.py:533
  119.9 3.1 %collective-permute-start.11 = (bf16[1,2,16,1024]{3,2,1,0:T(8,128)(2,1)S(1)}, bf16[1,2,16,1024]{3,2,1,0:T(8,128)(2,1)S(1)}, u32[]{:S(2)}, u32[]{:S(2)}) collective-permute-start(bf16[1,2,16,1024]{3,2,1,0:T(8,128)(2,1)S(1)} %fusion), channel_id=1, source_target_pairs={{4,0},{8,4},{12,8},{16,12},{20,16},{24,20},{28,24},{32,28},{36,32}... | collective-permute-start | bytes 196616 | tf_op jit(solution)/shard_map/ppermute | solution.py:51
  131.1 13.6 %collective-permute-start.10 = (bf16[256,512]{1,0:T(8,128)(2,1)}, bf16[256,512]{1,0:T(8,128)(2,1)}, u32[]{:S(2)}, u32[]{:S(2)}) collective-permute-start(bf16[256,512]{1,0:T(8,128)(2,1)} %get-tuple-element.66), channel_id=1, source_target_pairs={{0,4},{4,0},{8,12},{12,8},{16,20},{20,16},{24,28},{28,24},{32,36},... | collective-permute-start | bytes 786440 | tf_op jit(solution)/shard_map/ppermute | solution.py:30
  143.4 3.2 %collective-permute-start.12 = (bf16[2,2,16,1024]{3,2,1,0:T(8,128)(2,1)S(1)}, bf16[2,2,16,1024]{3,2,1,0:T(8,128)(2,1)S(1)}, u32[]{:S(2)}, u32[]{:S(2)}) collective-permute-start(bf16[2,2,16,1024]{3,2,1,0:T(8,128)(2,1)S(1)} %get-tuple-element.74), channel_id=1, source_target_pairs={{4,0},{8,4},{12,8},{16,12},{20,16},{24,20},{28,24},{32,28},{36,32}... | collective-permute-start | bytes 393224 | tf_op jit(solution)/shard_map/ppermute | solution.py:51
  (14 other events, 46.5 us)
Sparse Core Ops, SparseCore 0:
  10.2 59.4 all-gather.1
  81.4 80.7 reduce-scatter.1

commit v5 on v4

--- a/solution.py
+++ b/solution.py
@@ -113,19 +113,27 @@
     return value.astype(f32).reshape(CB, BLK).T
 
 
-def featurize_kernel(taps_ref, halo_ref, q_ref, k_ref, v_ref, prod_ref, qf_ref, kf_ref, vf_ref):
-    spread = [spread_taps(taps_ref, i, pl.program_id(0)) for i in range(3)]
+def forward_taps(signal, halo, taps):
+    ext = jnp.concatenate([halo.astype(f32), signal.astype(f32)], axis=0)
+    total = taps[:1] * ext[HALO:]
+    for j in range(1, TAPS):
+        total = total + taps[j : j + 1] * ext[HALO - j : HALO - j + BLK]
+    return total
+
+
+def product_kernel(taps_ref, halo_ref, k_ref, v_ref, prod_ref, kf_ref, vf_ref):
+    key_taps = spread_taps(taps_ref, 1, pl.program_id(0))
+    value_taps = spread_taps(taps_ref, 2, pl.program_id(0))
     for b in range(2):
-        feats = []
-        for i, (src, dst) in enumerate(((q_ref, qf_ref), (k_ref, kf_ref), (v_ref, vf_ref))):
-            ext = jnp.concatenate([halo_ref[i, b].astype(f32), src[b].astype(f32)], axis=0)
-            taps = spread[i]
-            total = taps[:1] * ext[HALO:]
-            for j in range(1, TAPS):
-                total = total + taps[j : j + 1] * ext[HALO - j : HALO - j + BLK]
-            dst[b] = total
-            feats.append(total)
-        prod_ref[:, :, b] = to_channels(feats[1] * feats[2])
+        kf_ref[b] = key = forward_taps(k_ref[b], halo_ref[1, b], key_taps)
+        vf_ref[b] = value = forward_taps(v_ref[b], halo_ref[2, b], value_taps)
+        prod_ref[:, :, b] = to_channels(key * value)
+
+
+def query_kernel(taps_ref, halo_ref, q_ref, qf_ref):
+    taps = spread_taps(taps_ref, 0, pl.program_id(0))
+    for b in range(2):
+        qf_ref[b] = forward_taps(q_ref[b], halo_ref[0, b], taps)
 
 
 chan_spec = pl.BlockSpec((CB // (2 * GROUP), 2, 2, GROUP, BLK), lambda c: (c, 0, 0, 0, 0))
@@ -142,17 +150,30 @@
     return jax.ShapeDtypeStruct((2, BLK, 1024), kind)
 
 
-def featurize(taps, halo, q, k, v):
-    return pl.pallas_call(
-        featurize_kernel,
+def featurize_product(taps, halo, k, v):
+    return pl.pallas_call(
+        product_kernel,
         grid=(1024 // CB,),
-        in_specs=[taps_spec, halo_spec, pos_spec, pos_spec, pos_spec],
-        out_specs=[chan_spec, pos_spec, pos_spec, pos_spec],
-        out_shape=[chan_shape(), pos_shape(f32), pos_shape(f32), pos_shape(f32)],
+        in_specs=[taps_spec, halo_spec, pos_spec, pos_spec],
+        out_specs=[chan_spec, pos_spec, pos_spec],
+        out_shape=[chan_shape(), pos_shape(f32), pos_shape(f32)],
         compiler_params=pltpu.CompilerParams(vmem_limit_bytes=62 * 1024 * 1024),
-        cost_estimate=pl.CostEstimate(flops=12_000_000, bytes_accessed=5_500_000, transcendentals=0),
-        name="featurize",
-    )(taps, halo, q, k, v)
+        cost_estimate=pl.CostEstimate(flops=8_000_000, bytes_accessed=3_800_000, transcendentals=0),
+        name="featurize_product",
+    )(taps, halo, k, v)
+
+
+def featurize_query(taps, halo, q):
+    return pl.pallas_call(
+        query_kernel,
+        grid=(1024 // CB,),
+        in_specs=[taps_spec, halo_spec, pos_spec],
+        out_specs=pos_spec,
+        out_shape=pos_shape(f32),
+        compiler_params=params("arbitrary"),
+        cost_estimate=pl.CostEstimate(flops=4_000_000, bytes_accessed=1_700_000, transcendentals=0),
+        name="featurize_query",
+    )(taps, halo, q)
 
 
 def fold(src_ref, dst_ref):
@@ -523,7 +544,7 @@
         in_specs=[smem] + [fixed] * 4 + [pl.BlockSpec((256, 512), lambda n: (0, n))] * 2,
         out_specs=pl.BlockSpec((4, 512, 512), lambda n: (0, 0, n)),
         out_shape=shape((4, 512, 1024)),
-        compiler_params=params("arbitrary"),
+        compiler_params=pltpu.CompilerParams(vmem_limit_bytes=62 * 1024 * 1024),
         cost_estimate=pl.CostEstimate(flops=2_200_000_000, bytes_accessed=7_800_000, transcendentals=0),
         name="grad_weight",
     )(at, *columns, own, other)
@@ -561,10 +582,13 @@
     columns = around(columns, move_y)
 
     tiles = toeplitz_tiles(long_filter)
-    prod, qf, kf, vf = featurize(taps, before, query_in, key_in, value_in)
+    prod, kf, vf = featurize_product(taps, before, key_in, value_in)
     prod = exchange(prod)
     prod, *columns = lax.optimization_barrier((prod, *columns))
-    conv = exchange(convolve(conv_kernel, "conv", prod, tiles))
+    conv = convolve(conv_kernel, "conv", prod, tiles)
+    conv, before = lax.optimization_barrier((conv, before))
+    conv = exchange(conv)
+    qf = featurize_query(taps, before, query_in)
     gated, conv = gate(conv, qf)
     gated_own = gated.reshape(positions, channels)
     gated_other = swap_core(gated_own)

time: 172 us -> 172 us (level)
  blocking collectives: 18.1 us -> 0 us
  waiting for transfers between devices: 30.3 us -> 40.9 us
  starting transfers between devices: 43.9 us -> 48 us
  Pallas kernels: 46.2 us -> 49.1 us
  local copies, waits for them, and re-layouts: 13.6 us -> 15.4 us
    all_to_all x1 -> x0, blocking collectives: 18.1 us -> none  [exchange(): lax.all_to_all(value, 'context', split_axis=0, concat_axis=0, tiled=True)]
    all_to_all x3 -> x4, waiting for transfers between devices: 9.99 us -> 21.4 us  [exchange(): lax.all_to_all(value, 'context', split_axis=0, concat_axis=0, tiled=True)]
    all_to_all x3 -> x4, starting transfers between devices: 21.9 us -> 27.7 us  [exchange(): lax.all_to_all(value, 'context', split_axis=0, concat_axis=0, tiled=True)]
    reduce_scatter x1, waiting for transfers between devices: 11.8 us -> 8.69 us  [body(): lax.psum_scatter(sums, 'context', scatter_dimension=0, axis_index_groups=...]
    unnamed x41 -> x51, local copies, waits for them, and re-layouts: 13.5 us -> 15.3 us
    ppermute x6, waiting for transfers between devices: 2.13 us -> 3.88 us  [move_y(): return lax.ppermute(value, 'tensor', [(i, (i + d) % NY) for i in range(NY)])]
    pallas_call x1 -> x2, Pallas kernels: 6.3 us -> 7.18 us  [the longest x1 5.43 us: featurize_product(): pl.pallas_call(product_kernel, grid=(1024 // CB,), in_specs=[taps_spec, h...]
  transfers between devices with their start and end apart: 18 -> 19, of which waited for: 9 -> 10; matrix products, arithmetic and copies ran while one was open for 2% -> 1% of each run, Pallas kernels for 27% -> 29%
where the time goes in v5:
time: 172 us; the launch traced here: 171 us
  Pallas kernels  49.1 us (29%)
  starting transfers between devices  48 us (28%)
  waiting for transfers between devices  40.9 us (24%)
  local copies, waits for them, and re-layouts  15.4 us (9%)
  between operations  14.4 us (8%)
  other arithmetic  3.42 us (2%)
    all_to_all x4, starting transfers between devices, exchange(): lax.all_to_all(value, 'context', split_axis=0, concat_axis=0, tiled=True)  27.7 us
    all_to_all x4, waiting for transfers between devices, exchange(): lax.all_to_all(value, 'context', split_axis=0, concat_axis=0, tiled=True)  21.4 us
    unnamed x51, local copies, waits for them, and re-layouts  15.3 us
    ppermute x6, starting transfers between devices, move_y(): return lax.ppermute(value, 'tensor', [(i, (i + d) % NY) for i in range(NY)])  10.3 us
    reduce_scatter x1, waiting for transfers between devices, body(): lax.psum_scatter(sums, 'context', scatter_dimension=0, axis_index_groups=...  8.69 us
    pallas_call x1, Pallas kernels, weight_grad_call(): pl.pallas_call(weight_grad_kernel, grid=(2,), in_specs=[smem] + [fixed] *...  5.69 us
    pallas_call x1, Pallas kernels, featurize_product(): pl.pallas_call(product_kernel, grid=(1024 // CB,), in_specs=[taps_spec, h...  5.43 us
    pallas_call x1, Pallas kernels, mixed_call(): pl.pallas_call(mixed_kernel, grid=(2,), in_specs=[smem, fixed, fixed, pl....  5.42 us
  transfers between devices with their start and end apart: 19, of which 10 were waited for; matrix products, arithmetic and copies ran while one was open for 1% of the time, Pallas kernels for 29%

profile of v5, /device:TPU:0, one launch (start us, length us, event | category | flops | bytes accessed | tf_op | source)
XLA Modules:
  0.0 171.3 jit_solution(6469464304866338057)
XLA Ops:
  10.7 2.4 %collective-permute-start.1 = (bf16[3,2,16,1024]{3,2,1,0:T(8,128)(2,1)}, bf16[3,2,16,1024]{3,2,1,0:T(8,128)(2,1)S(1)}, u32[]{:S(2)}, u32[]{:S(2)}) collective-permute-start(bf16[3,2,16,1024]{3,2,1,0:T(8,128)(2,1)} %get-tuple-element.46), channel_id=1, source_target_pairs={{0,4},{4,8},{8,12},{12,16},{16,20},{20,24},{24,28},{28,32},{32,36}... | collective-permute-start | bytes 589832 | tf_op jit(solution)/shard_map/ppermute | solution.py:51
  14.4 3.1 %collective-permute-start.4 = (bf16[512,512]{1,0:T(8,128)(2,1)S(1)}, bf16[512,512]{1,0:T(8,128)(2,1)S(1)}, u32[]{:S(2)}, u32[]{:S(2)}) collective-permute-start(bf16[512,512]{1,0:T(8,128)(2,1)S(1)} %pad_maximum_fusion.c0), channel_id=1, source_target_pairs={{0,3},{1,0},{2,1},{3,2},{4,7},{5,4},{6,5},{7,6},{8,11},{9,8},{10,9... | collective-permute-start | bytes 1572872 | tf_op jit(solution)/shard_map/ppermute | solution.py:46
  19.1 5.4 %featurize_product.1 = (bf16[32,2,2,16,128]{4,3,2,1,0:T(8,128)(2,1)}, f32[2,128,1024]{2,1,0:T(8,128)}, f32[2,128,1024]{2,1,0:T(8,128)}) custom-call(f32[3,7,64]{2,1,0:T(8,128)} %taps_ref.7, bf16[3,2,16,1024]{3,2,1,0:T(8,128)(2,1)} %copy-done.12, bf16[2,128,1024]{2,1,0:T(8,128)(2,1)} %k_ref.3, bf16[2,128,1024]{2,1,0:T(8,128)(2,1)} %v_ref.3), custom_call_target="tpu_custom_call" | custom-call | flops 8000000 | bytes 3800000 | tf_op jit(solution)/shard_map/featurize_product/pallas_call | solution.py:154
  24.5 11.7 %all-to-all-start = ((bf16[32,2,2,16,128]{4,3,2,1,0:T(8,128)(2,1)}), bf16[32,2,2,16,128]{4,3,2,1,0:T(8,128)(2,1)S(1)}, u32[]{:S(2)}, u32[]{:S(2)}) async-start(bf16[32,2,2,16,128]{4,3,2,1,0:T(8,128)(2,1)} %get-tuple-element.48), calls=%async_computation | async-start | bytes 1048576 | tf_op jit(solution)/shard_map/all_to_all | solution.py:554
  39.1 8.9 %all-to-all-done.x_ref.p_ref = bf16[32,2,2,16,128]{4,3,2,1,0:T(8,128)(2,1)S(1)} async-done(((bf16[32,2,2,16,128]{4,3,2,1,0:T(8,128)(2,1)}), bf16[32,2,2,16,128]{4,3,2,1,0:T(8,128)(2,1)S(1)}, u32[]{:S(2)}, u32[]{:S(2)}) %all-to-all-start) | async-done | bytes 524320 | tf_op jit(solution)/shard_map/all_to_all | solution.py:554
  48.0 2.4 %copy-done.1 = bf16[2,16,256,256]{3,2,1,0:T(8,128)(2,1)S(1)} copy-done((bf16[2,16,256,256]{3,2,1,0:T(8,128)(2,1)S(1)}, bf16[2,16,256,256]{3,2,1,0:T(8,128)(2,1)}, u32[]{:S(2)}) %copy-start.1) | copy-done | bytes 4194328
  50.3 2.3 %conv.1 = bf16[32,2,2,16,128]{4,3,2,1,0:T(8,128)(2,1)} custom-call(bf16[32,2,2,16,128]{4,3,2,1,0:T(8,128)(2,1)S(1)} %all-to-all-done.x_ref.p_ref, bf16[2,16,256,256]{3,2,1,0:T(8,128)(2,1)S(1)} %copy-done.1), custom_call_target="tpu_custom_call" | custom-call | flops 1100000000 | bytes 5300000 | tf_op jit(solution)/shard_map/conv/pallas_call | solution.py:223
  52.7 6.4 %all-to-all-start.1 = ((bf16[32,2,2,16,128]{4,3,2,1,0:T(8,128)(2,1)}), bf16[32,2,2,16,128]{4,3,2,1,0:T(8,128)(2,1)S(1)}, u32[]{:S(2)}, u32[]{:S(2)}) async-start(bf16[32,2,2,16,128]{4,3,2,1,0:T(8,128)(2,1)} %conv.1), calls=%async_computation.1 | async-start | bytes 1048576 | tf_op jit(solution)/shard_map/all_to_all | solution.py:554
  60.9 10.8 %all-to-all-done.1.conv_ref = bf16[32,2,2,16,128]{4,3,2,1,0:T(8,128)(2,1)S(1)} async-done(((bf16[32,2,2,16,128]{4,3,2,1,0:T(8,128)(2,1)}), bf16[32,2,2,16,128]{4,3,2,1,0:T(8,128)(2,1)S(1)}, u32[]{:S(2)}, u32[]{:S(2)}) %all-to-all-start.1) | async-done | bytes 524320 | tf_op jit(solution)/shard_map/all_to_all | solution.py:554
  76.0 5.7 %grad_weight.1 = bf16[4,512,1024]{2,1,0:T(8,128)(2,1)} custom-call(s32[4]{0:T(128)} %pad_add_fusion.at, bf16[512,512]{1,0:T(8,128)(2,1)} %copy-done.16, bf16[512,512]{1,0:T(8,128)(2,1)} %collective-permute-done.2.c1, bf16[512,512]{1,0:T(8,128)(2,1)} %collective-permute-done.3.c2, bf16[512,512]{1,0:T(8,128)(2,1)} %copy-done.20, bf16[256,1024]{1,0:T(8,128)(2,1)} %bitcast.19, ...), custom_call_target="tpu_custom_call" | custom-call | flops 2200000000 | bytes 7800000 | tf_op jit(solution)/shard_map/grad_weight/pallas_call | solution.py:541
  82.9 5.1 %grad_gated.1 = (f32[256,1024]{1,0:T(8,128)S(1)}, bf16[256,1024]{1,0:T(8,128)(2,1)S(1)}) custom-call(s32[4]{0:T(128)S(1)} %copy-done.19, bf16[512,512]{1,0:T(8,128)(2,1)S(1)} %copy-done.17, bf16[512,512]{1,0:T(8,128)(2,1)} %collective-permute-done.2.c1, bf16[512,512]{1,0:T(8,128)(2,1)} %collective-permute-done.3.c2, bf16[512,512]{1,0:T(8,128)(2,1)S(1)} %copy-done.21, ...), custom_call_target="tpu_custom_call" | custom-call | flops 2200000000 | bytes 7800000 | tf_op jit(solution)/shard_map/grad_gated/pallas_call | solution.py:475
  92.9 3.9 %all-to-all-start.2 = ((bf16[32,2,2,16,128]{4,3,2,1,0:T(8,128)(2,1)}), bf16[32,2,2,16,128]{4,3,2,1,0:T(8,128)(2,1)S(1)}, u32[]{:S(2)}, u32[]{:S(2)}) async-start(bf16[32,2,2,16,128]{4,3,2,1,0:T(8,128)(2,1)} %get-tuple-element.69), calls=%async_computation.2 | async-start | bytes 1048576 | tf_op jit(solution)/shard_map/all_to_all | solution.py:554
  97.8 5.4 %mixed.1 = (f32[512,512]{1,0:T(8,128)S(1)}, bf16[512,512]{1,0:T(8,128)(2,1)}, bf16[512,512]{1,0:T(8,128)(2,1)}, bf16[512,512]{1,0:T(8,128)(2,1)}) custom-call(s32[4]{0:T(128)S(1)} %copy-done.19, bf16[256,1024]{1,0:T(8,128)(2,1)S(1)} %bitcast.20, bf16[256,1024]{1,0:T(8,128)(2,1)} %collective-permute-done.5.other_g, bf16[4,512,1024]{2,1,0:T(8,128)(2,1)} %bitcast.26), custom_call_target="tpu_custom_call" | custom-call | flops 2200000000 | bytes 7800000 | tf_op jit(solution)/shard_map/mixed/pallas_call | solution.py:499
  105.7 2.7 %collective-permute-start.8 = (bf16[512,512]{1,0:T(8,128)(2,1)}, bf16[512,512]{1,0:T(8,128)(2,1)}, u32[]{:S(2)}, u32[]{:S(2)}) collective-permute-start(bf16[512,512]{1,0:T(8,128)(2,1)} %get-tuple-element.65), channel_id=1, source_target_pairs={{0,2},{1,3},{2,0},{3,1},{4,6},{5,7},{6,4},{7,5},{8,10},{9,11},{10,... | collective-permute-start | bytes 1572872 | tf_op jit(solution)/shard_map/ppermute | solution.py:46
  111.7 2.2 %copy-done.2 = bf16[2,16,256,256]{3,2,1,0:T(8,128)(2,1)S(1)} copy-done((bf16[2,16,256,256]{3,2,1,0:T(8,128)(2,1)S(1)}, bf16[2,16,256,256]{3,2,1,0:T(8,128)(2,1)}, u32[]{:S(2)}) %copy-start.2) | copy-done | bytes 4194328
  113.9 2.6 %corr.1 = bf16[32,2,2,16,128]{4,3,2,1,0:T(8,128)(2,1)} custom-call(bf16[32,2,2,16,128]{4,3,2,1,0:T(8,128)(2,1)S(1)} %all-to-all-done.2.x_ref.g_ref, bf16[2,16,256,256]{3,2,1,0:T(8,128)(2,1)S(1)} %copy-done.2), custom_call_target="tpu_custom_call" | custom-call | flops 1100000000 | bytes 5300000 | tf_op jit(solution)/shard_map/corr/pallas_call | solution.py:223
  116.5 5.8 %all-to-all-start.3 = ((bf16[32,2,2,16,128]{4,3,2,1,0:T(8,128)(2,1)}), bf16[32,2,2,16,128]{4,3,2,1,0:T(8,128)(2,1)}, u32[]{:S(2)}, u32[]{:S(2)}) async-start(bf16[32,2,2,16,128]{4,3,2,1,0:T(8,128)(2,1)} %corr.1), calls=%async_computation.3 | async-start | bytes 1048576 | tf_op jit(solution)/shard_map/all_to_all | solution.py:554
  125.5 2.6 %grad_query.1 = bf16[2,128,1024]{2,1,0:T(8,128)(2,1)} custom-call(f32[3,7,64]{2,1,0:T(8,128)S(1)} %copy-done.18, bf16[1,2,16,1024]{3,2,1,0:T(8,128)(2,1)S(1)} %collective-permute-done.11.halo_ref, f32[2,128,1024]{2,1,0:T(8,128)S(1)} %copy-done.9, bf16[2,128,1024]{2,1,0:T(8,128)(2,1)S(1)} %copy-done.15), custom_call_target="tpu_custom_call" | custom-call | flops 4000000 | bytes 2100000 | tf_op jit(solution)/shard_map/grad_query/pallas_call | solution.py:363
  128.1 3.9 %collective-permute-done.8.b_ref = bf16[512,512]{1,0:T(8,128)(2,1)} collective-permute-done((bf16[512,512]{1,0:T(8,128)(2,1)}, bf16[512,512]{1,0:T(8,128)(2,1)}, u32[]{:S(2)}, u32[]{:S(2)}) %collective-permute-start.8) | collective-permute-done | bytes 524320 | tf_op jit(solution)/shard_map/ppermute | solution.py:46
  135.4 4.5 %collective-permute-start.10 = (bf16[256,512]{1,0:T(8,128)(2,1)}, bf16[256,512]{1,0:T(8,128)(2,1)S(1)}, u32[]{:S(2)}, u32[]{:S(2)}) collective-permute-start(bf16[256,512]{1,0:T(8,128)(2,1)} %get-tuple-element.68), channel_id=1, source_target_pairs={{0,4},{4,0},{8,12},{12,8},{16,20},{20,16},{24,28},{28,24},{32,36},... | collective-permute-start | bytes 786440 | tf_op jit(solution)/shard_map/ppermute | solution.py:30
  141.0 3.2 %grad_long.1 = f32[2,1,4096]{2,1,0:T(1,128)S(1)} custom-call(bf16[32,2,2,16,128]{4,3,2,1,0:T(8,128)(2,1)S(1)} %all-to-all-done.x_ref.p_ref, bf16[32,2,2,16,128]{4,3,2,1,0:T(8,128)(2,1)S(1)} %copy-done.7), custom_call_target="tpu_custom_call" | custom-call | flops 2200000000 | bytes 1200000 | tf_op jit(solution)/shard_map/grad_long/pallas_call | solution.py:273
  144.8 2.2 %unpack.1 = (bf16[2,128,1024]{2,1,0:T(8,128)(2,1)S(1)}, bf16[2,2,16,1024]{3,2,1,0:T(8,128)(2,1)S(1)}) custom-call(bf16[32,2,2,16,128]{4,3,2,1,0:T(8,128)(2,1)} %all-to-all-done.3.gp_ref, f32[2,128,1024]{2,1,0:T(8,128)S(1)} %copy-done.3, f32[2,128,1024]{2,1,0:T(8,128)S(1)} %copy-done.4), custom_call_target="tpu_custom_call" | custom-call | flops 500000 | bytes 1200000 | tf_op jit(solution)/shard_map/unpack/pallas_call | solution.py:336
  150.3 3.7 %grad_kv.1 = (bf16[2,128,1024]{2,1,0:T(8,128)(2,1)}, bf16[2,128,1024]{2,1,0:T(8,128)(2,1)}) custom-call(f32[3,7,64]{2,1,0:T(8,128)S(1)} %copy-done.18, bf16[2,2,16,1024]{3,2,1,0:T(8,128)(2,1)S(1)} %collective-permute-done.12.halo_ref, bf16[2,128,1024]{2,1,0:T(8,128)(2,1)S(1)} %get-tuple-element.77.gp_ref, f32[2,128,1024]{2,1,0:T(8,128)S(1)} %copy-done.3, ...), custom_call_target="tpu_custom_call" | custom-call | flops 8000000 | bytes 4000000 | tf_op jit(solution)/shard_map/grad_kv/pallas_call | solution.py:390
  154.0 8.7 %reduce-scatter.2.cloned.1.call-done = bf16[128,1024]{1,0:T(8,128)(2,1)} async-done(((bf16[2048,1024]{1,0:T(8,128)(2,1)}), bf16[128,1024]{1,0:T(8,128)(2,1)}) %reduce-scatter.2.cloned.1.call-update) | async-done | bytes 262160 | tf_op jit(solution)/shard_map/reduce_scatter | solution.py:606
  (89 shorter events, 41.4 us)
Async XLA Ops:
  7.2 29.0 %copy-start.24 = (f32[2,4096]{1,0:T(2,128)S(1)}, f32[2,4096]{1,0:T(2,128)}, u32[]{:S(2)}) copy-start(f32[2,4096]{1,0:T(2,128)} %param.11) | copy-start | bytes 98308
  7.2 74.5 %all-gather.2.cloned.1.call-start = ((), (), s32[]{:S(2)}) async-start(), calls=%async_computation.5 | async-start | bytes 4456448 | tf_op jit(solution)/shard_map/all_gather | solution.py:568
  10.7 2.4 %collective-permute-start = (bf16[256,512]{1,0:T(8,128)(2,1)}, bf16[256,512]{1,0:T(8,128)(2,1)S(1)}, u32[]{:S(2)}, u32[]{:S(2)}) collective-permute-start(bf16[256,512]{1,0:T(8,128)(2,1)} %get-tuple-element.45), channel_id=1, source_target_pairs={{0,4},{4,0},{8,12},{12,8},{16,20},{20,16},{24,28},{28,24},{32,36},... | collective-permute-start | bytes 786440 | tf_op jit(solution)/shard_map/ppermute | solution.py:30
  10.7 3.7 %collective-permute-start.1 = (bf16[3,2,16,1024]{3,2,1,0:T(8,128)(2,1)}, bf16[3,2,16,1024]{3,2,1,0:T(8,128)(2,1)S(1)}, u32[]{:S(2)}, u32[]{:S(2)}) collective-permute-start(bf16[3,2,16,1024]{3,2,1,0:T(8,128)(2,1)} %get-tuple-element.46), channel_id=1, source_target_pairs={{0,4},{4,8},{8,12},{12,16},{16,20},{20,24},{24,28},{28,32},{32,36}... | collective-permute-start | bytes 589832 | tf_op jit(solution)/shard_map/ppermute | solution.py:51
  14.1 44.9 %copy-start.16 = (bf16[512,512]{1,0:T(8,128)(2,1)}, bf16[512,512]{1,0:T(8,128)(2,1)S(1)}, u32[]{:S(2)}) copy-start(bf16[512,512]{1,0:T(8,128)(2,1)S(1)} %pad_maximum_fusion.c0) | copy-start | bytes 1572868
  14.4 33.6 %collective-permute-start.4 = (bf16[512,512]{1,0:T(8,128)(2,1)S(1)}, bf16[512,512]{1,0:T(8,128)(2,1)S(1)}, u32[]{:S(2)}, u32[]{:S(2)}) collective-permute-start(bf16[512,512]{1,0:T(8,128)(2,1)S(1)} %pad_maximum_fusion.c0), channel_id=1, source_target_pairs={{0,3},{1,0},{2,1},{3,2},{4,7},{5,4},{6,5},{7,6},{8,11},{9,8},{10,9... | collective-permute-start | bytes 1572872 | tf_op jit(solution)/shard_map/ppermute | solution.py:46
  17.5 30.5 %collective-permute-start.3 = (bf16[512,512]{1,0:T(8,128)(2,1)S(1)}, bf16[512,512]{1,0:T(8,128)(2,1)}, u32[]{:S(2)}, u32[]{:S(2)}) collective-permute-start(bf16[512,512]{1,0:T(8,128)(2,1)S(1)} %pad_maximum_fusion.c0), channel_id=1, source_target_pairs={{0,2},{1,3},{2,0},{3,1},{4,6},{5,7},{6,4},{7,5},{8,10},{9,11},{10,... | collective-permute-start | bytes 1572872 | tf_op jit(solution)/shard_map/ppermute | solution.py:46
  18.1 29.9 %collective-permute-start.2 = (bf16[512,512]{1,0:T(8,128)(2,1)S(1)}, bf16[512,512]{1,0:T(8,128)(2,1)}, u32[]{:S(2)}, u32[]{:S(2)}) collective-permute-start(bf16[512,512]{1,0:T(8,128)(2,1)S(1)} %pad_maximum_fusion.c0), channel_id=1, source_target_pairs={{0,1},{1,2},{2,3},{3,0},{4,5},{5,6},{6,7},{7,4},{8,9},{9,10},{10,1... | collective-permute-start | bytes 1572872 | tf_op jit(solution)/shard_map/ppermute | solution.py:46
  24.5 23.4 %all-to-all-start = ((bf16[32,2,2,16,128]{4,3,2,1,0:T(8,128)(2,1)}), bf16[32,2,2,16,128]{4,3,2,1,0:T(8,128)(2,1)S(1)}, u32[]{:S(2)}, u32[]{:S(2)}) async-start(bf16[32,2,2,16,128]{4,3,2,1,0:T(8,128)(2,1)} %get-tuple-element.48), calls=%async_computation | async-start | bytes 1048576 | tf_op jit(solution)/shard_map/all_to_all | solution.py:554
  36.2 22.9 %copy-start.5 = (bf16[2,128,1024]{2,1,0:T(8,128)(2,1)S(1)}, bf16[2,128,1024]{2,1,0:T(8,128)(2,1)}, u32[]{:S(2)}) copy-start(bf16[2,128,1024]{2,1,0:T(8,128)(2,1)} %q_ref.3) | copy-start | bytes 1572868
  52.7 19.0 %all-to-all-start.1 = ((bf16[32,2,2,16,128]{4,3,2,1,0:T(8,128)(2,1)}), bf16[32,2,2,16,128]{4,3,2,1,0:T(8,128)(2,1)S(1)}, u32[]{:S(2)}, u32[]{:S(2)}) async-start(bf16[32,2,2,16,128]{4,3,2,1,0:T(8,128)(2,1)} %conv.1), calls=%async_computation.1 | async-start | bytes 1048576 | tf_op jit(solution)/shard_map/all_to_all | solution.py:554
  59.1 103.6 %reduce-scatter.2.cloned.1.call-start = ((), (), s32[]{:S(2)}) async-start(), calls=%async_computation.6 | async-start | bytes 4456448 | tf_op jit(solution)/shard_map/reduce_scatter | solution.py:606
  73.9 2.0 %collective-permute-start.5 = (bf16[256,1024]{1,0:T(8,128)(2,1)S(1)}, bf16[256,1024]{1,0:T(8,128)(2,1)}, u32[]{:S(2)}, u32[]{:S(2)}) collective-permute-start(bf16[256,1024]{1,0:T(8,128)(2,1)S(1)} %bitcast.18), channel_id=1, source_target_pairs={{0,4},{4,0},{8,12},{12,8},{16,20},{20,16},{24,28},{28,24},{32,36},... | collective-permute-start | bytes 1572872 | tf_op jit(solution)/shard_map/ppermute | solution.py:30
  88.0 2.0 %collective-permute-start.6 = (bf16[256,1024]{1,0:T(8,128)(2,1)S(1)}, bf16[256,1024]{1,0:T(8,128)(2,1)S(1)}, u32[]{:S(2)}, u32[]{:S(2)}) collective-permute-start(bf16[256,1024]{1,0:T(8,128)(2,1)S(1)} %get-tuple-element.60), channel_id=1, source_target_pairs={{0,4},{4,0},{8,12},{12,8},{16,20},{20,16},{24,28},{28,24},{32,36},... | collective-permute-start | bytes 1572872 | tf_op jit(solution)/shard_map/ppermute | solution.py:30
  92.9 18.8 %all-to-all-start.2 = ((bf16[32,2,2,16,128]{4,3,2,1,0:T(8,128)(2,1)}), bf16[32,2,2,16,128]{4,3,2,1,0:T(8,128)(2,1)S(1)}, u32[]{:S(2)}, u32[]{:S(2)}) async-start(bf16[32,2,2,16,128]{4,3,2,1,0:T(8,128)(2,1)} %get-tuple-element.69), calls=%async_computation.2 | async-start | bytes 1048576 | tf_op jit(solution)/shard_map/all_to_all | solution.py:554
  97.8 24.5 %copy-start.9 = (f32[2,128,1024]{2,1,0:T(8,128)S(1)}, f32[2,128,1024]{2,1,0:T(8,128)}, u32[]{:S(2)}) copy-start(f32[2,128,1024]{2,1,0:T(8,128)} %copy-done.8) | copy-start | bytes 3145732
  97.8 24.5 %copy-start.15 = (bf16[2,128,1024]{2,1,0:T(8,128)(2,1)S(1)}, bf16[2,128,1024]{2,1,0:T(8,128)(2,1)}, u32[]{:S(2)}) copy-start(bf16[2,128,1024]{2,1,0:T(8,128)(2,1)} %copy-done.14) | copy-start | bytes 1572868
  104.2 23.9 %collective-permute-start.7 = (bf16[512,512]{1,0:T(8,128)(2,1)}, bf16[512,512]{1,0:T(8,128)(2,1)}, u32[]{:S(2)}, u32[]{:S(2)}) collective-permute-start(bf16[512,512]{1,0:T(8,128)(2,1)} %get-tuple-element.64), channel_id=1, source_target_pairs={{0,1},{1,2},{2,3},{3,0},{4,5},{5,6},{6,7},{7,4},{8,9},{9,10},{10,1... | collective-permute-start | bytes 1572872 | tf_op jit(solution)/shard_map/ppermute | solution.py:46
  105.7 26.3 %collective-permute-start.8 = (bf16[512,512]{1,0:T(8,128)(2,1)}, bf16[512,512]{1,0:T(8,128)(2,1)}, u32[]{:S(2)}, u32[]{:S(2)}) collective-permute-start(bf16[512,512]{1,0:T(8,128)(2,1)} %get-tuple-element.65), channel_id=1, source_target_pairs={{0,2},{1,3},{2,0},{3,1},{4,6},{5,7},{6,4},{7,5},{8,10},{9,11},{10,... | collective-permute-start | bytes 1572872 | tf_op jit(solution)/shard_map/ppermute | solution.py:46
  108.4 23.6 %collective-permute-start.9 = (bf16[512,512]{1,0:T(8,128)(2,1)}, bf16[512,512]{1,0:T(8,128)(2,1)}, u32[]{:S(2)}, u32[]{:S(2)}) collective-permute-start(bf16[512,512]{1,0:T(8,128)(2,1)} %get-tuple-element.66), channel_id=1, source_target_pairs={{0,3},{1,0},{2,1},{3,2},{4,7},{5,4},{6,5},{7,6},{8,11},{9,8},{10,9... | collective-permute-start | bytes 1572872 | tf_op jit(solution)/shard_map/ppermute | solution.py:46
  116.5 28.3 %all-to-all-start.3 = ((bf16[32,2,2,16,128]{4,3,2,1,0:T(8,128)(2,1)}), bf16[32,2,2,16,128]{4,3,2,1,0:T(8,128)(2,1)}, u32[]{:S(2)}, u32[]{:S(2)}) async-start(bf16[32,2,2,16,128]{4,3,2,1,0:T(8,128)(2,1)} %corr.1), calls=%async_computation.3 | async-start | bytes 1048576 | tf_op jit(solution)/shard_map/all_to_all | solution.py:554
  122.3 3.1 %collective-permute-start.11 = (bf16[1,2,16,1024]{3,2,1,0:T(8,128)(2,1)S(1)}, bf16[1,2,16,1024]{3,2,1,0:T(8,128)(2,1)S(1)}, u32[]{:S(2)}, u32[]{:S(2)}) collective-permute-start(bf16[1,2,16,1024]{3,2,1,0:T(8,128)(2,1)S(1)} %fusion), channel_id=1, source_target_pairs={{4,0},{8,4},{12,8},{16,12},{20,16},{24,20},{28,24},{32,28},{36,32}... | collective-permute-start | bytes 196616 | tf_op jit(solution)/shard_map/ppermute | solution.py:51
  135.4 13.0 %collective-permute-start.10 = (bf16[256,512]{1,0:T(8,128)(2,1)}, bf16[256,512]{1,0:T(8,128)(2,1)S(1)}, u32[]{:S(2)}, u32[]{:S(2)}) collective-permute-start(bf16[256,512]{1,0:T(8,128)(2,1)} %get-tuple-element.68), channel_id=1, source_target_pairs={{0,4},{4,0},{8,12},{12,8},{16,20},{20,16},{24,28},{28,24},{32,36},... | collective-permute-start | bytes 786440 | tf_op jit(solution)/shard_map/ppermute | solution.py:30
  147.1 3.2 %collective-permute-start.12 = (bf16[2,2,16,1024]{3,2,1,0:T(8,128)(2,1)S(1)}, bf16[2,2,16,1024]{3,2,1,0:T(8,128)(2,1)S(1)}, u32[]{:S(2)}, u32[]{:S(2)}) collective-permute-start(bf16[2,2,16,1024]{3,2,1,0:T(8,128)(2,1)S(1)} %get-tuple-element.76), channel_id=1, source_target_pairs={{4,0},{8,4},{12,8},{16,12},{20,16},{24,20},{28,24},{32,28},{36,32}... | collective-permute-start | bytes 393224 | tf_op jit(solution)/shard_map/ppermute | solution.py:51
  (20 other events, 118.3 us)
Sparse Core Ops, SparseCore 0:
  10.2 56.6 all-gather.1
  81.9 80.7 reduce-scatter.1
